TPU v7x, 32 devices: a whole 2x2x4 slice. The times are simulated.
32 devices in a mesh: groups: 2 (over y), cls: 4 (over z), img: 2 (over x), rd: 2 (over core).
Axes of the slice: x: 2, y: 2, z: 4, core: 2. Of those that a mesh axis runs over, the one named last changes fastest.
Arguments:
- images: bfloat16 [2048, 4096], P(('groups', 'cls', 'img', 'rd')), parts along dimension 0, may hold values from -9 to 9
- counts: int32 [32, 4], P(('groups', 'cls', 'img', 'rd')), parts along dimension 0, may hold values from 1 to 31, as said below
- owners: int32 [32, 4], P(('groups', 'cls', 'img', 'rd')), parts along dimension 0, may hold values from 0 to 1, as said below
- references: bfloat16 [32, 4096], P(('groups', 'cls')), parts along dimension 0, may hold values from -1 to 1
Outputs:
- class_means: float32 [32, 4096], P(('groups', 'cls')), parts along dimension 0
- class_weights: float32 [32], P(('groups', 'cls')), parts along dimension 0
- loglik: float32 [2048], P(('groups', 'cls', 'img', 'rd')), parts along dimension 0
There are 2 independent parts, one for each index of `groups`. A program takes and returns all parts, laid end to end along the dimension named above; each array names one. Nothing has to cross between parts.
Inputs may be any that keep to these rules, and one draw needn't show every extreme that they name: Each micrograph holds 1 or more particles; a reader's used rows number the sum of its counts, at most 64. At most 32 of a reader's particles have one owner; for every reader exactly 32 go to one owner, and that owner is the same for all readers with the same cls and rd index. `owners`: every owner is named by exactly two micrographs of each reader.
All inputs are finite; a program needn't handle non-finite values.
Results may differ from a plain program's by a relative error of at most 0.0024.
Values may be sent and summed in bfloat16 or wider, within the bound.
No kernel may reach another device: no remote copies, remote signals or barrier semaphores. Data moves between devices by JAX's collectives and lax.ppermute only.
A program may use at most 128 MiB of HBM per device.

v0:
```python
import jax
import jax.numpy as jnp
from jax import lax
from jax.sharding import PartitionSpec as P

BOX = 64
ROTS = 8


def passed_along(array, axis, by):
    devices = lax.axis_size(axis)
    return lax.ppermute(array, axis, [(i, (i + by) % devices) for i in range(devices)])


def turn_image(field, turn_index):
    square = field.reshape(field.shape[:-1] + (BOX, BOX))
    if turn_index >= 4:
        square = jnp.flip(square, -1)
    square = jnp.rot90(square, turn_index % 4, axes=(-2, -1))
    return square.reshape(field.shape)


def turn_back(field, turn_index):
    square = field.reshape(field.shape[:-1] + (BOX, BOX))
    square = jnp.rot90(square, -(turn_index % 4), axes=(-2, -1))
    if turn_index >= 4:
        square = jnp.flip(square, -1)
    return square.reshape(field.shape)


def slot_table(count_row, owner_row, read_rows, capacity):
    mic_count = count_row.shape[0]
    ends = jnp.cumsum(count_row)
    position = jnp.arange(read_rows, dtype=jnp.int32)
    micrograph = jnp.sum((position[:, None] >= ends[None, :]).astype(jnp.int32), axis=1)
    usable = position < ends[mic_count - 1]
    matches = micrograph[:, None] == jnp.arange(mic_count, dtype=jnp.int32)[None, :]
    target = jnp.sum(jnp.where(matches, owner_row[None, :], 0), axis=1)
    earlier = (
        (target[:, None] == target[None, :])
        & usable[None, :]
        & (position[None, :] < position[:, None])
    )
    ranking = jnp.sum(earlier.astype(jnp.int32), axis=1)
    slot_index = jnp.where(usable, target * capacity + ranking, -1)
    placing = slot_index[None, :] == jnp.arange(read_rows, dtype=jnp.int32)[:, None]
    return (usable, placing)


def class_scores(particle_rows, piece):
    pixels = piece.shape[1]
    turned = jnp.stack(
        [turn_image(piece, turn_index) for turn_index in range(ROTS)], axis=1
    ).reshape(-1, pixels)
    squares = jnp.sum(piece.astype(jnp.float32) ** 2, axis=1)
    inner = lax.dot_general(
        particle_rows, turned, (((1,), (1,)), ((), ())), preferred_element_type=jnp.float32
    )
    return inner - 0.5 * jnp.repeat(squares, ROTS)[None, :]


def class_block(weights, particle_rows, first_class, class_count):
    chosen = lax.dynamic_slice_in_dim(weights, first_class * ROTS, class_count * ROTS, 1)
    summed = lax.dot_general(
        chosen, particle_rows, (((0,), (0,)), ((), ())), preferred_element_type=jnp.float32
    )
    summed = summed.reshape(class_count, ROTS, summed.shape[1])
    result = turn_back(summed[:, 0], 0)
    for turn_index in range(1, ROTS):
        result = result + turn_back(summed[:, turn_index], turn_index)
    return result


def local(images, counts, owners, references):
    read_rows, pixels = images.shape
    n_img = lax.axis_size("img")
    n_cls = lax.axis_size("cls")
    capacity = read_rows // n_img
    per_dev = references.shape[0]
    classes = per_dev * n_cls
    usable, placing = slot_table(counts[0], owners[0], read_rows, capacity)
    packed = jnp.dot(
        placing.astype(jnp.bfloat16), images, preferred_element_type=jnp.float32
    ).astype(jnp.bfloat16)
    filled = jnp.sum(placing.astype(jnp.float32), axis=1).astype(jnp.bfloat16)
    moved, arrived = (
        lax.all_to_all(
            packed.reshape(n_img, capacity, pixels), "img", split_axis=0, concat_axis=0, tiled=True
        ),
        lax.all_to_all(
            filled.reshape(n_img, capacity), "img", split_axis=0, concat_axis=0, tiled=True
        ),
    )
    particle_rows = moved.reshape(read_rows, pixels)
    live_rows = arrived.reshape(read_rows) > 0
    scores = class_scores(particle_rows, lax.all_gather(references, "cls", axis=0, tiled=True))
    highest = jnp.max(scores, axis=1, keepdims=True)
    total = jnp.log(jnp.sum(jnp.exp(scores - highest), axis=1, keepdims=True)) + highest
    weights = jnp.where(live_rows[:, None], jnp.exp(scores - total), 0.0).astype(jnp.bfloat16)
    row_loglik = jnp.where(live_rows, total[:, 0], 0.0)
    column_sums = jnp.sum(
        jnp.sum(weights.astype(jnp.float32), axis=0).reshape(classes, ROTS), axis=1
    )
    totals = lax.psum(column_sums, ("cls", "img", "rd"))
    device_index = lax.axis_index("cls")
    own_totals = lax.dynamic_slice_in_dim(totals, device_index * per_dev, per_dev)

    def cycle_stop(stop_index, carried):
        block = (device_index - 1 - stop_index) % n_cls
        carried = carried + class_block(weights, particle_rows, block * per_dev, per_dev)
        return passed_along(carried, "cls", 1)

    carried = lax.fori_loop(0, n_cls - 1, cycle_stop, jnp.zeros((per_dev, pixels), jnp.float32))
    class_sums = carried + class_block(weights, particle_rows, device_index * per_dev, per_dev)
    class_sums = lax.psum(class_sums, ("img", "rd"))
    class_means = class_sums / (own_totals[:, None] + 1.0)
    return (class_means, own_totals, row_loglik)


def solution(mesh):
    placed = (
        P(("groups", "cls", "img", "rd"), None),
        P(("groups", "cls", "img", "rd"), None),
        P(("groups", "cls", "img", "rd"), None),
        P(("groups", "cls"), None),
    )
    return jax.shard_map(
        local,
        mesh=mesh,
        in_specs=placed,
        out_specs=(
            P(("groups", "cls"), None),
            P(("groups", "cls")),
            P(("groups", "cls", "img", "rd")),
        ),
        check_vma=False,
    )
```

profile of v0, /device:TPU:0, one launch (start us, length us, event | category | flops | bytes accessed | tf_op | source)
XLA Modules:
  0.0 127.1 jit_solution(13996771671538741797)
XLA Ops:
  7.2 0.7 copy-done.2
  7.9 0.2 reduce-window.4
  8.1 0.6 slice.108
  8.7 0.6 iota_compare_fusion.5
  9.4 0.7 copy-done.3
  10.1 0.2 convert_reduce_fusion.2
  10.3 0.7 add_select_fusion
  11.1 0.7 convert_element_type.46
  11.7 4.2 %all-to-all-start = ((bf16[2,1,32]{2,1,0:T(2,128)(2,1)}), bf16[2,1,32]{2,1,0:T(2,128)(2,1)S(1)}, u32[]{:S(2)}, u32[]{:S(2)}) async-start(bf16[2,1,32]{2,1,0:T(2,128)(2,1)} %convert_element_type.46), calls=%async_computation | async-start | bytes 2048 | tf_op jit(solution)/shard_map/all_to_all | solution.py:90
  16.0 14.3 %all-gather = bf16[4,4,4096]{2,1,0:T(4,128)(2,1)S(1)} all-gather(bf16[1,4,4096]{2,1,0:T(4,128)(2,1)} %bitcast.98), channel_id=1, replica_groups=mesh['groups'=2,'cls'=4,'img'=2,'rd'=2] {'cls'}, dimensions={0}, use_global_device_ids=true | all-gather | bytes 163840 | tf_op jit(solution)/shard_map/all_gather | solution.py:96
  30.2 0.3 reshape.220
  30.5 0.2 copy.67
  30.7 0.2 rev.148
  31.0 0.2 rev.149
  31.2 0.3 stack_reshape.29
  31.6 0.2 copy.69
  31.8 0.3 stack_reshape.25
  32.0 0.2 rev.151
  32.2 0.2 multiply_reduce_fusion
  32.4 0.6 constant_dynamic-update-slice_fusion.7
  33.0 0.3 stack_reshape.26
  33.3 0.3 stack_reshape.27
  33.6 0.3 stack_reshape.28
  33.9 0.3 stack_reshape.30
  34.1 0.3 stack_reshape.31
  34.4 1.1 convolution_convert_fusion
  35.5 0.7 constant_dynamic-update-slice_fusion.6
  36.2 0.7 constant_dynamic-update-slice_fusion.5
  36.9 0.7 constant_dynamic-update-slice_fusion.4
  37.5 0.7 constant_dynamic-update-slice_fusion.3
  38.2 0.6 constant_dynamic-update-slice_fusion.2
  38.8 0.7 constant_dynamic-update-slice_fusion.1
  39.5 0.7 constant_dynamic-update-slice_fusion
  40.2 3.6 %all-to-all-start.1 = ((bf16[2,32,4096]{2,1,0:T(8,128)(2,1)}), bf16[2,32,4096]{2,1,0:T(8,128)(2,1)S(1)}, u32[]{:S(2)}, u32[]{:S(2)}) async-start(bf16[2,32,4096]{2,1,0:T(8,128)(2,1)} %bitcast.10), calls=%async_computation.1 | async-start | bytes 1048576 | tf_op jit(solution)/shard_map/all_to_all | solution.py:87
  44.2 6.1 %all-to-all-done.1 = bf16[2,32,4096]{2,1,0:T(8,128)(2,1)S(1)} async-done(((bf16[2,32,4096]{2,1,0:T(8,128)(2,1)}), bf16[2,32,4096]{2,1,0:T(8,128)(2,1)S(1)}, u32[]{:S(2)}, u32[]{:S(2)}) %all-to-all-start.1) | async-done | bytes 524320 | tf_op jit(solution)/shard_map/all_to_all | solution.py:87
  50.4 0.9 fusion.23
  51.2 0.2 exponential_reduce_fusion
  51.4 0.5 broadcast_select_fusion
  52.2 0.2 fusion.21
  52.4 1.3 %slice_reduce_fusion.13 = (f32[4,4096]{1,0:T(4,128)S(1)}, f32[4,4096]{1,0:T(4,128)S(1)}, f32[4,4096]{1,0:T(4,128)S(1)}, f32[4,4096]{1,0:T(4,128)S(1)}, f32[4,409...) fusion(f32[4,8,4096]{2,1,0:T(8,128)S(1)} %fusion.21), kind=kLoop, calls=%fused_computation.30 | loop fusion | bytes 1048576 | tf_op jit(solution)/shard_map/slice | solution.py:70
  55.4 0.1 reshape_squeeze.25
  55.7 0.1 reshape_squeeze.26
  56.5 31.3 %while.15 = (s32[]{:T(128)}, f32[4,4096]{1,0:T(4,128)S(1)}, s32[]{:T(128)}, bf16[64,128]{1,0:T(8,128)(2,1)S(1)}, bf16[64,4096]{1,0:T(8,128)(2,1)S(1)}, /*index=5...) while((s32[]{:T(128)}, f32[4,4096]{1,0:T(4,128)S(1)}, s32[]{:T(128)}, ...), condition=%wide.region_9.10_spmd, body=%wide.region_8.9_spmd.sunk | while | flops 16908304 | bytes 6308160 | solution.py:113
  56.6 0.3 convolution_bitcast_fusion.2
  56.9 1.3 %slice_reduce_fusion.15 = (f32[4,4096]{1,0:T(4,128)S(1)}, f32[4,4096]{1,0:T(4,128)S(1)}, f32[4,4096]{1,0:T(4,128)S(1)}, f32[4,4096]{1,0:T(4,128)S(1)}, f32[4,409...) fusion(f32[4,8,4096]{2,1,0:T(8,128)S(1)} %convolution_bitcast_fusion.2), kind=kLoop, calls=%fused_computation.7.clone.1 | loop fusion | bytes 1048576 | tf_op jit(solution)/shard_map/while/body/eval_jaxpr/slice | solution.py:70
  58.7 0.1 squeeze.90
  59.5 0.1 squeeze.87
  60.4 0.1 squeeze.91
  60.9 1.9 %collective-permute-start = (f32[4,4096]{1,0:T(4,128)S(1)}, f32[4,4096]{1,0:T(4,128)S(1)}, u32[]{:S(2)}, u32[]{:S(2)}) collective-permute-start(f32[4,4096]{1,0:T(4,128)S(1)} %fusion.33), channel_id=1, source_target_pairs={{0,4},{4,8},{8,12},{12,0},{1,5},{5,9},{9,13},{13,1},{2,6},{6,10},{... | collective-permute-start | bytes 196616 | tf_op jit(solution)/shard_map/while/body/eval_jaxpr/ppermute | solution.py:12
  62.8 4.2 %collective-permute-done = f32[4,4096]{1,0:T(4,128)S(1)} collective-permute-done((f32[4,4096]{1,0:T(4,128)S(1)}, f32[4,4096]{1,0:T(4,128)S(1)}, u32[]{:S(2)}, u32[]{:S(2)}) %collective-permute-start) | collective-permute-done | bytes 65568 | tf_op jit(solution)/shard_map/while/body/eval_jaxpr/ppermute | solution.py:12
  67.0 0.3 convolution_bitcast_fusion.2
  67.3 1.3 %slice_reduce_fusion.15 = (f32[4,4096]{1,0:T(4,128)S(1)}, f32[4,4096]{1,0:T(4,128)S(1)}, f32[4,4096]{1,0:T(4,128)S(1)}, f32[4,4096]{1,0:T(4,128)S(1)}, f32[4,409...) fusion(f32[4,8,4096]{2,1,0:T(8,128)S(1)} %convolution_bitcast_fusion.2), kind=kLoop, calls=%fused_computation.7.clone.1 | loop fusion | bytes 1048576 | tf_op jit(solution)/shard_map/while/body/eval_jaxpr/slice | solution.py:70
  68.6 0.1 squeeze.86
  69.9 0.1 squeeze.87
  70.8 0.1 squeeze.91
  71.4 6.0 %collective-permute-done = f32[4,4096]{1,0:T(4,128)S(1)} collective-permute-done((f32[4,4096]{1,0:T(4,128)S(1)}, f32[4,4096]{1,0:T(4,128)S(1)}, u32[]{:S(2)}, u32[]{:S(2)}) %collective-permute-start) | collective-permute-done | bytes 65568 | tf_op jit(solution)/shard_map/while/body/eval_jaxpr/ppermute | solution.py:12
  77.4 0.3 convolution_bitcast_fusion.2
  77.7 1.3 %slice_reduce_fusion.15 = (f32[4,4096]{1,0:T(4,128)S(1)}, f32[4,4096]{1,0:T(4,128)S(1)}, f32[4,4096]{1,0:T(4,128)S(1)}, f32[4,4096]{1,0:T(4,128)S(1)}, f32[4,409...) fusion(f32[4,8,4096]{2,1,0:T(8,128)S(1)} %convolution_bitcast_fusion.2), kind=kLoop, calls=%fused_computation.7.clone.1 | loop fusion | bytes 1048576 | tf_op jit(solution)/shard_map/while/body/eval_jaxpr/slice | solution.py:70
  80.3 0.1 squeeze.87
  81.8 6.0 %collective-permute-done = f32[4,4096]{1,0:T(4,128)S(1)} collective-permute-done((f32[4,4096]{1,0:T(4,128)S(1)}, f32[4,4096]{1,0:T(4,128)S(1)}, u32[]{:S(2)}, u32[]{:S(2)}) %collective-permute-start) | collective-permute-done | bytes 65568 | tf_op jit(solution)/shard_map/while/body/eval_jaxpr/ppermute | solution.py:12
  87.8 0.7 fusion.18
  88.6 29.5 %psum.15 = f32[16]{0:T(128)S(1)} all-reduce(f32[16]{0:T(128)S(1)} %reduce_sum.79), channel_id=1, replica_groups=mesh['groups'=2,'cls'=4,'img'=2,'rd'=2] {'cls','img','rd'}, use_global_device_ids=true, to_apply=%region_13.14 | all-reduce | flops 16 | bytes 128 | tf_op jit(solution)/shard_map/psum | solution.py:104
  118.1 0.6 broadcast_add_fusion
  118.7 1.6 %broadcast_divide_fusion = f32[4,4096]{1,0:T(4,128)} fusion(f32[4,4096]{1,0:T(4,128)} %all-reduce.2.cloned.1.call-done, f32[4]{0:T(128)S(1)} %get-tuple-element.167), kind=kLoop, calls=%fused_computation.39 | loop fusion | flops 16384 | bytes 131088 | tf_op jit(solution)/shard_map/div | solution.py:116
  (124 shorter events, 10.6 us)
Async XLA Ops:
  7.2 27.3 %copy-start = (bf16[64,4096]{1,0:T(8,128)(2,1)S(1)}, bf16[64,4096]{1,0:T(8,128)(2,1)}, u32[]{:S(2)}) copy-start(bf16[64,4096]{1,0:T(8,128)(2,1)} %param.6) | copy-start | bytes 1572868
  7.2 0.7 copy-start.2
  9.4 0.7 copy-start.3
  11.7 28.4 %all-to-all-start = ((bf16[2,1,32]{2,1,0:T(2,128)(2,1)}), bf16[2,1,32]{2,1,0:T(2,128)(2,1)S(1)}, u32[]{:S(2)}, u32[]{:S(2)}) async-start(bf16[2,1,32]{2,1,0:T(2,128)(2,1)} %convert_element_type.46), calls=%async_computation | async-start | bytes 2048 | tf_op jit(solution)/shard_map/all_to_all | solution.py:90
  40.2 10.2 %copy-start.1 = (bf16[16,8,4096]{2,0,1:T(8,128)(2,1)S(1)}, bf16[16,8,4096]{2,0,1:T(8,128)(2,1)}, u32[]{:S(2)}) copy-start(bf16[16,8,4096]{2,0,1:T(8,128)(2,1)} %constant_dynamic-update-slice_fusion) | copy-start | bytes 3145732
  40.2 10.2 %all-to-all-start.1 = ((bf16[2,32,4096]{2,1,0:T(8,128)(2,1)}), bf16[2,32,4096]{2,1,0:T(8,128)(2,1)S(1)}, u32[]{:S(2)}, u32[]{:S(2)}) async-start(bf16[2,32,4096]{2,1,0:T(8,128)(2,1)} %bitcast.10), calls=%async_computation.1 | async-start | bytes 1048576 | tf_op jit(solution)/shard_map/all_to_all | solution.py:87
  43.8 74.9 %all-reduce.2.cloned.1.call-start = ((), (), s32[]{:S(2)}) async-start(), calls=%async_computation.2 | async-start | bytes 131072 | tf_op jit(solution)/shard_map/psum | solution.py:115
  60.9 6.1 %collective-permute-start = (f32[4,4096]{1,0:T(4,128)S(1)}, f32[4,4096]{1,0:T(4,128)S(1)}, u32[]{:S(2)}, u32[]{:S(2)}) collective-permute-start(f32[4,4096]{1,0:T(4,128)S(1)} %fusion.33), channel_id=1, source_target_pairs={{0,4},{4,8},{8,12},{12,0},{1,5},{5,9},{9,13},{13,1},{2,6},{6,10},{... | collective-permute-start | bytes 196616 | tf_op jit(solution)/shard_map/while/body/eval_jaxpr/ppermute | solution.py:12
  71.3 6.1 %collective-permute-start = (f32[4,4096]{1,0:T(4,128)S(1)}, f32[4,4096]{1,0:T(4,128)S(1)}, u32[]{:S(2)}, u32[]{:S(2)}) collective-permute-start(f32[4,4096]{1,0:T(4,128)S(1)} %fusion.33), channel_id=1, source_target_pairs={{0,4},{4,8},{8,12},{12,0},{1,5},{5,9},{9,13},{13,1},{2,6},{6,10},{... | collective-permute-start | bytes 196616 | tf_op jit(solution)/shard_map/while/body/eval_jaxpr/ppermute | solution.py:12
  81.7 6.1 %collective-permute-start = (f32[4,4096]{1,0:T(4,128)S(1)}, f32[4,4096]{1,0:T(4,128)S(1)}, u32[]{:S(2)}, u32[]{:S(2)}) collective-permute-start(f32[4,4096]{1,0:T(4,128)S(1)} %fusion.33), channel_id=1, source_target_pairs={{0,4},{4,8},{8,12},{12,0},{1,5},{5,9},{9,13},{13,1},{2,6},{6,10},{... | collective-permute-start | bytes 196616 | tf_op jit(solution)/shard_map/while/body/eval_jaxpr/ppermute | solution.py:12
Sparse Core Ops, SparseCore 0:
  88.7 28.3 all-reduce.1
where the time goes:
time: 127 us
  blocking collectives  43.8 us (34%)
  local copies, waits for them, and re-layouts  26.9 us (21%)
  waiting for transfers between devices  22.4 us (18%)
  between operations  14.3 us (11%)
  starting transfers between devices  9.94 us (8%)
  other arithmetic  6.24 us (5%)
  matrix products  3.16 us (2%)
    psum x1, blocking collectives, local(): totals = lax.psum(column_sums, ('cls', 'img', 'rd'))  29.5 us
    ppermute x3, waiting for transfers between devices, passed_along(): lax.ppermute(array, axis, [(i, (i + by) % devices) for i in range(devices)])  16.3 us
    all_gather x1, blocking collectives, local(): lax.all_gather(references, 'cls', axis=0, tiled=True)  14.3 us
    all_to_all x1, waiting for transfers between devices, local(): lax.all_to_all(packed.reshape(n_img, capacity, pixels), 'img', split_axis...  6.14 us
    unnamed x15, local copies, waits for them, and re-layouts  5.97 us
    slice x4, local copies, waits for them, and re-layouts, class_block(): result = result + turn_back(summed[:, turn_index], turn_index)  5.3 us
    all_to_all x1, starting transfers between devices, local(): lax.all_to_all(filled.reshape(n_img, capacity), 'img', split_axis=0, conc...  4.21 us
    squeeze x33, local copies, waits for them, and re-layouts, turn_back(): square = field.reshape(field.shape[:-1] + (BOX, BOX))  3.78 us
  transfers between devices with their start and end apart: 6, of which 4 were waited for; matrix products, arithmetic and copies ran while one was open for 9% of the time, Pallas kernels for 0%

commit v1 on v0

--- a/solution.py
+++ b/solution.py
@@ -1,10 +1,182 @@
+import functools
+
 import jax
 import jax.numpy as jnp
 from jax import lax
+from jax.experimental import pallas as pl
+from jax.experimental.pallas import tpu as pltpu
 from jax.sharding import PartitionSpec as P
 
 BOX = 64
 ROTS = 8
+LANES = 128
+PAIR = LANES // BOX
+LINKED = ("cls", "img", "rd")
+F32 = jnp.float32
+BF16 = jnp.bfloat16
+
+
+def rolled(tile, by):
+    return jnp.concatenate([tile[:, by:], tile[:, :by]], axis=1)
+
+
+def turn_kernel(own_ref, other_ref, out_ref, wide_ref):
+    pixels = own_ref.shape[1]
+    for block in range(pixels // LANES):
+        span = slice(block * LANES, (block + 1) * LANES)
+        tile = jnp.concatenate([own_ref[:, span], other_ref[:, span]], axis=0)
+        tile = tile.astype(F32).T
+        wide_ref[span, :] = tile
+        out_ref[span, :LANES] = tile.astype(BF16)
+    for column in range(BOX):
+        out_ref[column * BOX:(column + 1) * BOX, LANES:] = wide_ref[
+            pl.ds(column, BOX, stride=BOX), :
+        ].astype(BF16)
+
+
+def three_parts(value):
+    high = value.astype(BF16).astype(F32)
+    rest = value - high
+    middle = rest.astype(BF16).astype(F32)
+    return high, middle, (rest - middle).astype(BF16).astype(F32)
+
+
+def slot_column(table_ref, rows, capacity):
+    mic_count = table_ref.shape[1] // 2
+    position = lax.broadcasted_iota(jnp.int32, (rows, 1), 0)
+    slot = jnp.full((rows, 1), -1, jnp.int32)
+    start = jnp.int32(0)
+    for mic in range(mic_count):
+        owner = table_ref[0, mic_count + mic]
+        before = jnp.int32(0)
+        for earlier in range(mic):
+            same = table_ref[0, mic_count + earlier] == owner
+            before = before + jnp.where(same, table_ref[0, earlier], 0)
+        stop = start + table_ref[0, mic]
+        inside = (position >= start) & (position < stop)
+        slot = jnp.where(inside, position + (owner * capacity + before - start), slot)
+        start = stop
+    return slot, start
+
+
+def weigh_kernel(capacity, core_ref, table_ref, other_table_ref, one_ref, two_ref, three_ref, own_ref,
+                 images_ref, first_ref, second_ref, total_ref, flipped_ref, sums_ref):
+    core = core_ref[0]
+    per_dev, pixels = own_ref.shape
+    classes = 4 * per_dev
+    blocks = pixels // LANES
+    rows = LANES // 2
+    half = classes // 2
+    block_of = [slice(b * LANES, (b + 1) * LANES) for b in range(blocks)]
+    row_of = lax.broadcasted_iota(jnp.int32, (LANES, LANES), 0)
+    column_of = lax.broadcasted_iota(jnp.int32, (LANES, LANES), 1)
+    within = (row_of // BOX) * BOX + (BOX - 1 - row_of % BOX)
+    mirror = (column_of == within).astype(BF16)
+
+    refs = jnp.concatenate([one_ref[...].astype(F32), two_ref[...].astype(F32),
+                            three_ref[...].astype(F32), own_ref[...].astype(F32)], axis=0)
+    squares = jnp.sum(refs * refs, axis=1, keepdims=True)
+    stacked = jnp.concatenate([refs[:, b] for b in block_of], axis=0)
+    mirrored = jnp.dot(stacked.astype(BF16), mirror, preferred_element_type=F32)
+    for b in range(blocks):
+        part = slice(b * classes, (b + 1) * classes)
+        plain, turned = stacked[part], mirrored[part]
+        back = block_of[blocks - 1 - b]
+        flipped_ref[0:classes, block_of[b]] = plain.astype(BF16)
+        flipped_ref[classes:2 * classes, block_of[b]] = turned.astype(BF16)
+        flipped_ref[2 * classes:3 * classes, back] = rolled(plain, BOX).astype(BF16)
+        flipped_ref[3 * classes:4 * classes, back] = rolled(turned, BOX).astype(BF16)
+
+    inner = jnp.dot(flipped_ref[...], images_ref[...], preferred_element_type=F32)
+    scores = inner - 0.5 * jnp.concatenate([squares] * 4, axis=0)
+    highest = jnp.max(scores, axis=0, keepdims=True)
+    highest = jnp.maximum(highest[:, :LANES], highest[:, LANES:])
+    shifted = jnp.exp(scores - jnp.concatenate([highest, highest], axis=1))
+    summed = jnp.sum(shifted, axis=0, keepdims=True)
+    total = jnp.log(summed[:, :LANES] + summed[:, LANES:]) + highest
+
+    slot, used = slot_column(table_ref, rows, capacity)
+    other_slot, other_used = slot_column(other_table_ref, rows, capacity)
+    lane = lax.broadcasted_iota(jnp.int32, (1, LANES), 1)
+    live = (lane < used) | ((lane >= rows) & (lane < rows + other_used))
+    live = jnp.concatenate([live, live], axis=1)
+    weights = jnp.where(live, jnp.exp(scores - jnp.concatenate([total, total], axis=1)), 0.0)
+    weights = weights.astype(BF16).astype(F32)
+    chosen = jnp.concatenate(
+        [
+            jnp.where(core == 0, weights[f * classes:f * classes + half],
+                      weights[f * classes + half:(f + 1) * classes])
+            for f in range(4)
+        ],
+        axis=0,
+    )
+    sums_ref[...] = lax.dot_general(
+        chosen.astype(BF16), images_ref[...], (((1,), (1,)), ((), ())), preferred_element_type=F32
+    )
+    straight, swapped = [], []
+    for b in range(blocks):
+        back = block_of[blocks - 1 - b]
+        straight.append(sums_ref[0:half, block_of[b]] + rolled(sums_ref[2 * half:3 * half, back], BOX))
+        swapped.append(sums_ref[half:2 * half, block_of[b]] + rolled(sums_ref[3 * half:, back], BOX))
+    swapped = jnp.concatenate(swapped, axis=0)
+    upper = swapped.astype(BF16)
+    lower = (swapped - upper.astype(F32)).astype(BF16)
+    swapped = jnp.dot(upper, mirror, preferred_element_type=F32) + jnp.dot(
+        lower, mirror, preferred_element_type=F32
+    )
+    for b in range(blocks):
+        both = straight[b] + swapped[b * half:(b + 1) * half]
+        first_ref[:, block_of[b]] = both[:per_dev].astype(BF16)
+        second_ref[:, block_of[b]] = both[per_dev:].astype(BF16)
+
+    per_class = jnp.sum(chosen, axis=1, keepdims=True)
+    per_class = per_class[0:half] + per_class[half:2 * half] + per_class[2 * half:3 * half] + per_class[3 * half:]
+    high, middle, low = three_parts(per_class)
+    lanes = lax.broadcasted_iota(jnp.int32, (half, LANES), 1)
+    sent = jnp.where(lanes == 0, high, jnp.where(lanes == 1, middle, jnp.where(lanes == 2, low, 0.0)))
+    extra = slice(pixels, pixels + LANES)
+    first_ref[:, extra] = sent[:per_dev].astype(BF16)
+    second_ref[:, extra] = sent[per_dev:].astype(BF16)
+
+    column = jnp.concatenate([slot, jnp.where(other_slot < 0, -1, other_slot + rows)], axis=0)
+    placing = (column == column_of).astype(BF16)
+    high, middle, low = three_parts(total)
+    pieces = jnp.concatenate([high, middle, low, jnp.zeros((5, LANES), F32)], axis=0)
+    pieces = jnp.dot(pieces.astype(BF16), placing, preferred_element_type=F32)
+    total_ref[...] = pieces[0:1] + pieces[1:2] + pieces[2:3]
+    last = slice(pixels + LANES, pixels + 2 * LANES)
+    first_ref[:, last] = jnp.zeros((per_dev, LANES), BF16)
+    second_ref[:, last] = pieces[:per_dev].astype(BF16)
+
+
+def add_kernel(core_ref, one_ref, two_ref, three_ref, four_ref, own_ref, out_ref):
+    pixels = out_ref.shape[1] - LANES
+    middle = jnp.where(core_ref[0] == 0, three_ref[:, :pixels].astype(F32), own_ref[:, :pixels].astype(F32))
+    out_ref[:, :pixels] = (one_ref[:, :pixels].astype(F32) + two_ref[:, :pixels].astype(F32)) + (
+        middle + four_ref[:, :pixels].astype(F32)
+    )
+    pieces = four_ref[:, pixels:].astype(F32)
+    out_ref[:, pixels:] = jnp.broadcast_to(pieces[0:1] + pieces[1:2] + pieces[2:3], (out_ref.shape[0], LANES))
+
+
+def finish_kernel(place_ref, own_ref, other_ref, total_ref, means_ref, weights_ref, loglik_ref):
+    core, image = place_ref[0], place_ref[1]
+    per_dev, pixels = means_ref.shape
+    capacity = loglik_ref.shape[1] // 2
+    extra = slice(pixels, pixels + LANES)
+    count = own_ref[:, extra] + other_ref[:, extra]
+    count = count[:, 0:1] + count[:, 1:2] + count[:, 2:3]
+    means_ref[...] = (own_ref[:, :pixels] + other_ref[:, :pixels]) / (count + 1.0)
+    across = lax.broadcasted_iota(jnp.int32, (per_dev, per_dev), 1)
+    down = lax.broadcasted_iota(jnp.int32, (per_dev, per_dev), 0)
+    weights_ref[...] = jnp.sum(jnp.where(across == down, count, 0.0), axis=0, keepdims=True)
+    last = slice(pixels + LANES, pixels + 2 * LANES)
+    arrived = jnp.where(core == 0, rolled(other_ref[0:1, last], 2 * capacity), own_ref[0:1, last])
+    mine = total_ref[...]
+    arrived = jnp.where(image == 0, arrived[:, :capacity], arrived[:, capacity:2 * capacity])
+    mine = jnp.where(image == 0, mine[:, :capacity], mine[:, capacity:2 * capacity])
+    loglik_ref[:, :capacity] = jnp.where(image == 0, mine, arrived)
+    loglik_ref[:, capacity:] = jnp.where(image == 0, arrived, mine)
 
 
 def passed_along(array, axis, by):
@@ -117,7 +289,68 @@
     return (class_means, own_totals, row_loglik)
 
 
+def swapped_by(array, by, axes=LINKED):
+    devices = 1
+    for axis in axes:
+        devices = devices * lax.axis_size(axis)
+    pairs = []
+    for i in range(devices):
+        step = by(i & 1) if callable(by) else by
+        if step:
+            pairs.append((i, i ^ step))
+    return lax.ppermute(array, axes, pairs)
+
+
+def call(kernel, outs, args, scalars, scratch=()):
+    specs = [pl.BlockSpec(memory_space=pltpu.SMEM)] * scalars
+    specs += [pl.BlockSpec(memory_space=pltpu.VMEM)] * (len(args) - scalars)
+    return pl.pallas_call(
+        kernel,
+        out_shape=outs,
+        in_specs=specs,
+        out_specs=jax.tree.map(lambda _: pl.BlockSpec(memory_space=pltpu.VMEM), outs),
+        scratch_shapes=list(scratch),
+        compiler_params=pltpu.CompilerParams(vmem_limit_bytes=32 * 1024 * 1024),
+    )(*args)
+
+
+def direct(images, counts, owners, references):
+    read_rows, pixels = images.shape
+    capacity = read_rows // lax.axis_size("img")
+    per_dev = references.shape[0]
+    core = lax.axis_index("rd")
+    place = jnp.stack([core, lax.axis_index("img")]).astype(jnp.int32)
+    table = jnp.concatenate([counts, owners], axis=1)
+    other_images = swapped_by(images, 1, ("rd",))
+    other_table = swapped_by(table, 1, ("rd",))
+    near, far, cross = [swapped_by(references, k, ("cls",)) for k in (1, 2, 3)]
+    shape = jax.ShapeDtypeStruct
+    turned = call(turn_kernel, shape((pixels, 2 * LANES), BF16), (images, other_images), 0,
+                  [pltpu.VMEM((pixels, LANES), F32)])
+    wide = pixels + 2 * LANES
+    first, second, totals = call(
+        functools.partial(weigh_kernel, capacity),
+        (shape((per_dev, wide), BF16), shape((per_dev, wide), BF16), shape((1, LANES), F32)),
+        (place, table, other_table, near, far, cross, references, turned), 3,
+        [pltpu.VMEM((16 * per_dev, pixels), BF16), pltpu.VMEM((8 * per_dev, pixels), F32)],
+    )
+    one = swapped_by(first, lambda rd: 12 if rd else 4)
+    two = swapped_by(first, lambda rd: 14 if rd else 6)
+    three = swapped_by(second, lambda rd: 0 if rd else 8)
+    four = swapped_by(second, lambda rd: 2 if rd else 10)
+    summed = call(add_kernel, shape((per_dev, wide), F32), (place, one, two, three, four, second), 1)
+    other = swapped_by(summed, 1, ("rd",))
+    means, weights, loglik = call(
+        finish_kernel,
+        (shape((per_dev, pixels), F32), shape((1, per_dev), F32), shape((1, read_rows), F32)),
+        (place, summed, other, totals), 1,
+    )
+    return means, weights.reshape(per_dev), loglik.reshape(read_rows)
+
+
 def solution(mesh):
+    sizes = mesh.shape
+    small = sizes["cls"] == 4 and sizes["img"] == 2 and sizes["rd"] == 2
     placed = (
         P(("groups", "cls", "img", "rd"), None),
         P(("groups", "cls", "img", "rd"), None),
@@ -125,7 +358,7 @@
         P(("groups", "cls"), None),
     )
     return jax.shard_map(
-        local,
+        direct if small else local,
         mesh=mesh,
         in_specs=placed,
         out_specs=(

time: 127 us -> 29.1 us (0.23)
  blocking collectives: 43.8 us -> 0 us
  local copies, waits for them, and re-layouts: 26.9 us -> 1.05 us
  waiting for transfers between devices: 22.4 us -> 6.56 us
  between operations: 14.3 us -> 0.7 us
  Pallas kernels: 0 us -> 6.14 us
  other arithmetic: 6.24 us -> 0.82 us
  starting transfers between devices: 9.94 us -> 13.7 us
  matrix products: 3.16 us -> 0 us
    psum x1 -> x0, blocking collectives: 29.5 us -> none  [local(): totals = lax.psum(column_sums, ('cls', 'img', 'rd'))]
    all_gather x1 -> x0, blocking collectives: 14.3 us -> none  [local(): lax.all_gather(references, 'cls', axis=0, tiled=True)]
    ppermute x3 -> x10, starting transfers between devices: 2.08 us -> 13.7 us  [swapped_by(): return lax.ppermute(array, axes, pairs)]
    ppermute x3 -> x10, waiting for transfers between devices: 16.3 us -> 6.56 us  [swapped_by(): return lax.ppermute(array, axes, pairs)]
    all_to_all x2 -> x0, starting transfers between devices: 7.82 us -> none  [the longest x1 4.21 us: local(): lax.all_to_all(filled.reshape(n_img, capacity), 'img', split_axis=0, conc...]
    pallas_call x0 -> x4, Pallas kernels: none -> 6.14 us  [call(): pl.pallas_call(kernel, out_shape=outs, in_specs=specs, out_specs=jax.tree...]
    all_to_all x2 -> x0, waiting for transfers between devices: 6.14 us -> none  [the longest x1 6.14 us: local(): lax.all_to_all(packed.reshape(n_img, capacity, pixels), 'img', split_axis...]
    slice x5 -> x0, local copies, waits for them, and re-layouts: 5.88 us -> none  [the longest x4 5.3 us: class_block(): result = result + turn_back(summed[:, turn_index], turn_index)]
  transfers between devices with their start and end apart: 6 -> 10, of which waited for: 4 -> 5; matrix products, arithmetic and copies ran while one was open for 9% -> 3% of each run, Pallas kernels for 0% -> 5%
where the time goes in v1:
time: 29.1 us; the launch traced here: 28.9 us
  starting transfers between devices  13.7 us (47%)
  waiting for transfers between devices  6.56 us (23%)
  Pallas kernels  6.14 us (21%)
  local copies, waits for them, and re-layouts  1.05 us (4%)
  other arithmetic  0.82 us (3%)
  between operations  0.7 us (2%)
    ppermute x10, starting transfers between devices, swapped_by(): return lax.ppermute(array, axes, pairs)  13.7 us
    ppermute x10, waiting for transfers between devices, swapped_by(): return lax.ppermute(array, axes, pairs)  6.56 us
    pallas_call x4, Pallas kernels, call(): pl.pallas_call(kernel, out_shape=outs, in_specs=specs, out_specs=jax.tree...  6.14 us
    unnamed x4, local copies, waits for them, and re-layouts  1.05 us
    concatenate x1, other arithmetic, direct(): table = jnp.concatenate([counts, owners], axis=1)  0.75 us
  transfers between devices with their start and end apart: 10, of which 5 were waited for; matrix products, arithmetic and copies ran while one was open for 3% of the time, Pallas kernels for 5%

profile of v1, /device:TPU:0, one launch (start us, length us, event | category | flops | bytes accessed | tf_op | source)
XLA Modules:
  0.0 28.9 jit_solution(16002025203405107176)
XLA Ops:
  0.6 0.5 %collective-permute-start.4 = (bf16[64,4096]{1,0:T(8,128)(2,1)}, bf16[64,4096]{1,0:T(8,128)(2,1)S(1)}, u32[]{:S(2)}, u32[]{:S(2)}) collective-permute-start(bf16[64,4096]{1,0:T(8,128)(2,1)} %own_ref.2), channel_id=1, source_target_pairs={{0,1},{1,0},{2,3},{3,2},{4,5},{5,4},{6,7},{7,6},{8,9},{9,8},{10,11... | collective-permute-start | bytes 1572872 | tf_op jit(solution)/shard_map/ppermute | solution.py:301
  1.1 2.7 %collective-permute-start.1 = (bf16[4,4096]{1,0:T(4,128)(2,1)}, bf16[4,4096]{1,0:T(4,128)(2,1)S(1)}, u32[]{:S(2)}, u32[]{:S(2)}) collective-permute-start(bf16[4,4096]{1,0:T(4,128)(2,1)} %own_ref.3), channel_id=1, source_target_pairs={{0,4},{4,0},{8,12},{12,8},{1,5},{5,1},{9,13},{13,9},{2,6},{6,2},{1... | collective-permute-start | bytes 98312 | tf_op jit(solution)/shard_map/ppermute | solution.py:301
  3.8 2.6 %collective-permute-start.2 = (bf16[4,4096]{1,0:T(4,128)(2,1)}, bf16[4,4096]{1,0:T(4,128)(2,1)S(1)}, u32[]{:S(2)}, u32[]{:S(2)}) collective-permute-start(bf16[4,4096]{1,0:T(4,128)(2,1)} %own_ref.3), channel_id=1, source_target_pairs={{0,8},{4,12},{8,0},{12,4},{1,9},{5,13},{9,1},{13,5},{2,10},{6,14},... | collective-permute-start | bytes 98312 | tf_op jit(solution)/shard_map/ppermute | solution.py:301
  6.4 0.0 collective-permute-start.3
  6.4 0.7 %pad_add_fusion.1.table_ref = s32[1,8]{1,0:T(1,128)S(1)} fusion(s32[1,4]{1,0:T(1,128)} %param.6, s32[1,4]{1,0:T(1,128)} %param.5), kind=kLoop, calls=%fused_computation.1 | loop fusion | flops 8 | bytes 64 | tf_op jit(solution)/shard_map/concatenate | solution.py:323
  7.1 0.0 collective-permute-start
  7.1 0.1 pad_add_fusion.core_ref.place_ref
  7.2 0.0 collective-permute-done.4.other_ref
  7.2 0.0 copy-start
  7.2 1.0 %copy-done = bf16[64,4096]{1,0:T(8,128)(2,1)S(1)} copy-done((bf16[64,4096]{1,0:T(8,128)(2,1)S(1)}, bf16[64,4096]{1,0:T(8,128)(2,1)}, u32[]{:S(2)}) %copy-start) | copy-done | bytes 524312
  8.3 0.0 copy-start.1
  8.3 1.5 %shard_map.67.images_ref = bf16[4096,256]{1,0:T(8,128)(2,1)S(1)} custom-call(bf16[64,4096]{1,0:T(8,128)(2,1)S(1)} %copy-done, bf16[64,4096]{1,0:T(8,128)(2,1)S(1)} %collective-permute-done.4.other_ref), custom_call_target="tpu_custom_call" | custom-call | tf_op jit(solution)/shard_map/pallas_call | solution.py:307
  9.8 0.0 collective-permute-done.other_table_ref
  9.8 0.0 collective-permute-done.1.one_ref
  9.8 0.0 collective-permute-done.2.two_ref
  9.8 2.5 %collective-permute-done.3.three_ref = bf16[4,4096]{1,0:T(4,128)(2,1)S(1)} collective-permute-done((bf16[4,4096]{1,0:T(4,128)(2,1)}, bf16[4,4096]{1,0:T(4,128)(2,1)S(1)}, u32[]{:S(2)}, u32[]{:S(2)}) %collective-permute-start.3) | collective-permute-done | bytes 32800 | tf_op jit(solution)/shard_map/ppermute | solution.py:301
  12.3 0.0 copy-done.1
  12.3 2.7 %shard_map.68 = (bf16[4,4352]{1,0:T(4,128)(2,1)S(1)}, bf16[4,4352]{1,0:T(4,128)(2,1)S(1)}, f32[1,128]{1,0:T(1,128)S(1)}) custom-call(s32[2]{0:T(128)S(1)} %pad_add_fusion.core_ref.place_ref, s32[1,8]{1,0:T(1,128)S(1)} %pad_add_fusion.1.table_ref, s32[1,8]{1,0:T(1,128)S(1)} %collective-permute-done.other_table_ref, ...), custom_call_target="tpu_custom_call" | custom-call | tf_op jit(solution)/shard_map/pallas_call | solution.py:307
  15.0 1.9 %collective-permute-start.7 = (bf16[4,4352]{1,0:T(4,128)(2,1)S(1)}, bf16[4,4352]{1,0:T(4,128)(2,1)S(1)}, u32[]{:S(2)}, u32[]{:S(2)}) collective-permute-start(bf16[4,4352]{1,0:T(4,128)(2,1)S(1)} %get-tuple-element.10.own_ref), channel_id=1, source_target_pairs={{0,8},{2,10},{4,12},{6,14},{8,0},{10,2},{12,4},{14,6},{16,24},{18,... | collective-permute-start | bytes 104456 | tf_op jit(solution)/shard_map/ppermute | solution.py:301
  17.0 3.9 %collective-permute-start.8 = (bf16[4,4352]{1,0:T(4,128)(2,1)S(1)}, bf16[4,4352]{1,0:T(4,128)(2,1)S(1)}, u32[]{:S(2)}, u32[]{:S(2)}) collective-permute-start(bf16[4,4352]{1,0:T(4,128)(2,1)S(1)} %get-tuple-element.10.own_ref), channel_id=1, source_target_pairs={{0,10},{1,3},{2,8},{3,1},{4,14},{5,7},{6,12},{7,5},{8,2},{9,11},{1... | collective-permute-start | bytes 104456 | tf_op jit(solution)/shard_map/ppermute | solution.py:301
  20.9 0.0 collective-permute-start.5
  20.9 2.0 %collective-permute-start.6 = (bf16[4,4352]{1,0:T(4,128)(2,1)S(1)}, bf16[4,4352]{1,0:T(4,128)(2,1)S(1)}, u32[]{:S(2)}, u32[]{:S(2)}) collective-permute-start(bf16[4,4352]{1,0:T(4,128)(2,1)S(1)} %get-tuple-element.9), channel_id=1, source_target_pairs={{0,6},{1,15},{2,4},{3,13},{4,2},{5,11},{6,0},{7,9},{8,14},{9,7},{1... | collective-permute-start | bytes 104456 | tf_op jit(solution)/shard_map/ppermute | solution.py:301
  22.9 0.0 collective-permute-done.7.three_ref
  22.9 0.2 collective-permute-done.8.four_ref
  23.1 1.7 %collective-permute-done.5.one_ref = bf16[4,4352]{1,0:T(4,128)(2,1)S(1)} collective-permute-done((bf16[4,4352]{1,0:T(4,128)(2,1)S(1)}, bf16[4,4352]{1,0:T(4,128)(2,1)S(1)}, u32[]{:S(2)}, u32[]{:S(2)}) %collective-permute-start.5) | collective-permute-done | bytes 34848 | tf_op jit(solution)/shard_map/ppermute | solution.py:301
  24.8 0.9 %collective-permute-done.6.two_ref = bf16[4,4352]{1,0:T(4,128)(2,1)S(1)} collective-permute-done((bf16[4,4352]{1,0:T(4,128)(2,1)S(1)}, bf16[4,4352]{1,0:T(4,128)(2,1)S(1)}, u32[]{:S(2)}, u32[]{:S(2)}) %collective-permute-start.6) | collective-permute-done | bytes 34848 | tf_op jit(solution)/shard_map/ppermute | solution.py:301
  25.7 0.6 %shard_map.69.own_ref = f32[4,4352]{1,0:T(4,128)S(1)} custom-call(s32[2]{0:T(128)S(1)} %pad_add_fusion.core_ref.place_ref, bf16[4,4352]{1,0:T(4,128)(2,1)S(1)} %collective-permute-done.5.one_ref, bf16[4,4352]{1,0:T(4,128)(2,1)S(1)} %collective-permute-done.6.two_ref, bf16[4,4352]{1,0:T(4,128)(2,1)S(1)} %collective-permute-done.7.three_ref, ...), custom_call_target="tpu_custom_call" | custom-call | tf_op jit(solution)/shard_map/pallas_call | solution.py:307
  26.3 0.1 collective-permute-start.9
  26.4 1.2 %collective-permute-done.9.other_ref = f32[4,4352]{1,0:T(4,128)S(1)} collective-permute-done((f32[4,4352]{1,0:T(4,128)S(1)}, f32[4,4352]{1,0:T(4,128)S(1)}, u32[]{:S(2)}, u32[]{:S(2)}) %collective-permute-start.9) | collective-permute-done | bytes 69664 | tf_op jit(solution)/shard_map/ppermute | solution.py:301
  27.6 1.3 %shard_map.70 = (f32[4,4096]{1,0:T(4,128)}, f32[1,4]{1,0:T(1,128)}, f32[1,64]{1,0:T(1,128)}) custom-call(s32[2]{0:T(128)S(1)} %pad_add_fusion.core_ref.place_ref, f32[4,4352]{1,0:T(4,128)S(1)} %shard_map.69.own_ref, f32[4,4352]{1,0:T(4,128)S(1)} %collective-permute-done.9.other_ref, f32[1,128]{1,0:T(1,128)S(1)} %get-tuple-element.11.total_ref), custom_call_target="tpu_custom_call" | custom-call | tf_op jit(solution)/shard_map/pallas_call | solution.py:307
Async XLA Ops:
  0.6 6.6 %collective-permute-start.4 = (bf16[64,4096]{1,0:T(8,128)(2,1)}, bf16[64,4096]{1,0:T(8,128)(2,1)S(1)}, u32[]{:S(2)}, u32[]{:S(2)}) collective-permute-start(bf16[64,4096]{1,0:T(8,128)(2,1)} %own_ref.2), channel_id=1, source_target_pairs={{0,1},{1,0},{2,3},{3,2},{4,5},{5,4},{6,7},{7,6},{8,9},{9,8},{10,11... | collective-permute-start | bytes 1572872 | tf_op jit(solution)/shard_map/ppermute | solution.py:301
  1.1 8.7 %collective-permute-start.1 = (bf16[4,4096]{1,0:T(4,128)(2,1)}, bf16[4,4096]{1,0:T(4,128)(2,1)S(1)}, u32[]{:S(2)}, u32[]{:S(2)}) collective-permute-start(bf16[4,4096]{1,0:T(4,128)(2,1)} %own_ref.3), channel_id=1, source_target_pairs={{0,4},{4,0},{8,12},{12,8},{1,5},{5,1},{9,13},{13,9},{2,6},{6,2},{1... | collective-permute-start | bytes 98312 | tf_op jit(solution)/shard_map/ppermute | solution.py:301
  3.8 6.0 %collective-permute-start.2 = (bf16[4,4096]{1,0:T(4,128)(2,1)}, bf16[4,4096]{1,0:T(4,128)(2,1)S(1)}, u32[]{:S(2)}, u32[]{:S(2)}) collective-permute-start(bf16[4,4096]{1,0:T(4,128)(2,1)} %own_ref.3), channel_id=1, source_target_pairs={{0,8},{4,12},{8,0},{12,4},{1,9},{5,13},{9,1},{13,5},{2,10},{6,14},... | collective-permute-start | bytes 98312 | tf_op jit(solution)/shard_map/ppermute | solution.py:301
  6.4 5.9 %collective-permute-start.3 = (bf16[4,4096]{1,0:T(4,128)(2,1)}, bf16[4,4096]{1,0:T(4,128)(2,1)S(1)}, u32[]{:S(2)}, u32[]{:S(2)}) collective-permute-start(bf16[4,4096]{1,0:T(4,128)(2,1)} %own_ref.3), channel_id=1, source_target_pairs={{0,12},{4,8},{8,4},{12,0},{1,13},{5,9},{9,5},{13,1},{2,14},{6,10},... | collective-permute-start | bytes 98312 | tf_op jit(solution)/shard_map/ppermute | solution.py:301
  7.1 2.7 %collective-permute-start = (s32[1,8]{1,0:T(1,128)S(1)}, s32[1,8]{1,0:T(1,128)S(1)}, u32[]{:S(2)}, u32[]{:S(2)}) collective-permute-start(s32[1,8]{1,0:T(1,128)S(1)} %pad_add_fusion.1.table_ref), channel_id=1, source_target_pairs={{0,1},{1,0},{2,3},{3,2},{4,5},{5,4},{6,7},{7,6},{8,9},{9,8},{10,11... | collective-permute-start | bytes 104 | tf_op jit(solution)/shard_map/ppermute | solution.py:301
  7.2 1.0 %copy-start = (bf16[64,4096]{1,0:T(8,128)(2,1)S(1)}, bf16[64,4096]{1,0:T(8,128)(2,1)}, u32[]{:S(2)}) copy-start(bf16[64,4096]{1,0:T(8,128)(2,1)} %own_ref.2) | copy-start | bytes 1572868
  8.3 4.1 %copy-start.1 = (bf16[4,4096]{1,0:T(4,128)(2,1)S(1)}, bf16[4,4096]{1,0:T(4,128)(2,1)}, u32[]{:S(2)}) copy-start(bf16[4,4096]{1,0:T(4,128)(2,1)} %own_ref.3) | copy-start | bytes 98308
  15.0 7.8 %collective-permute-start.7 = (bf16[4,4352]{1,0:T(4,128)(2,1)S(1)}, bf16[4,4352]{1,0:T(4,128)(2,1)S(1)}, u32[]{:S(2)}, u32[]{:S(2)}) collective-permute-start(bf16[4,4352]{1,0:T(4,128)(2,1)S(1)} %get-tuple-element.10.own_ref), channel_id=1, source_target_pairs={{0,8},{2,10},{4,12},{6,14},{8,0},{10,2},{12,4},{14,6},{16,24},{18,... | collective-permute-start | bytes 104456 | tf_op jit(solution)/shard_map/ppermute | solution.py:301
  17.0 6.1 %collective-permute-start.8 = (bf16[4,4352]{1,0:T(4,128)(2,1)S(1)}, bf16[4,4352]{1,0:T(4,128)(2,1)S(1)}, u32[]{:S(2)}, u32[]{:S(2)}) collective-permute-start(bf16[4,4352]{1,0:T(4,128)(2,1)S(1)} %get-tuple-element.10.own_ref), channel_id=1, source_target_pairs={{0,10},{1,3},{2,8},{3,1},{4,14},{5,7},{6,12},{7,5},{8,2},{9,11},{1... | collective-permute-start | bytes 104456 | tf_op jit(solution)/shard_map/ppermute | solution.py:301
  20.9 3.9 %collective-permute-start.5 = (bf16[4,4352]{1,0:T(4,128)(2,1)S(1)}, bf16[4,4352]{1,0:T(4,128)(2,1)S(1)}, u32[]{:S(2)}, u32[]{:S(2)}) collective-permute-start(bf16[4,4352]{1,0:T(4,128)(2,1)S(1)} %get-tuple-element.9), channel_id=1, source_target_pairs={{0,4},{1,13},{2,6},{3,15},{4,0},{5,9},{6,2},{7,11},{8,12},{9,5},{1... | collective-permute-start | bytes 104456 | tf_op jit(solution)/shard_map/ppermute | solution.py:301
  20.9 4.8 %collective-permute-start.6 = (bf16[4,4352]{1,0:T(4,128)(2,1)S(1)}, bf16[4,4352]{1,0:T(4,128)(2,1)S(1)}, u32[]{:S(2)}, u32[]{:S(2)}) collective-permute-start(bf16[4,4352]{1,0:T(4,128)(2,1)S(1)} %get-tuple-element.9), channel_id=1, source_target_pairs={{0,6},{1,15},{2,4},{3,13},{4,2},{5,11},{6,0},{7,9},{8,14},{9,7},{1... | collective-permute-start | bytes 104456 | tf_op jit(solution)/shard_map/ppermute | solution.py:301
  26.3 1.3 %collective-permute-start.9 = (f32[4,4352]{1,0:T(4,128)S(1)}, f32[4,4352]{1,0:T(4,128)S(1)}, u32[]{:S(2)}, u32[]{:S(2)}) collective-permute-start(f32[4,4352]{1,0:T(4,128)S(1)} %shard_map.69.own_ref), channel_id=1, source_target_pairs={{0,1},{1,0},{2,3},{3,2},{4,5},{5,4},{6,7},{7,6},{8,9},{9,8},{10,11... | collective-permute-start | bytes 208904 | tf_op jit(solution)/shard_map/ppermute | solution.py:301

commit v2 on v1

--- a/solution.py
+++ b/solution.py
@@ -20,9 +20,18 @@
     return jnp.concatenate([tile[:, by:], tile[:, :by]], axis=1)
 
 
-def turn_kernel(own_ref, other_ref, out_ref, wide_ref):
-    pixels = own_ref.shape[1]
+def turn_kernel(own_hbm, other_ref, out_ref, own_ref, wide_ref, arrived):
+    pixels = other_ref.shape[1]
+    pieces = arrived.shape[0]
+    width = pixels // pieces
+    copies = []
+    for piece in range(pieces):
+        span = pl.ds(piece * width, width)
+        copies.append(pltpu.make_async_copy(own_hbm.at[:, span], own_ref.at[:, span], arrived.at[piece]))
+        copies[-1].start()
     for block in range(pixels // LANES):
+        if block * LANES % width == 0:
+            copies[block * LANES // width].wait()
         span = slice(block * LANES, (block + 1) * LANES)
         tile = jnp.concatenate([own_ref[:, span], other_ref[:, span]], axis=0)
         tile = tile.astype(F32).T
@@ -41,95 +50,97 @@
     return high, middle, (rest - middle).astype(BF16).astype(F32)
 
 
-def slot_column(table_ref, rows, capacity):
-    mic_count = table_ref.shape[1] // 2
-    position = lax.broadcasted_iota(jnp.int32, (rows, 1), 0)
-    slot = jnp.full((rows, 1), -1, jnp.int32)
+def slot_row(counts_ref, owners_ref, capacity):
+    mic_count = counts_ref.shape[1]
+    position = lax.broadcasted_iota(jnp.int32, (1, LANES), 1)
+    slot = jnp.full((1, LANES), -1, jnp.int32)
     start = jnp.int32(0)
     for mic in range(mic_count):
-        owner = table_ref[0, mic_count + mic]
+        owner = owners_ref[0, mic]
         before = jnp.int32(0)
         for earlier in range(mic):
-            same = table_ref[0, mic_count + earlier] == owner
-            before = before + jnp.where(same, table_ref[0, earlier], 0)
-        stop = start + table_ref[0, mic]
+            before = before + jnp.where(owners_ref[0, earlier] == owner, counts_ref[0, earlier], 0)
+        stop = start + counts_ref[0, mic]
         inside = (position >= start) & (position < stop)
         slot = jnp.where(inside, position + (owner * capacity + before - start), slot)
         start = stop
-    return slot, start
-
-
-def weigh_kernel(capacity, core_ref, table_ref, other_table_ref, one_ref, two_ref, three_ref, own_ref,
-                 images_ref, first_ref, second_ref, total_ref, flipped_ref, sums_ref):
-    core = core_ref[0]
+    return slot
+
+
+def mirror_of_rows():
+    row = lax.broadcasted_iota(jnp.int32, (LANES, LANES), 0)
+    column = lax.broadcasted_iota(jnp.int32, (LANES, LANES), 1)
+    return (column == (row // BOX) * BOX + (BOX - 1 - row % BOX)).astype(BF16)
+
+
+def spans(pixels):
+    return [slice(b * LANES, (b + 1) * LANES) for b in range(pixels // LANES)]
+
+
+def score_kernel(capacity, counts_ref, owners_ref, first_ref, second_ref, own_ref, images_ref, scores_ref, stats_ref, flipped_ref):
     per_dev, pixels = own_ref.shape
-    classes = 4 * per_dev
-    blocks = pixels // LANES
-    rows = LANES // 2
-    half = classes // 2
-    block_of = [slice(b * LANES, (b + 1) * LANES) for b in range(blocks)]
-    row_of = lax.broadcasted_iota(jnp.int32, (LANES, LANES), 0)
-    column_of = lax.broadcasted_iota(jnp.int32, (LANES, LANES), 1)
-    within = (row_of // BOX) * BOX + (BOX - 1 - row_of % BOX)
-    mirror = (column_of == within).astype(BF16)
-
-    refs = jnp.concatenate([one_ref[...].astype(F32), two_ref[...].astype(F32),
-                            three_ref[...].astype(F32), own_ref[...].astype(F32)], axis=0)
+    half = 2 * per_dev
+    block_of = spans(pixels)
+    second = jnp.where(lax.axis_index("rd") == 0, second_ref[...].astype(F32), own_ref[...].astype(F32))
+    refs = jnp.concatenate([first_ref[...].astype(F32), second], axis=0)
     squares = jnp.sum(refs * refs, axis=1, keepdims=True)
     stacked = jnp.concatenate([refs[:, b] for b in block_of], axis=0)
-    mirrored = jnp.dot(stacked.astype(BF16), mirror, preferred_element_type=F32)
-    for b in range(blocks):
-        part = slice(b * classes, (b + 1) * classes)
-        plain, turned = stacked[part], mirrored[part]
-        back = block_of[blocks - 1 - b]
-        flipped_ref[0:classes, block_of[b]] = plain.astype(BF16)
-        flipped_ref[classes:2 * classes, block_of[b]] = turned.astype(BF16)
-        flipped_ref[2 * classes:3 * classes, back] = rolled(plain, BOX).astype(BF16)
-        flipped_ref[3 * classes:4 * classes, back] = rolled(turned, BOX).astype(BF16)
-
+    mirrored = jnp.dot(stacked.astype(BF16), mirror_of_rows(), preferred_element_type=F32)
+    for b in range(len(block_of)):
+        part = slice(b * half, (b + 1) * half)
+        both = jnp.concatenate([stacked[part], mirrored[part]], axis=0)
+        flipped_ref[:2 * half, block_of[b]] = both.astype(BF16)
+        flipped_ref[2 * half:, block_of[-1 - b]] = rolled(both, BOX).astype(BF16)
     inner = jnp.dot(flipped_ref[...], images_ref[...], preferred_element_type=F32)
     scores = inner - 0.5 * jnp.concatenate([squares] * 4, axis=0)
+    scores_ref[...] = scores
     highest = jnp.max(scores, axis=0, keepdims=True)
     highest = jnp.maximum(highest[:, :LANES], highest[:, LANES:])
-    shifted = jnp.exp(scores - jnp.concatenate([highest, highest], axis=1))
-    summed = jnp.sum(shifted, axis=0, keepdims=True)
-    total = jnp.log(summed[:, :LANES] + summed[:, LANES:]) + highest
-
-    slot, used = slot_column(table_ref, rows, capacity)
-    other_slot, other_used = slot_column(other_table_ref, rows, capacity)
+    summed = jnp.sum(jnp.exp(scores - jnp.concatenate([highest, highest], axis=1)), axis=0, keepdims=True)
+    summed = summed[:, :LANES] + summed[:, LANES:]
+    slot = slot_row(counts_ref, owners_ref, capacity).astype(F32)
+    stats_ref[...] = jnp.concatenate([highest, summed, slot, jnp.zeros((5, LANES), F32)], axis=0)
+
+
+def weigh_kernel(scores_ref, stats_ref, other_stats_ref, images_ref, first_ref, second_ref, total_ref, sums_ref):
+    per_dev = first_ref.shape[0]
+    pixels = images_ref.shape[0]
+    rows = LANES // 2
+    half = 2 * per_dev
+    block_of = spans(pixels)
+    scores = scores_ref[...]
+    other = rolled(other_stats_ref[...], BOX)
+    highest = jnp.maximum(stats_ref[0:1], other[0:1])
+    summed = stats_ref[1:2] * jnp.exp(stats_ref[0:1] - highest) + other[1:2] * jnp.exp(other[0:1] - highest)
+    total = jnp.log(summed) + highest
+
     lane = lax.broadcasted_iota(jnp.int32, (1, LANES), 1)
-    live = (lane < used) | ((lane >= rows) & (lane < rows + other_used))
+    slot = jnp.where(lane < rows, stats_ref[2:3], other[2:3]).astype(jnp.int32)
+    live = slot >= 0
+    slot = jnp.where(live & (lane >= rows), slot + rows, slot)
     live = jnp.concatenate([live, live], axis=1)
-    weights = jnp.where(live, jnp.exp(scores - jnp.concatenate([total, total], axis=1)), 0.0)
-    weights = weights.astype(BF16).astype(F32)
-    chosen = jnp.concatenate(
-        [
-            jnp.where(core == 0, weights[f * classes:f * classes + half],
-                      weights[f * classes + half:(f + 1) * classes])
-            for f in range(4)
-        ],
-        axis=0,
-    )
+    weights = jnp.where(live, jnp.exp(scores - jnp.concatenate([total, total], axis=1)), 0.0).astype(BF16)
     sums_ref[...] = lax.dot_general(
-        chosen.astype(BF16), images_ref[...], (((1,), (1,)), ((), ())), preferred_element_type=F32
+        weights, images_ref[...], (((1,), (1,)), ((), ())), preferred_element_type=F32
     )
     straight, swapped = [], []
-    for b in range(blocks):
-        back = block_of[blocks - 1 - b]
+    for b in range(len(block_of)):
+        back = block_of[-1 - b]
         straight.append(sums_ref[0:half, block_of[b]] + rolled(sums_ref[2 * half:3 * half, back], BOX))
         swapped.append(sums_ref[half:2 * half, block_of[b]] + rolled(sums_ref[3 * half:, back], BOX))
     swapped = jnp.concatenate(swapped, axis=0)
     upper = swapped.astype(BF16)
     lower = (swapped - upper.astype(F32)).astype(BF16)
+    mirror = mirror_of_rows()
     swapped = jnp.dot(upper, mirror, preferred_element_type=F32) + jnp.dot(
         lower, mirror, preferred_element_type=F32
     )
-    for b in range(blocks):
+    for b in range(len(block_of)):
         both = straight[b] + swapped[b * half:(b + 1) * half]
         first_ref[:, block_of[b]] = both[:per_dev].astype(BF16)
         second_ref[:, block_of[b]] = both[per_dev:].astype(BF16)
 
-    per_class = jnp.sum(chosen, axis=1, keepdims=True)
+    per_class = jnp.sum(weights.astype(F32), axis=1, keepdims=True)
     per_class = per_class[0:half] + per_class[half:2 * half] + per_class[2 * half:3 * half] + per_class[3 * half:]
     high, middle, low = three_parts(per_class)
     lanes = lax.broadcasted_iota(jnp.int32, (half, LANES), 1)
@@ -138,20 +149,20 @@
     first_ref[:, extra] = sent[:per_dev].astype(BF16)
     second_ref[:, extra] = sent[per_dev:].astype(BF16)
 
-    column = jnp.concatenate([slot, jnp.where(other_slot < 0, -1, other_slot + rows)], axis=0)
-    placing = (column == column_of).astype(BF16)
-    high, middle, low = three_parts(total)
-    pieces = jnp.concatenate([high, middle, low, jnp.zeros((5, LANES), F32)], axis=0)
-    pieces = jnp.dot(pieces.astype(BF16), placing, preferred_element_type=F32)
+    placing = (slot == lax.broadcasted_iota(jnp.int32, (LANES, LANES), 0)).astype(BF16)
+    pieces = jnp.concatenate([*three_parts(total), jnp.zeros((5, LANES), F32)], axis=0)
+    pieces = lax.dot_general(
+        pieces.astype(BF16), placing, (((1,), (1,)), ((), ())), preferred_element_type=F32
+    )
     total_ref[...] = pieces[0:1] + pieces[1:2] + pieces[2:3]
     last = slice(pixels + LANES, pixels + 2 * LANES)
     first_ref[:, last] = jnp.zeros((per_dev, LANES), BF16)
     second_ref[:, last] = pieces[:per_dev].astype(BF16)
 
 
-def add_kernel(core_ref, one_ref, two_ref, three_ref, four_ref, own_ref, out_ref):
+def add_kernel(two_ref, one_ref, three_ref, four_ref, own_ref, out_ref):
     pixels = out_ref.shape[1] - LANES
-    middle = jnp.where(core_ref[0] == 0, three_ref[:, :pixels].astype(F32), own_ref[:, :pixels].astype(F32))
+    middle = jnp.where(lax.axis_index("rd") == 0, three_ref[:, :pixels].astype(F32), own_ref[:, :pixels].astype(F32))
     out_ref[:, :pixels] = (one_ref[:, :pixels].astype(F32) + two_ref[:, :pixels].astype(F32)) + (
         middle + four_ref[:, :pixels].astype(F32)
     )
@@ -159,24 +170,40 @@
     out_ref[:, pixels:] = jnp.broadcast_to(pieces[0:1] + pieces[1:2] + pieces[2:3], (out_ref.shape[0], LANES))
 
 
-def finish_kernel(place_ref, own_ref, other_ref, total_ref, means_ref, weights_ref, loglik_ref):
-    core, image = place_ref[0], place_ref[1]
+def finish_kernel(own_ref, other_ref, total_ref, means_hbm, weights_hbm, loglik_hbm,
+                  means_ref, weights_ref, loglik_ref, sent):
     per_dev, pixels = means_ref.shape
     capacity = loglik_ref.shape[1] // 2
     extra = slice(pixels, pixels + LANES)
+    last = slice(pixels + LANES, pixels + 2 * LANES)
+    pieces = sent.shape[0] - 2
+    width = pixels // pieces
     count = own_ref[:, extra] + other_ref[:, extra]
     count = count[:, 0:1] + count[:, 1:2] + count[:, 2:3]
-    means_ref[...] = (own_ref[:, :pixels] + other_ref[:, :pixels]) / (count + 1.0)
+    scale = 1.0 / (count + 1.0)
+    copies = []
+    for piece in range(pieces):
+        span = pl.ds(piece * width, width)
+        means_ref[:, span] = (own_ref[:, span] + other_ref[:, span]) * scale
+        copies.append(pltpu.make_async_copy(means_ref.at[:, span], means_hbm.at[:, span], sent.at[piece]))
+        copies[-1].start()
     across = lax.broadcasted_iota(jnp.int32, (per_dev, per_dev), 1)
     down = lax.broadcasted_iota(jnp.int32, (per_dev, per_dev), 0)
     weights_ref[...] = jnp.sum(jnp.where(across == down, count, 0.0), axis=0, keepdims=True)
-    last = slice(pixels + LANES, pixels + 2 * LANES)
-    arrived = jnp.where(core == 0, rolled(other_ref[0:1, last], 2 * capacity), own_ref[0:1, last])
-    mine = total_ref[...]
-    arrived = jnp.where(image == 0, arrived[:, :capacity], arrived[:, capacity:2 * capacity])
-    mine = jnp.where(image == 0, mine[:, :capacity], mine[:, capacity:2 * capacity])
-    loglik_ref[:, :capacity] = jnp.where(image == 0, mine, arrived)
-    loglik_ref[:, capacity:] = jnp.where(image == 0, arrived, mine)
+    copies.append(pltpu.make_async_copy(weights_ref, weights_hbm, sent.at[pieces]))
+    copies[-1].start()
+    first = lax.axis_index("img") == 0
+    arrived = jnp.where(
+        lax.axis_index("rd") == 0, rolled(other_ref[0:1, last], 2 * capacity), own_ref[0:1, last]
+    )
+    arrived = jnp.where(first, arrived[:, :capacity], arrived[:, capacity:2 * capacity])
+    mine = jnp.where(first, total_ref[:, :capacity], total_ref[:, capacity:2 * capacity])
+    loglik_ref[:, :capacity] = jnp.where(first, mine, arrived)
+    loglik_ref[:, capacity:] = jnp.where(first, arrived, mine)
+    copies.append(pltpu.make_async_copy(loglik_ref, loglik_hbm, sent.at[pieces + 1]))
+    copies[-1].start()
+    for copy in copies:
+        copy.wait()
 
 
 def passed_along(array, axis, by):
@@ -301,14 +328,17 @@
     return lax.ppermute(array, axes, pairs)
 
 
-def call(kernel, outs, args, scalars, scratch=()):
-    specs = [pl.BlockSpec(memory_space=pltpu.SMEM)] * scalars
-    specs += [pl.BlockSpec(memory_space=pltpu.VMEM)] * (len(args) - scalars)
+def call(kernel, outs, args, scalars=(), scratch=(), in_hbm=(), outs_in_hbm=False):
+    specs = [
+        pl.BlockSpec(memory_space=pltpu.SMEM if i in scalars else pltpu.HBM if i in in_hbm else pltpu.VMEM)
+        for i in range(len(args))
+    ]
+    out_space = pltpu.HBM if outs_in_hbm else pltpu.VMEM
     return pl.pallas_call(
         kernel,
         out_shape=outs,
         in_specs=specs,
-        out_specs=jax.tree.map(lambda _: pl.BlockSpec(memory_space=pltpu.VMEM), outs),
+        out_specs=jax.tree.map(lambda _: pl.BlockSpec(memory_space=out_space), outs),
         scratch_shapes=list(scratch),
         compiler_params=pltpu.CompilerParams(vmem_limit_bytes=32 * 1024 * 1024),
     )(*args)
@@ -318,32 +348,39 @@
     read_rows, pixels = images.shape
     capacity = read_rows // lax.axis_size("img")
     per_dev = references.shape[0]
-    core = lax.axis_index("rd")
-    place = jnp.stack([core, lax.axis_index("img")]).astype(jnp.int32)
-    table = jnp.concatenate([counts, owners], axis=1)
     other_images = swapped_by(images, 1, ("rd",))
-    other_table = swapped_by(table, 1, ("rd",))
-    near, far, cross = [swapped_by(references, k, ("cls",)) for k in (1, 2, 3)]
+    ref_far = swapped_by(references, lambda rd: 12 if rd else 8)
+    ref_near = swapped_by(references, 4)
     shape = jax.ShapeDtypeStruct
-    turned = call(turn_kernel, shape((pixels, 2 * LANES), BF16), (images, other_images), 0,
-                  [pltpu.VMEM((pixels, LANES), F32)])
+    turned = call(
+        turn_kernel, shape((pixels, 2 * LANES), BF16), (images, other_images), (),
+        [pltpu.VMEM((read_rows, pixels), BF16), pltpu.VMEM((pixels, LANES), F32), pltpu.SemaphoreType.DMA((4,))],
+        in_hbm=(0,),
+    )
+    scores, stats = call(
+        functools.partial(score_kernel, capacity),
+        (shape((8 * per_dev, 2 * LANES), F32), shape((8, LANES), F32)),
+        (counts, owners, ref_far, ref_near, references, turned), (0, 1),
+        [pltpu.VMEM((8 * per_dev, pixels), BF16)],
+    )
+    other_stats = swapped_by(stats, 1, ("rd",))
     wide = pixels + 2 * LANES
-    first, second, totals = call(
-        functools.partial(weigh_kernel, capacity),
+    far, near, totals = call(
+        weigh_kernel,
         (shape((per_dev, wide), BF16), shape((per_dev, wide), BF16), shape((1, LANES), F32)),
-        (place, table, other_table, near, far, cross, references, turned), 3,
-        [pltpu.VMEM((16 * per_dev, pixels), BF16), pltpu.VMEM((8 * per_dev, pixels), F32)],
-    )
-    one = swapped_by(first, lambda rd: 12 if rd else 4)
-    two = swapped_by(first, lambda rd: 14 if rd else 6)
-    three = swapped_by(second, lambda rd: 0 if rd else 8)
-    four = swapped_by(second, lambda rd: 2 if rd else 10)
-    summed = call(add_kernel, shape((per_dev, wide), F32), (place, one, two, three, four, second), 1)
+        (scores, stats, other_stats, turned), (), [pltpu.VMEM((8 * per_dev, pixels), F32)],
+    )
+    two = swapped_by(far, lambda rd: 14 if rd else 10)
+    one = swapped_by(far, lambda rd: 12 if rd else 8)
+    four = swapped_by(near, lambda rd: 2 if rd else 6)
+    three = swapped_by(near, 4)
+    summed = call(add_kernel, shape((per_dev, wide), F32), (two, one, three, four, near))
     other = swapped_by(summed, 1, ("rd",))
+    outs = (shape((per_dev, pixels), F32), shape((1, per_dev), F32), shape((1, read_rows), F32))
     means, weights, loglik = call(
-        finish_kernel,
-        (shape((per_dev, pixels), F32), shape((1, per_dev), F32), shape((1, read_rows), F32)),
-        (place, summed, other, totals), 1,
+        finish_kernel, outs, (summed, other, totals), (),
+        [pltpu.VMEM(out.shape, out.dtype) for out in outs] + [pltpu.SemaphoreType.DMA((6,))],
+        outs_in_hbm=True,
     )
     return means, weights.reshape(per_dev), loglik.reshape(read_rows)
 

time: 29.1 us -> 24.8 us (0.85)
  starting transfers between devices: 13.7 us -> 11.8 us
  Pallas kernels: 6.14 us -> 5.05 us
  other arithmetic: 0.82 us -> 0 us
  waiting for transfers between devices: 6.56 us -> 5.99 us
    ppermute x10 -> x9, starting transfers between devices: 13.7 us -> 11.8 us  [swapped_by(): return lax.ppermute(array, axes, pairs)]
    pallas_call x4 -> x5, Pallas kernels: 6.14 us -> 5.05 us  [call(): pl.pallas_call(kernel, out_shape=outs, in_specs=specs, out_specs=jax.tree...]
    concatenate x1 -> x0, other arithmetic: 0.75 us -> none  [direct(): table = jnp.concatenate([counts, owners], axis=1)]
    ppermute x10 -> x9, waiting for transfers between devices: 6.56 us -> 5.99 us  [swapped_by(): return lax.ppermute(array, axes, pairs)]
    unnamed x4 -> x8, local copies, waits for them, and re-layouts: 1.05 us -> 1.05 us
  transfers between devices with their start and end apart: 10 -> 9, of which waited for: 5 -> 3; matrix products, arithmetic and copies ran while one was open for 3% -> 0% of each run, Pallas kernels for 5% -> 8%
where the time goes in v2:
time: 24.8 us; the launch traced here: 24.6 us
  starting transfers between devices  11.8 us (48%)
  waiting for transfers between devices  5.99 us (24%)
  Pallas kernels  5.05 us (20%)
  local copies, waits for them, and re-layouts  1.05 us (4%)
  between operations  0.72 us (3%)
    ppermute x9, starting transfers between devices, swapped_by(): return lax.ppermute(array, axes, pairs)  11.8 us
    ppermute x9, waiting for transfers between devices, swapped_by(): return lax.ppermute(array, axes, pairs)  5.99 us
    pallas_call x5, Pallas kernels, call(): pl.pallas_call(kernel, out_shape=outs, in_specs=specs, out_specs=jax.tree...  5.05 us
    unnamed x8, local copies, waits for them, and re-layouts  1.05 us
  transfers between devices with their start and end apart: 9, of which 3 were waited for; matrix products, arithmetic and copies ran while one was open for 0% of the time, Pallas kernels for 8%

profile of v2, /device:TPU:0, one launch (start us, length us, event | category | flops | bytes accessed | tf_op | source)
XLA Modules:
  0.0 24.6 jit_solution(15107979408449087534)
XLA Ops:
  0.6 0.5 %collective-permute-start.2 = (bf16[64,4096]{1,0:T(8,128)(2,1)}, bf16[64,4096]{1,0:T(8,128)(2,1)S(1)}, u32[]{:S(2)}, u32[]{:S(2)}) collective-permute-start(bf16[64,4096]{1,0:T(8,128)(2,1)} %own_hbm.1), channel_id=1, source_target_pairs={{0,1},{1,0},{2,3},{3,2},{4,5},{5,4},{6,7},{7,6},{8,9},{9,8},{10,11... | collective-permute-start | bytes 1572872 | tf_op jit(solution)/shard_map/ppermute | solution.py:328
  1.1 3.7 %collective-permute-start = (bf16[4,4096]{1,0:T(4,128)(2,1)}, bf16[4,4096]{1,0:T(4,128)(2,1)S(1)}, u32[]{:S(2)}, u32[]{:S(2)}) collective-permute-start(bf16[4,4096]{1,0:T(4,128)(2,1)} %own_ref.1), channel_id=1, source_target_pairs={{0,8},{1,13},{2,10},{3,15},{4,12},{5,9},{6,14},{7,11},{8,0},{9,5},... | collective-permute-start | bytes 98312 | tf_op jit(solution)/shard_map/ppermute | solution.py:328
  4.8 1.6 %collective-permute-start.1 = (bf16[4,4096]{1,0:T(4,128)(2,1)}, bf16[4,4096]{1,0:T(4,128)(2,1)S(1)}, u32[]{:S(2)}, u32[]{:S(2)}) collective-permute-start(bf16[4,4096]{1,0:T(4,128)(2,1)} %own_ref.1), channel_id=1, source_target_pairs={{0,4},{1,5},{2,6},{3,7},{4,0},{5,1},{6,2},{7,3},{8,12},{9,13},{10,... | collective-permute-start | bytes 98312 | tf_op jit(solution)/shard_map/ppermute | solution.py:328
  6.4 0.0 collective-permute-done.2.other_ref
  6.4 0.0 copy-start
  6.4 1.0 %copy-done = bf16[64,4096]{1,0:T(8,128)(2,1)S(1)} copy-done((bf16[64,4096]{1,0:T(8,128)(2,1)S(1)}, bf16[64,4096]{1,0:T(8,128)(2,1)}, u32[]{:S(2)}) %copy-start) | copy-done | bytes 524312
  7.4 0.0 copy-start.1
  7.4 0.0 copy-start.2
  7.4 0.0 copy-start.3
  7.4 2.0 %shard_map.67.images_ref = bf16[4096,256]{1,0:T(8,128)(2,1)S(1)} custom-call(bf16[64,4096]{1,0:T(8,128)(2,1)S(1)} %copy-done, bf16[64,4096]{1,0:T(8,128)(2,1)S(1)} %collective-permute-done.2.other_ref), custom_call_target="tpu_custom_call" | custom-call | tf_op jit(solution)/shard_map/pallas_call | solution.py:337
  9.5 0.0 collective-permute-done.first_ref
  9.5 0.0 collective-permute-done.1.second_ref
  9.5 0.0 copy-done.1
  9.5 0.0 copy-done.2
  9.5 0.0 copy-done.3
  9.5 1.2 %shard_map.68 = (f32[32,256]{1,0:T(8,128)S(1)}, f32[8,128]{1,0:T(8,128)S(1)}) custom-call(s32[1,4]{1,0:T(1,128)S(1)} %copy-done.2, s32[1,4]{1,0:T(1,128)S(1)} %copy-done.3, bf16[4,4096]{1,0:T(4,128)(2,1)S(1)} %collective-permute-done.first_ref, bf16[4,4096]{1,0:T(4,128)(2,1)S(1)} %collective-permute-done.1.second_ref, bf16[4,4096]{1,0:T(4,128)(2,1)S(1)} %copy-done.1, ...), custom_call_target="tpu_custom_call" | custom-call | tf_op jit(solution)/shard_map/pallas_call | solution.py:337
  10.7 0.1 collective-permute-start.3
  10.8 1.2 %collective-permute-done.3.other_stats_ref = f32[8,128]{1,0:T(8,128)S(1)} collective-permute-done((f32[8,128]{1,0:T(8,128)S(1)}, f32[8,128]{1,0:T(8,128)S(1)}, u32[]{:S(2)}, u32[]{:S(2)}) %collective-permute-start.3) | collective-permute-done | bytes 4128 | tf_op jit(solution)/shard_map/ppermute | solution.py:328
  11.9 1.0 %shard_map.69 = (bf16[4,4352]{1,0:T(4,128)(2,1)S(1)}, bf16[4,4352]{1,0:T(4,128)(2,1)S(1)}, f32[1,128]{1,0:T(1,128)S(1)}) custom-call(f32[32,256]{1,0:T(8,128)S(1)} %get-tuple-element.11.scores_ref, f32[8,128]{1,0:T(8,128)S(1)} %get-tuple-element.12.stats_ref, f32[8,128]{1,0:T(8,128)S(1)} %collective-permute-done.3.other_stats_ref, ...), custom_call_target="tpu_custom_call" | custom-call | tf_op jit(solution)/shard_map/pallas_call | solution.py:337
  12.9 1.1 %collective-permute-start.6 = (bf16[4,4352]{1,0:T(4,128)(2,1)S(1)}, bf16[4,4352]{1,0:T(4,128)(2,1)S(1)}, u32[]{:S(2)}, u32[]{:S(2)}) collective-permute-start(bf16[4,4352]{1,0:T(4,128)(2,1)S(1)} %get-tuple-element.14.own_ref), channel_id=1, source_target_pairs={{0,4},{1,5},{2,6},{3,7},{4,0},{5,1},{6,2},{7,3},{8,12},{9,13},{10,... | collective-permute-start | bytes 104456 | tf_op jit(solution)/shard_map/ppermute | solution.py:328
  14.0 2.0 %collective-permute-start.7 = (bf16[4,4352]{1,0:T(4,128)(2,1)S(1)}, bf16[4,4352]{1,0:T(4,128)(2,1)S(1)}, u32[]{:S(2)}, u32[]{:S(2)}) collective-permute-start(bf16[4,4352]{1,0:T(4,128)(2,1)S(1)} %get-tuple-element.14.own_ref), channel_id=1, source_target_pairs={{0,6},{1,3},{2,4},{3,1},{4,2},{5,7},{6,0},{7,5},{8,14},{9,11},{10,... | collective-permute-start | bytes 104456 | tf_op jit(solution)/shard_map/ppermute | solution.py:328
  16.0 0.5 %collective-permute-start.4 = (bf16[4,4352]{1,0:T(4,128)(2,1)S(1)}, bf16[4,4352]{1,0:T(4,128)(2,1)S(1)}, u32[]{:S(2)}, u32[]{:S(2)}) collective-permute-start(bf16[4,4352]{1,0:T(4,128)(2,1)S(1)} %get-tuple-element.13), channel_id=1, source_target_pairs={{0,10},{1,15},{2,8},{3,13},{4,14},{5,11},{6,12},{7,9},{8,2},{9,7},... | collective-permute-start | bytes 104456 | tf_op jit(solution)/shard_map/ppermute | solution.py:328
  16.4 2.4 %collective-permute-start.5 = (bf16[4,4352]{1,0:T(4,128)(2,1)S(1)}, bf16[4,4352]{1,0:T(4,128)(2,1)S(1)}, u32[]{:S(2)}, u32[]{:S(2)}) collective-permute-start(bf16[4,4352]{1,0:T(4,128)(2,1)S(1)} %get-tuple-element.13), channel_id=1, source_target_pairs={{0,8},{1,13},{2,10},{3,15},{4,12},{5,9},{6,14},{7,11},{8,0},{9,5},... | collective-permute-start | bytes 104456 | tf_op jit(solution)/shard_map/ppermute | solution.py:328
  18.9 0.0 collective-permute-done.6.three_ref
  18.9 0.0 collective-permute-done.7.four_ref
  18.9 3.6 %collective-permute-done.4.two_ref = bf16[4,4352]{1,0:T(4,128)(2,1)S(1)} collective-permute-done((bf16[4,4352]{1,0:T(4,128)(2,1)S(1)}, bf16[4,4352]{1,0:T(4,128)(2,1)S(1)}, u32[]{:S(2)}, u32[]{:S(2)}) %collective-permute-start.4) | collective-permute-done | bytes 34848 | tf_op jit(solution)/shard_map/ppermute | solution.py:328
  22.4 0.0 collective-permute-done.5.one_ref
  22.5 0.1 collective-permute-start.8
  22.5 1.2 %collective-permute-done.8.other_ref = f32[4,4352]{1,0:T(4,128)S(1)} collective-permute-done((f32[4,4352]{1,0:T(4,128)S(1)}, f32[4,4352]{1,0:T(4,128)S(1)}, u32[]{:S(2)}, u32[]{:S(2)}) %collective-permute-start.8) | collective-permute-done | bytes 69664 | tf_op jit(solution)/shard_map/ppermute | solution.py:328
  23.8 0.8 %shard_map.71 = (f32[4,4096]{1,0:T(4,128)}, f32[1,4]{1,0:T(1,128)}, f32[1,64]{1,0:T(1,128)}) custom-call(f32[4,4352]{1,0:T(4,128)S(1)} %shard_map.70.own_ref, f32[4,4352]{1,0:T(4,128)S(1)} %collective-permute-done.8.other_ref, f32[1,128]{1,0:T(1,128)S(1)} %get-tuple-element.15.total_ref), custom_call_target="tpu_custom_call" | custom-call | tf_op jit(solution)/shard_map/pallas_call | solution.py:337
  (1 shorter events, 0.0 us)
Async XLA Ops:
  0.6 5.8 %collective-permute-start.2 = (bf16[64,4096]{1,0:T(8,128)(2,1)}, bf16[64,4096]{1,0:T(8,128)(2,1)S(1)}, u32[]{:S(2)}, u32[]{:S(2)}) collective-permute-start(bf16[64,4096]{1,0:T(8,128)(2,1)} %own_hbm.1), channel_id=1, source_target_pairs={{0,1},{1,0},{2,3},{3,2},{4,5},{5,4},{6,7},{7,6},{8,9},{9,8},{10,11... | collective-permute-start | bytes 1572872 | tf_op jit(solution)/shard_map/ppermute | solution.py:328
  1.1 8.3 %collective-permute-start = (bf16[4,4096]{1,0:T(4,128)(2,1)}, bf16[4,4096]{1,0:T(4,128)(2,1)S(1)}, u32[]{:S(2)}, u32[]{:S(2)}) collective-permute-start(bf16[4,4096]{1,0:T(4,128)(2,1)} %own_ref.1), channel_id=1, source_target_pairs={{0,8},{1,13},{2,10},{3,15},{4,12},{5,9},{6,14},{7,11},{8,0},{9,5},... | collective-permute-start | bytes 98312 | tf_op jit(solution)/shard_map/ppermute | solution.py:328
  4.8 4.7 %collective-permute-start.1 = (bf16[4,4096]{1,0:T(4,128)(2,1)}, bf16[4,4096]{1,0:T(4,128)(2,1)S(1)}, u32[]{:S(2)}, u32[]{:S(2)}) collective-permute-start(bf16[4,4096]{1,0:T(4,128)(2,1)} %own_ref.1), channel_id=1, source_target_pairs={{0,4},{1,5},{2,6},{3,7},{4,0},{5,1},{6,2},{7,3},{8,12},{9,13},{10,... | collective-permute-start | bytes 98312 | tf_op jit(solution)/shard_map/ppermute | solution.py:328
  6.4 1.0 %copy-start = (bf16[64,4096]{1,0:T(8,128)(2,1)S(1)}, bf16[64,4096]{1,0:T(8,128)(2,1)}, u32[]{:S(2)}) copy-start(bf16[64,4096]{1,0:T(8,128)(2,1)} %own_hbm.1) | copy-start | bytes 1572868
  7.4 2.1 %copy-start.1 = (bf16[4,4096]{1,0:T(4,128)(2,1)S(1)}, bf16[4,4096]{1,0:T(4,128)(2,1)}, u32[]{:S(2)}) copy-start(bf16[4,4096]{1,0:T(4,128)(2,1)} %own_ref.1) | copy-start | bytes 98308
  7.4 2.1 %copy-start.2 = (s32[1,4]{1,0:T(1,128)S(1)}, s32[1,4]{1,0:T(1,128)}, u32[]{:S(2)}) copy-start(s32[1,4]{1,0:T(1,128)} %counts_ref.1) | copy-start | bytes 52
  7.4 2.1 %copy-start.3 = (s32[1,4]{1,0:T(1,128)S(1)}, s32[1,4]{1,0:T(1,128)}, u32[]{:S(2)}) copy-start(s32[1,4]{1,0:T(1,128)} %owners_ref.1) | copy-start | bytes 52
  10.7 1.2 %collective-permute-start.3 = (f32[8,128]{1,0:T(8,128)S(1)}, f32[8,128]{1,0:T(8,128)S(1)}, u32[]{:S(2)}, u32[]{:S(2)}) collective-permute-start(f32[8,128]{1,0:T(8,128)S(1)} %get-tuple-element.12.stats_ref), channel_id=1, source_target_pairs={{0,1},{1,0},{2,3},{3,2},{4,5},{5,4},{6,7},{7,6},{8,9},{9,8},{10,11... | collective-permute-start | bytes 12296 | tf_op jit(solution)/shard_map/ppermute | solution.py:328
  12.9 5.9 %collective-permute-start.6 = (bf16[4,4352]{1,0:T(4,128)(2,1)S(1)}, bf16[4,4352]{1,0:T(4,128)(2,1)S(1)}, u32[]{:S(2)}, u32[]{:S(2)}) collective-permute-start(bf16[4,4352]{1,0:T(4,128)(2,1)S(1)} %get-tuple-element.14.own_ref), channel_id=1, source_target_pairs={{0,4},{1,5},{2,6},{3,7},{4,0},{5,1},{6,2},{7,3},{8,12},{9,13},{10,... | collective-permute-start | bytes 104456 | tf_op jit(solution)/shard_map/ppermute | solution.py:328
  14.0 4.9 %collective-permute-start.7 = (bf16[4,4352]{1,0:T(4,128)(2,1)S(1)}, bf16[4,4352]{1,0:T(4,128)(2,1)S(1)}, u32[]{:S(2)}, u32[]{:S(2)}) collective-permute-start(bf16[4,4352]{1,0:T(4,128)(2,1)S(1)} %get-tuple-element.14.own_ref), channel_id=1, source_target_pairs={{0,6},{1,3},{2,4},{3,1},{4,2},{5,7},{6,0},{7,5},{8,14},{9,11},{10,... | collective-permute-start | bytes 104456 | tf_op jit(solution)/shard_map/ppermute | solution.py:328
  16.0 6.5 %collective-permute-start.4 = (bf16[4,4352]{1,0:T(4,128)(2,1)S(1)}, bf16[4,4352]{1,0:T(4,128)(2,1)S(1)}, u32[]{:S(2)}, u32[]{:S(2)}) collective-permute-start(bf16[4,4352]{1,0:T(4,128)(2,1)S(1)} %get-tuple-element.13), channel_id=1, source_target_pairs={{0,10},{1,15},{2,8},{3,13},{4,14},{5,11},{6,12},{7,9},{8,2},{9,7},... | collective-permute-start | bytes 104456 | tf_op jit(solution)/shard_map/ppermute | solution.py:328
  16.4 6.0 %collective-permute-start.5 = (bf16[4,4352]{1,0:T(4,128)(2,1)S(1)}, bf16[4,4352]{1,0:T(4,128)(2,1)S(1)}, u32[]{:S(2)}, u32[]{:S(2)}) collective-permute-start(bf16[4,4352]{1,0:T(4,128)(2,1)S(1)} %get-tuple-element.13), channel_id=1, source_target_pairs={{0,8},{1,13},{2,10},{3,15},{4,12},{5,9},{6,14},{7,11},{8,0},{9,5},... | collective-permute-start | bytes 104456 | tf_op jit(solution)/shard_map/ppermute | solution.py:328
  22.5 1.3 %collective-permute-start.8 = (f32[4,4352]{1,0:T(4,128)S(1)}, f32[4,4352]{1,0:T(4,128)S(1)}, u32[]{:S(2)}, u32[]{:S(2)}) collective-permute-start(f32[4,4352]{1,0:T(4,128)S(1)} %shard_map.70.own_ref), channel_id=1, source_target_pairs={{0,1},{1,0},{2,3},{3,2},{4,5},{5,4},{6,7},{7,6},{8,9},{9,8},{10,11... | collective-permute-start | bytes 208904 | tf_op jit(solution)/shard_map/ppermute | solution.py:328

commit v3 on v2

--- a/solution.py
+++ b/solution.py
@@ -34,9 +34,9 @@
             copies[block * LANES // width].wait()
         span = slice(block * LANES, (block + 1) * LANES)
         tile = jnp.concatenate([own_ref[:, span], other_ref[:, span]], axis=0)
-        tile = tile.astype(F32).T
-        wide_ref[span, :] = tile
-        out_ref[span, :LANES] = tile.astype(BF16)
+        tile = tile.T
+        wide_ref[span, :] = tile.astype(F32)
+        out_ref[span, :LANES] = tile
     for column in range(BOX):
         out_ref[column * BOX:(column + 1) * BOX, LANES:] = wide_ref[
             pl.ds(column, BOX, stride=BOX), :
@@ -52,17 +52,18 @@
 
 def slot_row(counts_ref, owners_ref, capacity):
     mic_count = counts_ref.shape[1]
+    counts = [counts_ref[:, m:m + 1] for m in range(mic_count)]
+    owners = [owners_ref[:, m:m + 1] for m in range(mic_count)]
     position = lax.broadcasted_iota(jnp.int32, (1, LANES), 1)
     slot = jnp.full((1, LANES), -1, jnp.int32)
-    start = jnp.int32(0)
+    start = jnp.zeros((1, 1), jnp.int32)
     for mic in range(mic_count):
-        owner = owners_ref[0, mic]
-        before = jnp.int32(0)
+        before = jnp.zeros((1, 1), jnp.int32)
         for earlier in range(mic):
-            before = before + jnp.where(owners_ref[0, earlier] == owner, counts_ref[0, earlier], 0)
-        stop = start + counts_ref[0, mic]
+            before = before + jnp.where(owners[earlier] == owners[mic], counts[earlier], 0)
+        stop = start + counts[mic]
         inside = (position >= start) & (position < stop)
-        slot = jnp.where(inside, position + (owner * capacity + before - start), slot)
+        slot = jnp.where(inside, position + (owners[mic] * capacity + before - start), slot)
         start = stop
     return slot
 
@@ -81,7 +82,7 @@
     per_dev, pixels = own_ref.shape
     half = 2 * per_dev
     block_of = spans(pixels)
-    second = jnp.where(lax.axis_index("rd") == 0, second_ref[...].astype(F32), own_ref[...].astype(F32))
+    second = jnp.where(lax.axis_index("rd") == 1, second_ref[...].astype(F32), own_ref[...].astype(F32))
     refs = jnp.concatenate([first_ref[...].astype(F32), second], axis=0)
     squares = jnp.sum(refs * refs, axis=1, keepdims=True)
     stacked = jnp.concatenate([refs[:, b] for b in block_of], axis=0)
@@ -102,7 +103,7 @@
     stats_ref[...] = jnp.concatenate([highest, summed, slot, jnp.zeros((5, LANES), F32)], axis=0)
 
 
-def weigh_kernel(scores_ref, stats_ref, other_stats_ref, images_ref, first_ref, second_ref, total_ref, sums_ref):
+def weigh_kernel(scores_ref, stats_ref, other_stats_ref, images_ref, first_ref, second_ref, total_ref, kept_ref, sums_ref):
     per_dev = first_ref.shape[0]
     pixels = images_ref.shape[0]
     rows = LANES // 2
@@ -158,11 +159,12 @@
     last = slice(pixels + LANES, pixels + 2 * LANES)
     first_ref[:, last] = jnp.zeros((per_dev, LANES), BF16)
     second_ref[:, last] = pieces[:per_dev].astype(BF16)
-
-
-def add_kernel(two_ref, one_ref, three_ref, four_ref, own_ref, out_ref):
+    kept_ref[...] = second_ref[...]
+
+
+def add_kernel(four_ref, two_ref, three_ref, one_ref, own_ref, out_ref):
     pixels = out_ref.shape[1] - LANES
-    middle = jnp.where(lax.axis_index("rd") == 0, three_ref[:, :pixels].astype(F32), own_ref[:, :pixels].astype(F32))
+    middle = jnp.where(lax.axis_index("rd") == 1, three_ref[:, :pixels].astype(F32), own_ref[:, :pixels].astype(F32))
     out_ref[:, :pixels] = (one_ref[:, :pixels].astype(F32) + two_ref[:, :pixels].astype(F32)) + (
         middle + four_ref[:, :pixels].astype(F32)
     )
@@ -194,7 +196,7 @@
     copies[-1].start()
     first = lax.axis_index("img") == 0
     arrived = jnp.where(
-        lax.axis_index("rd") == 0, rolled(other_ref[0:1, last], 2 * capacity), own_ref[0:1, last]
+        lax.axis_index("rd") == 1, rolled(other_ref[0:1, last], 2 * capacity), own_ref[0:1, last]
     )
     arrived = jnp.where(first, arrived[:, :capacity], arrived[:, capacity:2 * capacity])
     mine = jnp.where(first, total_ref[:, :capacity], total_ref[:, capacity:2 * capacity])
@@ -349,32 +351,33 @@
     capacity = read_rows // lax.axis_size("img")
     per_dev = references.shape[0]
     other_images = swapped_by(images, 1, ("rd",))
-    ref_far = swapped_by(references, lambda rd: 12 if rd else 8)
-    ref_near = swapped_by(references, 4)
+    ref_far = swapped_by(references, lambda rd: 8 if rd else 4)
+    ref_near = swapped_by(references, lambda rd: 12 if rd else 2)
     shape = jax.ShapeDtypeStruct
+    images = pltpu.with_memory_space_constraint(images, pltpu.HBM)
     turned = call(
         turn_kernel, shape((pixels, 2 * LANES), BF16), (images, other_images), (),
-        [pltpu.VMEM((read_rows, pixels), BF16), pltpu.VMEM((pixels, LANES), F32), pltpu.SemaphoreType.DMA((4,))],
+        [pltpu.VMEM((read_rows, pixels), BF16), pltpu.VMEM((pixels, LANES), F32), pltpu.SemaphoreType.DMA((2,))],
         in_hbm=(0,),
     )
     scores, stats = call(
         functools.partial(score_kernel, capacity),
         (shape((8 * per_dev, 2 * LANES), F32), shape((8, LANES), F32)),
-        (counts, owners, ref_far, ref_near, references, turned), (0, 1),
+        (counts, owners, ref_far, ref_near, references, turned), (),
         [pltpu.VMEM((8 * per_dev, pixels), BF16)],
     )
     other_stats = swapped_by(stats, 1, ("rd",))
     wide = pixels + 2 * LANES
-    far, near, totals = call(
+    far, near, totals, kept = call(
         weigh_kernel,
-        (shape((per_dev, wide), BF16), shape((per_dev, wide), BF16), shape((1, LANES), F32)),
+        (shape((per_dev, wide), BF16), shape((per_dev, wide), BF16), shape((1, LANES), F32), shape((per_dev, wide), BF16)),
         (scores, stats, other_stats, turned), (), [pltpu.VMEM((8 * per_dev, pixels), F32)],
     )
-    two = swapped_by(far, lambda rd: 14 if rd else 10)
-    one = swapped_by(far, lambda rd: 12 if rd else 8)
-    four = swapped_by(near, lambda rd: 2 if rd else 6)
-    three = swapped_by(near, 4)
-    summed = call(add_kernel, shape((per_dev, wide), F32), (two, one, three, four, near))
+    two = swapped_by(far, lambda rd: 10 if rd else 6)
+    one = swapped_by(far, lambda rd: 8 if rd else 4)
+    four = swapped_by(near, lambda rd: 14 if rd else 2)
+    three = swapped_by(near, lambda rd: 12 if rd else 2)
+    summed = call(add_kernel, shape((per_dev, wide), F32), (four, two, three, one, kept))
     other = swapped_by(summed, 1, ("rd",))
     outs = (shape((per_dev, pixels), F32), shape((1, per_dev), F32), shape((1, read_rows), F32))
     means, weights, loglik = call(

time: 24.8 us -> 22.6 us (0.911)
  waiting for transfers between devices: 5.99 us -> 3.66 us
  starting transfers between devices: 11.8 us -> 13 us
  local copies, waits for them, and re-layouts: 1.05 us -> 0.01 us
    ppermute x9, waiting for transfers between devices: 5.99 us -> 3.66 us  [swapped_by(): return lax.ppermute(array, axes, pairs)]
    ppermute x9, starting transfers between devices: 11.8 us -> 13 us  [swapped_by(): return lax.ppermute(array, axes, pairs)]
    unnamed x8 -> x6, local copies, waits for them, and re-layouts: 1.05 us -> 0.01 us
  transfers between devices with their start and end apart: 9 -> 9, of which waited for: 3 -> 4; matrix products, arithmetic and copies ran while one was open for 0% -> 0% of each run, Pallas kernels for 8% -> 12%
where the time goes in v3:
time: 22.6 us; the launch traced here: 22.5 us
  starting transfers between devices  13 us (58%)
  Pallas kernels  5.09 us (23%)
  waiting for transfers between devices  3.66 us (16%)
  between operations  0.72 us (3%)
    ppermute x9, starting transfers between devices, swapped_by(): return lax.ppermute(array, axes, pairs)  13 us
    pallas_call x5, Pallas kernels, call(): pl.pallas_call(kernel, out_shape=outs, in_specs=specs, out_specs=jax.tree...  5.09 us
    ppermute x9, waiting for transfers between devices, swapped_by(): return lax.ppermute(array, axes, pairs)  3.66 us
  transfers between devices with their start and end apart: 9, of which 4 were waited for; matrix products, arithmetic and copies ran while one was open for 0% of the time, Pallas kernels for 12%

profile of v3, /device:TPU:0, one launch (start us, length us, event | category | flops | bytes accessed | tf_op | source)
XLA Modules:
  0.0 22.5 jit_solution(15521980152125943388)
XLA Ops:
  0.6 0.0 copy-start
  0.6 0.0 copy-start.1
  0.7 0.0 copy-start.2
  0.7 0.5 %collective-permute-start.2 = (bf16[64,4096]{1,0:T(8,128)(2,1)}, bf16[64,4096]{1,0:T(8,128)(2,1)S(1)}, u32[]{:S(2)}, u32[]{:S(2)}) collective-permute-start(bf16[64,4096]{1,0:T(8,128)(2,1)} %own_hbm.1), channel_id=1, source_target_pairs={{0,1},{1,0},{2,3},{3,2},{4,5},{5,4},{6,7},{7,6},{8,9},{9,8},{10,11... | collective-permute-start | bytes 1572872 | tf_op jit(solution)/shard_map/ppermute | solution.py:330
  1.2 2.6 %collective-permute-start = (bf16[4,4096]{1,0:T(4,128)(2,1)}, bf16[4,4096]{1,0:T(4,128)(2,1)S(1)}, u32[]{:S(2)}, u32[]{:S(2)}) collective-permute-start(bf16[4,4096]{1,0:T(4,128)(2,1)} %own_ref.1), channel_id=1, source_target_pairs={{0,4},{1,9},{2,6},{3,11},{4,0},{5,13},{6,2},{7,15},{8,12},{9,1},{1... | collective-permute-start | bytes 98312 | tf_op jit(solution)/shard_map/ppermute | solution.py:330
  3.8 1.5 %collective-permute-start.1 = (bf16[4,4096]{1,0:T(4,128)(2,1)}, bf16[4,4096]{1,0:T(4,128)(2,1)S(1)}, u32[]{:S(2)}, u32[]{:S(2)}) collective-permute-start(bf16[4,4096]{1,0:T(4,128)(2,1)} %own_ref.1), channel_id=1, source_target_pairs={{0,2},{1,13},{2,0},{3,15},{4,6},{5,9},{6,4},{7,11},{8,10},{9,5},{1... | collective-permute-start | bytes 98312 | tf_op jit(solution)/shard_map/ppermute | solution.py:330
  5.3 0.0 collective-permute-done.2.other_ref
  5.3 2.6 %shard_map.67.images_ref = bf16[4096,256]{1,0:T(8,128)(2,1)S(1)} custom-call(bf16[64,4096]{1,0:T(8,128)(2,1)} %own_hbm.1, bf16[64,4096]{1,0:T(8,128)(2,1)S(1)} %collective-permute-done.2.other_ref), custom_call_target="tpu_custom_call" | custom-call | tf_op jit(solution)/shard_map/pallas_call | solution.py:339
  7.9 0.0 collective-permute-done.first_ref
  8.0 0.0 collective-permute-done.1.second_ref
  8.0 0.0 copy-done
  8.0 0.0 copy-done.1
  8.0 0.0 copy-done.2
  8.0 0.6 %shard_map.68 = (f32[32,256]{1,0:T(8,128)S(1)}, f32[8,128]{1,0:T(8,128)S(1)}) custom-call(s32[1,4]{1,0:T(1,128)S(1)} %copy-done.1, s32[1,4]{1,0:T(1,128)S(1)} %copy-done.2, bf16[4,4096]{1,0:T(4,128)(2,1)S(1)} %collective-permute-done.first_ref, bf16[4,4096]{1,0:T(4,128)(2,1)S(1)} %collective-permute-done.1.second_ref, bf16[4,4096]{1,0:T(4,128)(2,1)S(1)} %copy-done, ...), custom_call_target="tpu_custom_call" | custom-call | tf_op jit(solution)/shard_map/pallas_call | solution.py:339
  8.6 1.8 %collective-permute-start.3 = (f32[8,128]{1,0:T(8,128)S(1)}, f32[8,128]{1,0:T(8,128)S(1)}, u32[]{:S(2)}, u32[]{:S(2)}) collective-permute-start(f32[8,128]{1,0:T(8,128)S(1)} %get-tuple-element.13.stats_ref), channel_id=1, source_target_pairs={{0,1},{1,0},{2,3},{3,2},{4,5},{5,4},{6,7},{7,6},{8,9},{9,8},{10,11... | collective-permute-start | bytes 12296 | tf_op jit(solution)/shard_map/ppermute | solution.py:330
  10.5 0.8 %collective-permute-done.3.other_stats_ref = f32[8,128]{1,0:T(8,128)S(1)} collective-permute-done((f32[8,128]{1,0:T(8,128)S(1)}, f32[8,128]{1,0:T(8,128)S(1)}, u32[]{:S(2)}, u32[]{:S(2)}) %collective-permute-start.3) | collective-permute-done | bytes 4128 | tf_op jit(solution)/shard_map/ppermute | solution.py:330
  11.3 1.0 %shard_map.69 = (bf16[4,4352]{1,0:T(4,128)(2,1)S(1)}, bf16[4,4352]{1,0:T(4,128)(2,1)S(1)}, f32[1,128]{1,0:T(1,128)S(1)}, bf16[4,4352]{1,0:T(4,128)(2,1)S(1)}) custom-call(f32[32,256]{1,0:T(8,128)S(1)} %get-tuple-element.12.scores_ref, f32[8,128]{1,0:T(8,128)S(1)} %get-tuple-element.13.stats_ref, f32[8,128]{1,0:T(8,128)S(1)} %collective-permute-done.3.other_stats_ref, ...), custom_call_target="tpu_custom_call" | custom-call | tf_op jit(solution)/shard_map/pallas_call | solution.py:339
  12.3 1.6 %collective-permute-start.4 = (bf16[4,4352]{1,0:T(4,128)(2,1)S(1)}, bf16[4,4352]{1,0:T(4,128)(2,1)S(1)}, u32[]{:S(2)}, u32[]{:S(2)}) collective-permute-start(bf16[4,4352]{1,0:T(4,128)(2,1)S(1)} %get-tuple-element.14), channel_id=1, source_target_pairs={{0,2},{1,15},{2,0},{3,13},{4,6},{5,11},{6,4},{7,9},{8,10},{9,7},{1... | collective-permute-start | bytes 104456 | tf_op jit(solution)/shard_map/ppermute | solution.py:330
  13.9 0.0 collective-permute-start.5
  13.9 1.2 %collective-permute-start.6 = (bf16[4,4352]{1,0:T(4,128)(2,1)S(1)}, bf16[4,4352]{1,0:T(4,128)(2,1)S(1)}, u32[]{:S(2)}, u32[]{:S(2)}) collective-permute-start(bf16[4,4352]{1,0:T(4,128)(2,1)S(1)} %get-tuple-element.14), channel_id=1, source_target_pairs={{0,2},{1,13},{2,0},{3,15},{4,6},{5,9},{6,4},{7,11},{8,10},{9,5},{1... | collective-permute-start | bytes 104456 | tf_op jit(solution)/shard_map/ppermute | solution.py:330
  15.1 2.3 %collective-permute-start.7 = (bf16[4,4352]{1,0:T(4,128)(2,1)S(1)}, bf16[4,4352]{1,0:T(4,128)(2,1)S(1)}, u32[]{:S(2)}, u32[]{:S(2)}) collective-permute-start(bf16[4,4352]{1,0:T(4,128)(2,1)S(1)} %get-tuple-element.15), channel_id=1, source_target_pairs={{0,4},{1,9},{2,6},{3,11},{4,0},{5,13},{6,2},{7,15},{8,12},{9,1},{1... | collective-permute-start | bytes 104456 | tf_op jit(solution)/shard_map/ppermute | solution.py:330
  17.3 0.0 collective-permute-done.4.four_ref
  17.3 1.4 %collective-permute-done.5.two_ref = bf16[4,4352]{1,0:T(4,128)(2,1)S(1)} collective-permute-done((bf16[4,4352]{1,0:T(4,128)(2,1)S(1)}, bf16[4,4352]{1,0:T(4,128)(2,1)S(1)}, u32[]{:S(2)}, u32[]{:S(2)}) %collective-permute-start.5) | collective-permute-done | bytes 34848 | tf_op jit(solution)/shard_map/ppermute | solution.py:330
  18.7 0.0 collective-permute-done.6.three_ref
  18.7 0.5 %collective-permute-done.7.one_ref = bf16[4,4352]{1,0:T(4,128)(2,1)S(1)} collective-permute-done((bf16[4,4352]{1,0:T(4,128)(2,1)S(1)}, bf16[4,4352]{1,0:T(4,128)(2,1)S(1)}, u32[]{:S(2)}, u32[]{:S(2)}) %collective-permute-start.7) | collective-permute-done | bytes 34848 | tf_op jit(solution)/shard_map/ppermute | solution.py:330
  19.3 1.5 %collective-permute-start.8 = (f32[4,4352]{1,0:T(4,128)S(1)}, f32[4,4352]{1,0:T(4,128)S(1)}, u32[]{:S(2)}, u32[]{:S(2)}) collective-permute-start(f32[4,4352]{1,0:T(4,128)S(1)} %shard_map.70.own_ref), channel_id=1, source_target_pairs={{0,1},{1,0},{2,3},{3,2},{4,5},{5,4},{6,7},{7,6},{8,9},{9,8},{10,11... | collective-permute-start | bytes 208904 | tf_op jit(solution)/shard_map/ppermute | solution.py:330
  20.8 0.9 %collective-permute-done.8.other_ref = f32[4,4352]{1,0:T(4,128)S(1)} collective-permute-done((f32[4,4352]{1,0:T(4,128)S(1)}, f32[4,4352]{1,0:T(4,128)S(1)}, u32[]{:S(2)}, u32[]{:S(2)}) %collective-permute-start.8) | collective-permute-done | bytes 69664 | tf_op jit(solution)/shard_map/ppermute | solution.py:330
  21.7 0.8 %shard_map.71 = (f32[4,4096]{1,0:T(4,128)}, f32[1,4]{1,0:T(1,128)}, f32[1,64]{1,0:T(1,128)}) custom-call(f32[4,4352]{1,0:T(4,128)S(1)} %shard_map.70.own_ref, f32[4,4352]{1,0:T(4,128)S(1)} %collective-permute-done.8.other_ref, f32[1,128]{1,0:T(1,128)S(1)} %get-tuple-element.17.total_ref), custom_call_target="tpu_custom_call" | custom-call | tf_op jit(solution)/shard_map/pallas_call | solution.py:339
  (1 shorter events, 0.0 us)
Async XLA Ops:
  0.6 7.3 %copy-start = (bf16[4,4096]{1,0:T(4,128)(2,1)S(1)}, bf16[4,4096]{1,0:T(4,128)(2,1)}, u32[]{:S(2)}) copy-start(bf16[4,4096]{1,0:T(4,128)(2,1)} %own_ref.1) | copy-start | bytes 98308
  0.6 7.3 %copy-start.1 = (s32[1,4]{1,0:T(1,128)S(1)}, s32[1,4]{1,0:T(1,128)}, u32[]{:S(2)}) copy-start(s32[1,4]{1,0:T(1,128)} %counts_ref.1) | copy-start | bytes 52
  0.7 7.3 %copy-start.2 = (s32[1,4]{1,0:T(1,128)S(1)}, s32[1,4]{1,0:T(1,128)}, u32[]{:S(2)}) copy-start(s32[1,4]{1,0:T(1,128)} %owners_ref.1) | copy-start | bytes 52
  0.7 4.7 %collective-permute-start.2 = (bf16[64,4096]{1,0:T(8,128)(2,1)}, bf16[64,4096]{1,0:T(8,128)(2,1)S(1)}, u32[]{:S(2)}, u32[]{:S(2)}) collective-permute-start(bf16[64,4096]{1,0:T(8,128)(2,1)} %own_hbm.1), channel_id=1, source_target_pairs={{0,1},{1,0},{2,3},{3,2},{4,5},{5,4},{6,7},{7,6},{8,9},{9,8},{10,11... | collective-permute-start | bytes 1572872 | tf_op jit(solution)/shard_map/ppermute | solution.py:330
  1.2 6.8 %collective-permute-start = (bf16[4,4096]{1,0:T(4,128)(2,1)}, bf16[4,4096]{1,0:T(4,128)(2,1)S(1)}, u32[]{:S(2)}, u32[]{:S(2)}) collective-permute-start(bf16[4,4096]{1,0:T(4,128)(2,1)} %own_ref.1), channel_id=1, source_target_pairs={{0,4},{1,9},{2,6},{3,11},{4,0},{5,13},{6,2},{7,15},{8,12},{9,1},{1... | collective-permute-start | bytes 98312 | tf_op jit(solution)/shard_map/ppermute | solution.py:330
  3.8 4.1 %collective-permute-start.1 = (bf16[4,4096]{1,0:T(4,128)(2,1)}, bf16[4,4096]{1,0:T(4,128)(2,1)S(1)}, u32[]{:S(2)}, u32[]{:S(2)}) collective-permute-start(bf16[4,4096]{1,0:T(4,128)(2,1)} %own_ref.1), channel_id=1, source_target_pairs={{0,2},{1,13},{2,0},{3,15},{4,6},{5,9},{6,4},{7,11},{8,10},{9,5},{1... | collective-permute-start | bytes 98312 | tf_op jit(solution)/shard_map/ppermute | solution.py:330
  8.6 2.7 %collective-permute-start.3 = (f32[8,128]{1,0:T(8,128)S(1)}, f32[8,128]{1,0:T(8,128)S(1)}, u32[]{:S(2)}, u32[]{:S(2)}) collective-permute-start(f32[8,128]{1,0:T(8,128)S(1)} %get-tuple-element.13.stats_ref), channel_id=1, source_target_pairs={{0,1},{1,0},{2,3},{3,2},{4,5},{5,4},{6,7},{7,6},{8,9},{9,8},{10,11... | collective-permute-start | bytes 12296 | tf_op jit(solution)/shard_map/ppermute | solution.py:330
  12.3 5.0 %collective-permute-start.4 = (bf16[4,4352]{1,0:T(4,128)(2,1)S(1)}, bf16[4,4352]{1,0:T(4,128)(2,1)S(1)}, u32[]{:S(2)}, u32[]{:S(2)}) collective-permute-start(bf16[4,4352]{1,0:T(4,128)(2,1)S(1)} %get-tuple-element.14), channel_id=1, source_target_pairs={{0,2},{1,15},{2,0},{3,13},{4,6},{5,11},{6,4},{7,9},{8,10},{9,7},{1... | collective-permute-start | bytes 104456 | tf_op jit(solution)/shard_map/ppermute | solution.py:330
  13.9 4.9 %collective-permute-start.5 = (bf16[4,4352]{1,0:T(4,128)(2,1)S(1)}, bf16[4,4352]{1,0:T(4,128)(2,1)S(1)}, u32[]{:S(2)}, u32[]{:S(2)}) collective-permute-start(bf16[4,4352]{1,0:T(4,128)(2,1)S(1)} %get-tuple-element.15), channel_id=1, source_target_pairs={{0,6},{1,11},{2,4},{3,9},{4,2},{5,15},{6,0},{7,13},{8,14},{9,3},{1... | collective-permute-start | bytes 104456 | tf_op jit(solution)/shard_map/ppermute | solution.py:330
  13.9 4.9 %collective-permute-start.6 = (bf16[4,4352]{1,0:T(4,128)(2,1)S(1)}, bf16[4,4352]{1,0:T(4,128)(2,1)S(1)}, u32[]{:S(2)}, u32[]{:S(2)}) collective-permute-start(bf16[4,4352]{1,0:T(4,128)(2,1)S(1)} %get-tuple-element.14), channel_id=1, source_target_pairs={{0,2},{1,13},{2,0},{3,15},{4,6},{5,9},{6,4},{7,11},{8,10},{9,5},{1... | collective-permute-start | bytes 104456 | tf_op jit(solution)/shard_map/ppermute | solution.py:330
  15.1 4.2 %collective-permute-start.7 = (bf16[4,4352]{1,0:T(4,128)(2,1)S(1)}, bf16[4,4352]{1,0:T(4,128)(2,1)S(1)}, u32[]{:S(2)}, u32[]{:S(2)}) collective-permute-start(bf16[4,4352]{1,0:T(4,128)(2,1)S(1)} %get-tuple-element.15), channel_id=1, source_target_pairs={{0,4},{1,9},{2,6},{3,11},{4,0},{5,13},{6,2},{7,15},{8,12},{9,1},{1... | collective-permute-start | bytes 104456 | tf_op jit(solution)/shard_map/ppermute | solution.py:330
  19.3 2.4 %collective-permute-start.8 = (f32[4,4352]{1,0:T(4,128)S(1)}, f32[4,4352]{1,0:T(4,128)S(1)}, u32[]{:S(2)}, u32[]{:S(2)}) collective-permute-start(f32[4,4352]{1,0:T(4,128)S(1)} %shard_map.70.own_ref), channel_id=1, source_target_pairs={{0,1},{1,0},{2,3},{3,2},{4,5},{5,4},{6,7},{7,6},{8,9},{9,8},{10,11... | collective-permute-start | bytes 208904 | tf_op jit(solution)/shard_map/ppermute | solution.py:330

commit v4 on v3

--- a/solution.py
+++ b/solution.py
@@ -20,34 +20,8 @@
     return jnp.concatenate([tile[:, by:], tile[:, :by]], axis=1)
 
 
-def turn_kernel(own_hbm, other_ref, out_ref, own_ref, wide_ref, arrived):
-    pixels = other_ref.shape[1]
-    pieces = arrived.shape[0]
-    width = pixels // pieces
-    copies = []
-    for piece in range(pieces):
-        span = pl.ds(piece * width, width)
-        copies.append(pltpu.make_async_copy(own_hbm.at[:, span], own_ref.at[:, span], arrived.at[piece]))
-        copies[-1].start()
-    for block in range(pixels // LANES):
-        if block * LANES % width == 0:
-            copies[block * LANES // width].wait()
-        span = slice(block * LANES, (block + 1) * LANES)
-        tile = jnp.concatenate([own_ref[:, span], other_ref[:, span]], axis=0)
-        tile = tile.T
-        wide_ref[span, :] = tile.astype(F32)
-        out_ref[span, :LANES] = tile
-    for column in range(BOX):
-        out_ref[column * BOX:(column + 1) * BOX, LANES:] = wide_ref[
-            pl.ds(column, BOX, stride=BOX), :
-        ].astype(BF16)
-
-
-def three_parts(value):
-    high = value.astype(BF16).astype(F32)
-    rest = value - high
-    middle = rest.astype(BF16).astype(F32)
-    return high, middle, (rest - middle).astype(BF16).astype(F32)
+def spans(pixels):
+    return [slice(b * LANES, (b + 1) * LANES) for b in range(pixels // LANES)]
 
 
 def slot_row(counts_ref, owners_ref, capacity):
@@ -68,22 +42,63 @@
     return slot
 
 
+def turn_kernel(capacity, own_hbm, counts_hbm, owners_hbm, classes_hbm, other_ref,
+                out_ref, flat_ref, slots_ref, classes_ref, own_ref, counts_ref, owners_ref, arrived):
+    pixels = other_ref.shape[1]
+    pieces = arrived.shape[0] - 3
+    width = pixels // pieces
+    copies = []
+    for piece in range(pieces):
+        span = pl.ds(piece * width, width)
+        copies.append(pltpu.make_async_copy(own_hbm.at[:, span], own_ref.at[:, span], arrived.at[piece]))
+        copies[-1].start()
+    small = [
+        pltpu.make_async_copy(source, target, arrived.at[pieces + i])
+        for i, (source, target) in enumerate(
+            ((counts_hbm, counts_ref), (owners_hbm, owners_ref), (classes_hbm, classes_ref))
+        )
+    ]
+    for copy in small:
+        copy.start()
+    for block, span in enumerate(spans(pixels)):
+        if block * LANES % width == 0:
+            copies[block * LANES // width].wait()
+        tile = jnp.concatenate([own_ref[:, span], other_ref[:, span]], axis=0)
+        flat_ref[:LANES, span] = tile
+        out_ref[span, :LANES] = tile.T
+    square = out_ref[:, :LANES].reshape(BOX, BOX, LANES)
+    out_ref[:, LANES:] = jnp.swapaxes(square, 0, 1).reshape(pixels, LANES)
+    for span in spans(pixels):
+        flat_ref[LANES:, span] = out_ref[span, LANES:].T
+    for copy in small:
+        copy.wait()
+    slot = slot_row(counts_ref, owners_ref, capacity).astype(F32)
+    slots_ref[...] = jnp.broadcast_to(slot, slots_ref.shape)
+
+
+def three_parts(value):
+    high = value.astype(BF16).astype(F32)
+    rest = value - high
+    middle = rest.astype(BF16).astype(F32)
+    return high, middle, (rest - middle).astype(BF16).astype(F32)
+
+
 def mirror_of_rows():
     row = lax.broadcasted_iota(jnp.int32, (LANES, LANES), 0)
     column = lax.broadcasted_iota(jnp.int32, (LANES, LANES), 1)
     return (column == (row // BOX) * BOX + (BOX - 1 - row % BOX)).astype(BF16)
 
 
-def spans(pixels):
-    return [slice(b * LANES, (b + 1) * LANES) for b in range(pixels // LANES)]
-
-
-def score_kernel(capacity, counts_ref, owners_ref, first_ref, second_ref, own_ref, images_ref, scores_ref, stats_ref, flipped_ref):
+def score_kernel(slots_ref, two_ref, one_ref, own_ref, images_ref, scores_ref, sent_ref,
+                 flipped_ref):
     per_dev, pixels = own_ref.shape
     half = 2 * per_dev
     block_of = spans(pixels)
-    second = jnp.where(lax.axis_index("rd") == 1, second_ref[...].astype(F32), own_ref[...].astype(F32))
-    refs = jnp.concatenate([first_ref[...].astype(F32), second], axis=0)
+    lead = lax.axis_index("rd") == 0
+    two = two_ref[...].astype(F32)
+    refs = jnp.concatenate(
+        [jnp.where(lead, one_ref[...].astype(F32), two), jnp.where(lead, two, own_ref[...].astype(F32))], axis=0
+    )
     squares = jnp.sum(refs * refs, axis=1, keepdims=True)
     stacked = jnp.concatenate([refs[:, b] for b in block_of], axis=0)
     mirrored = jnp.dot(stacked.astype(BF16), mirror_of_rows(), preferred_element_type=F32)
@@ -95,35 +110,43 @@
     inner = jnp.dot(flipped_ref[...], images_ref[...], preferred_element_type=F32)
     scores = inner - 0.5 * jnp.concatenate([squares] * 4, axis=0)
     scores_ref[...] = scores
+    for f in range(4):
+        sent_ref[f * per_dev:(f + 1) * per_dev] = scores[f * half + per_dev:(f + 1) * half]
     highest = jnp.max(scores, axis=0, keepdims=True)
     highest = jnp.maximum(highest[:, :LANES], highest[:, LANES:])
     summed = jnp.sum(jnp.exp(scores - jnp.concatenate([highest, highest], axis=1)), axis=0, keepdims=True)
     summed = summed[:, :LANES] + summed[:, LANES:]
-    slot = slot_row(counts_ref, owners_ref, capacity).astype(F32)
-    stats_ref[...] = jnp.concatenate([highest, summed, slot, jnp.zeros((5, LANES), F32)], axis=0)
-
-
-def weigh_kernel(scores_ref, stats_ref, other_stats_ref, images_ref, first_ref, second_ref, total_ref, kept_ref, sums_ref):
+    stats = jnp.concatenate([highest, summed, slots_ref[2:]], axis=0)
+    sent_ref[4 * per_dev:] = jnp.concatenate([stats, stats], axis=1)
+
+
+def weigh_kernel(scores_ref, sent_ref, arrived_ref, images_ref, first_ref, second_ref, total_ref, kept_ref, sums_ref):
     per_dev = first_ref.shape[0]
-    pixels = images_ref.shape[0]
+    pixels = images_ref.shape[1]
     rows = LANES // 2
     half = 2 * per_dev
     block_of = spans(pixels)
-    scores = scores_ref[...]
-    other = rolled(other_stats_ref[...], BOX)
-    highest = jnp.maximum(stats_ref[0:1], other[0:1])
-    summed = stats_ref[1:2] * jnp.exp(stats_ref[0:1] - highest) + other[1:2] * jnp.exp(other[0:1] - highest)
+    top = 4 * per_dev
+    stats = sent_ref[top:, :LANES]
+    other = rolled(arrived_ref[top:, :LANES], BOX)
+    arrived = jnp.concatenate(
+        [rolled(arrived_ref[:top, :LANES], BOX), rolled(arrived_ref[:top, LANES:], BOX)], axis=1
+    )
+    scores = []
+    for f in range(4):
+        scores += [scores_ref[f * half:f * half + per_dev], arrived[f * per_dev:(f + 1) * per_dev]]
+    scores = jnp.concatenate(scores, axis=0)
+    highest = jnp.maximum(stats[0:1], other[0:1])
+    summed = stats[1:2] * jnp.exp(stats[0:1] - highest) + other[1:2] * jnp.exp(other[0:1] - highest)
     total = jnp.log(summed) + highest
 
     lane = lax.broadcasted_iota(jnp.int32, (1, LANES), 1)
-    slot = jnp.where(lane < rows, stats_ref[2:3], other[2:3]).astype(jnp.int32)
+    slot = jnp.where(lane < rows, stats[2:3], other[2:3]).astype(jnp.int32)
     live = slot >= 0
     slot = jnp.where(live & (lane >= rows), slot + rows, slot)
     live = jnp.concatenate([live, live], axis=1)
     weights = jnp.where(live, jnp.exp(scores - jnp.concatenate([total, total], axis=1)), 0.0).astype(BF16)
-    sums_ref[...] = lax.dot_general(
-        weights, images_ref[...], (((1,), (1,)), ((), ())), preferred_element_type=F32
-    )
+    sums_ref[...] = jnp.dot(weights, images_ref[...], preferred_element_type=F32)
     straight, swapped = [], []
     for b in range(len(block_of)):
         back = block_of[-1 - b]
@@ -162,7 +185,7 @@
     kept_ref[...] = second_ref[...]
 
 
-def add_kernel(four_ref, two_ref, three_ref, one_ref, own_ref, out_ref):
+def add_kernel(two_ref, four_ref, one_ref, three_ref, own_ref, out_ref):
     pixels = out_ref.shape[1] - LANES
     middle = jnp.where(lax.axis_index("rd") == 1, three_ref[:, :pixels].astype(F32), own_ref[:, :pixels].astype(F32))
     out_ref[:, :pixels] = (one_ref[:, :pixels].astype(F32) + two_ref[:, :pixels].astype(F32)) + (
@@ -342,7 +365,7 @@
         in_specs=specs,
         out_specs=jax.tree.map(lambda _: pl.BlockSpec(memory_space=out_space), outs),
         scratch_shapes=list(scratch),
-        compiler_params=pltpu.CompilerParams(vmem_limit_bytes=32 * 1024 * 1024),
+        compiler_params=pltpu.CompilerParams(vmem_limit_bytes=16 * 1024 * 1024),
     )(*args)
 
 
@@ -351,33 +374,37 @@
     capacity = read_rows // lax.axis_size("img")
     per_dev = references.shape[0]
     other_images = swapped_by(images, 1, ("rd",))
-    ref_far = swapped_by(references, lambda rd: 8 if rd else 4)
-    ref_near = swapped_by(references, lambda rd: 12 if rd else 2)
+    ref_one = swapped_by(references, 4)
+    ref_two = swapped_by(references, lambda rd: 12 if rd else 8)
     shape = jax.ShapeDtypeStruct
-    images = pltpu.with_memory_space_constraint(images, pltpu.HBM)
-    turned = call(
-        turn_kernel, shape((pixels, 2 * LANES), BF16), (images, other_images), (),
-        [pltpu.VMEM((read_rows, pixels), BF16), pltpu.VMEM((pixels, LANES), F32), pltpu.SemaphoreType.DMA((2,))],
-        in_hbm=(0,),
-    )
-    scores, stats = call(
-        functools.partial(score_kernel, capacity),
-        (shape((8 * per_dev, 2 * LANES), F32), shape((8, LANES), F32)),
-        (counts, owners, ref_far, ref_near, references, turned), (),
+    in_hbm = [pltpu.with_memory_space_constraint(x, pltpu.HBM) for x in (images, counts, owners, references)]
+    turned, flat, slots, classes = call(
+        functools.partial(turn_kernel, capacity),
+        (shape((pixels, 2 * LANES), BF16), shape((2 * LANES, pixels), BF16), shape((8, LANES), F32),
+         shape(references.shape, BF16)),
+        (*in_hbm, other_images), (),
+        [pltpu.VMEM((read_rows, pixels), BF16), pltpu.VMEM(counts.shape, jnp.int32),
+         pltpu.VMEM(owners.shape, jnp.int32), pltpu.SemaphoreType.DMA((5,))],
+        in_hbm=(0, 1, 2, 3),
+    )
+    scores, sent = call(
+        score_kernel,
+        (shape((8 * per_dev, 2 * LANES), F32), shape((4 * per_dev + 8, 2 * LANES), F32)),
+        (slots, ref_two, ref_one, classes, turned), (),
         [pltpu.VMEM((8 * per_dev, pixels), BF16)],
     )
-    other_stats = swapped_by(stats, 1, ("rd",))
+    arrived = swapped_by(sent, 1, ("rd",))
     wide = pixels + 2 * LANES
     far, near, totals, kept = call(
         weigh_kernel,
         (shape((per_dev, wide), BF16), shape((per_dev, wide), BF16), shape((1, LANES), F32), shape((per_dev, wide), BF16)),
-        (scores, stats, other_stats, turned), (), [pltpu.VMEM((8 * per_dev, pixels), F32)],
-    )
-    two = swapped_by(far, lambda rd: 10 if rd else 6)
-    one = swapped_by(far, lambda rd: 8 if rd else 4)
-    four = swapped_by(near, lambda rd: 14 if rd else 2)
-    three = swapped_by(near, lambda rd: 12 if rd else 2)
-    summed = call(add_kernel, shape((per_dev, wide), F32), (four, two, three, one, kept))
+        (scores, sent, arrived, flat), (), [pltpu.VMEM((8 * per_dev, pixels), F32)],
+    )
+    two = swapped_by(far, lambda rd: 14 if rd else 6)
+    one = swapped_by(far, lambda rd: 12 if rd else 4)
+    four = swapped_by(near, lambda rd: 10 if rd else 2)
+    three = swapped_by(near, lambda rd: 8 if rd else 2)
+    summed = call(add_kernel, shape((per_dev, wide), F32), (two, four, one, three, kept))
     other = swapped_by(summed, 1, ("rd",))
     outs = (shape((per_dev, pixels), F32), shape((1, per_dev), F32), shape((1, read_rows), F32))
     means, weights, loglik = call(

time: 22.6 us -> 22.1 us (0.978)
  waiting for transfers between devices: 3.66 us -> 4.89 us
  starting transfers between devices: 13 us -> 12 us
  Pallas kernels: 5.09 us -> 4.49 us
    ppermute x9, waiting for transfers between devices: 3.66 us -> 4.89 us  [swapped_by(): return lax.ppermute(array, axes, pairs)]
    ppermute x9, starting transfers between devices: 13 us -> 12 us  [swapped_by(): return lax.ppermute(array, axes, pairs)]
    pallas_call x5, Pallas kernels: 5.09 us -> 4.49 us  [call(): pl.pallas_call(kernel, out_shape=outs, in_specs=specs, out_specs=jax.tree...]
  transfers between devices with their start and end apart: 9 -> 9, of which waited for: 4 -> 6; matrix products, arithmetic and copies ran while one was open for 0% -> 0% of each run, Pallas kernels for 12% -> 10%
where the time goes in v4:
time: 22.1 us; the launch traced here: 22 us
  starting transfers between devices  12 us (54%)
  waiting for transfers between devices  4.89 us (22%)
  Pallas kernels  4.49 us (20%)
  between operations  0.67 us (3%)
    ppermute x9, starting transfers between devices, swapped_by(): return lax.ppermute(array, axes, pairs)  12 us
    ppermute x9, waiting for transfers between devices, swapped_by(): return lax.ppermute(array, axes, pairs)  4.89 us
    pallas_call x5, Pallas kernels, call(): pl.pallas_call(kernel, out_shape=outs, in_specs=specs, out_specs=jax.tree...  4.49 us
  transfers between devices with their start and end apart: 9, of which 6 were waited for; matrix products, arithmetic and copies ran while one was open for 0% of the time, Pallas kernels for 10%

profile of v4, /device:TPU:0, one launch (start us, length us, event | category | flops | bytes accessed | tf_op | source)
XLA Modules:
  0.0 22.0 jit_solution(13567875627192404531)
XLA Ops:
  0.6 0.5 %collective-permute-start = (bf16[64,4096]{1,0:T(8,128)(2,1)}, bf16[64,4096]{1,0:T(8,128)(2,1)S(1)}, u32[]{:S(2)}, u32[]{:S(2)}) collective-permute-start(bf16[64,4096]{1,0:T(8,128)(2,1)} %own_hbm.1), channel_id=1, source_target_pairs={{0,1},{1,0},{2,3},{3,2},{4,5},{5,4},{6,7},{7,6},{8,9},{9,8},{10,11... | collective-permute-start | bytes 1572872 | tf_op jit(solution)/shard_map/ppermute | solution.py:353
  1.1 3.7 %collective-permute-start.1 = (bf16[4,4096]{1,0:T(4,128)(2,1)}, bf16[4,4096]{1,0:T(4,128)(2,1)S(1)}, u32[]{:S(2)}, u32[]{:S(2)}) collective-permute-start(bf16[4,4096]{1,0:T(4,128)(2,1)} %classes_hbm.1), channel_id=1, source_target_pairs={{0,8},{1,13},{2,10},{3,15},{4,12},{5,9},{6,14},{7,11},{8,0},{9,5},... | collective-permute-start | bytes 98312 | tf_op jit(solution)/shard_map/ppermute | solution.py:353
  4.8 1.6 %collective-permute-start.2 = (bf16[4,4096]{1,0:T(4,128)(2,1)}, bf16[4,4096]{1,0:T(4,128)(2,1)S(1)}, u32[]{:S(2)}, u32[]{:S(2)}) collective-permute-start(bf16[4,4096]{1,0:T(4,128)(2,1)} %classes_hbm.1), channel_id=1, source_target_pairs={{0,4},{1,5},{2,6},{3,7},{4,0},{5,1},{6,2},{7,3},{8,12},{9,13},{10,... | collective-permute-start | bytes 98312 | tf_op jit(solution)/shard_map/ppermute | solution.py:353
  6.4 0.0 collective-permute-done.other_ref
  6.4 2.2 %shard_map.67 = (bf16[4096,256]{1,0:T(8,128)(2,1)S(1)}, bf16[256,4096]{1,0:T(8,128)(2,1)S(1)}, f32[8,128]{1,0:T(8,128)S(1)}, bf16[4,4096]{1,0:T(4,128)(2,1)S(1)}) custom-call(bf16[64,4096]{1,0:T(8,128)(2,1)} %own_hbm.1, s32[1,4]{1,0:T(1,128)} %counts_hbm.1, s32[1,4]{1,0:T(1,128)} %owners_hbm.1, bf16[4,4096]{1,0:T(4,128)(2,1)} %classes_hbm.1, ...), custom_call_target="tpu_custom_call" | custom-call | tf_op jit(solution)/shard_map/pallas_call | solution.py:362
  8.6 0.0 collective-permute-done.1.two_ref
  8.6 0.4 %collective-permute-done.2.one_ref = bf16[4,4096]{1,0:T(4,128)(2,1)S(1)} collective-permute-done((bf16[4,4096]{1,0:T(4,128)(2,1)}, bf16[4,4096]{1,0:T(4,128)(2,1)S(1)}, u32[]{:S(2)}, u32[]{:S(2)}) %collective-permute-start.2) | collective-permute-done | bytes 32800 | tf_op jit(solution)/shard_map/ppermute | solution.py:353
  9.1 0.6 %shard_map.68 = (f32[32,256]{1,0:T(8,128)S(1)}, f32[24,256]{1,0:T(8,128)S(1)}) custom-call(f32[8,128]{1,0:T(8,128)S(1)} %get-tuple-element.16.slots_ref, bf16[4,4096]{1,0:T(4,128)(2,1)S(1)} %collective-permute-done.1.two_ref, bf16[4,4096]{1,0:T(4,128)(2,1)S(1)} %collective-permute-done.2.one_ref, bf16[4,4096]{1,0:T(4,128)(2,1)S(1)} %get-tuple-element.17.own_ref, ...), custom_call_target="tpu_custom_call" | custom-call | tf_op jit(solution)/shard_map/pallas_call | solution.py:362
  9.7 0.2 collective-permute-start.3
  9.9 1.1 %collective-permute-done.3.arrived_ref = f32[24,256]{1,0:T(8,128)S(1)} collective-permute-done((f32[24,256]{1,0:T(8,128)S(1)}, f32[24,256]{1,0:T(8,128)S(1)}, u32[]{:S(2)}, u32[]{:S(2)}) %collective-permute-start.3) | collective-permute-done | bytes 24608 | tf_op jit(solution)/shard_map/ppermute | solution.py:353
  11.0 0.8 %shard_map.69 = (bf16[4,4352]{1,0:T(4,128)(2,1)S(1)}, bf16[4,4352]{1,0:T(4,128)(2,1)S(1)}, f32[1,128]{1,0:T(1,128)S(1)}, bf16[4,4352]{1,0:T(4,128)(2,1)S(1)}) custom-call(f32[32,256]{1,0:T(8,128)S(1)} %get-tuple-element.19.scores_ref, f32[24,256]{1,0:T(8,128)S(1)} %get-tuple-element.20.sent_ref, f32[24,256]{1,0:T(8,128)S(1)} %collective-permute-done.3.arrived_ref, ...), custom_call_target="tpu_custom_call" | custom-call | tf_op jit(solution)/shard_map/pallas_call | solution.py:362
  11.8 2.4 %collective-permute-start.4 = (bf16[4,4352]{1,0:T(4,128)(2,1)S(1)}, bf16[4,4352]{1,0:T(4,128)(2,1)S(1)}, u32[]{:S(2)}, u32[]{:S(2)}) collective-permute-start(bf16[4,4352]{1,0:T(4,128)(2,1)S(1)} %get-tuple-element.22), channel_id=1, source_target_pairs={{0,6},{1,15},{2,4},{3,13},{4,2},{5,11},{6,0},{7,9},{8,14},{9,7},{1... | collective-permute-start | bytes 104456 | tf_op jit(solution)/shard_map/ppermute | solution.py:353
  14.2 0.5 %collective-permute-start.5 = (bf16[4,4352]{1,0:T(4,128)(2,1)S(1)}, bf16[4,4352]{1,0:T(4,128)(2,1)S(1)}, u32[]{:S(2)}, u32[]{:S(2)}) collective-permute-start(bf16[4,4352]{1,0:T(4,128)(2,1)S(1)} %get-tuple-element.23), channel_id=1, source_target_pairs={{0,2},{1,11},{2,0},{3,9},{4,6},{5,15},{6,4},{7,13},{8,10},{9,3},{1... | collective-permute-start | bytes 104456 | tf_op jit(solution)/shard_map/ppermute | solution.py:353
  14.7 0.6 %collective-permute-start.6 = (bf16[4,4352]{1,0:T(4,128)(2,1)S(1)}, bf16[4,4352]{1,0:T(4,128)(2,1)S(1)}, u32[]{:S(2)}, u32[]{:S(2)}) collective-permute-start(bf16[4,4352]{1,0:T(4,128)(2,1)S(1)} %get-tuple-element.22), channel_id=1, source_target_pairs={{0,4},{1,13},{2,6},{3,15},{4,0},{5,9},{6,2},{7,11},{8,12},{9,5},{1... | collective-permute-start | bytes 104456 | tf_op jit(solution)/shard_map/ppermute | solution.py:353
  15.3 1.5 %collective-permute-start.7 = (bf16[4,4352]{1,0:T(4,128)(2,1)S(1)}, bf16[4,4352]{1,0:T(4,128)(2,1)S(1)}, u32[]{:S(2)}, u32[]{:S(2)}) collective-permute-start(bf16[4,4352]{1,0:T(4,128)(2,1)S(1)} %get-tuple-element.23), channel_id=1, source_target_pairs={{0,2},{1,9},{2,0},{3,11},{4,6},{5,13},{6,4},{7,15},{8,10},{9,1},{1... | collective-permute-start | bytes 104456 | tf_op jit(solution)/shard_map/ppermute | solution.py:353
  16.8 0.0 collective-permute-done.4.two_ref
  16.8 1.3 %collective-permute-done.5.four_ref = bf16[4,4352]{1,0:T(4,128)(2,1)S(1)} collective-permute-done((bf16[4,4352]{1,0:T(4,128)(2,1)S(1)}, bf16[4,4352]{1,0:T(4,128)(2,1)S(1)}, u32[]{:S(2)}, u32[]{:S(2)}) %collective-permute-start.5) | collective-permute-done | bytes 34848 | tf_op jit(solution)/shard_map/ppermute | solution.py:353
  18.1 0.9 %collective-permute-done.6.one_ref = bf16[4,4352]{1,0:T(4,128)(2,1)S(1)} collective-permute-done((bf16[4,4352]{1,0:T(4,128)(2,1)S(1)}, bf16[4,4352]{1,0:T(4,128)(2,1)S(1)}, u32[]{:S(2)}, u32[]{:S(2)}) %collective-permute-start.6) | collective-permute-done | bytes 34848 | tf_op jit(solution)/shard_map/ppermute | solution.py:353
  19.0 0.2 %collective-permute-done.7.three_ref = bf16[4,4352]{1,0:T(4,128)(2,1)S(1)} collective-permute-done((bf16[4,4352]{1,0:T(4,128)(2,1)S(1)}, bf16[4,4352]{1,0:T(4,128)(2,1)S(1)}, u32[]{:S(2)}, u32[]{:S(2)}) %collective-permute-start.7) | collective-permute-done | bytes 34848 | tf_op jit(solution)/shard_map/ppermute | solution.py:353
  19.3 1.0 %collective-permute-start.8 = (f32[4,4352]{1,0:T(4,128)S(1)}, f32[4,4352]{1,0:T(4,128)S(1)}, u32[]{:S(2)}, u32[]{:S(2)}) collective-permute-start(f32[4,4352]{1,0:T(4,128)S(1)} %shard_map.70.own_ref), channel_id=1, source_target_pairs={{0,1},{1,0},{2,3},{3,2},{4,5},{5,4},{6,7},{7,6},{8,9},{9,8},{10,11... | collective-permute-start | bytes 208904 | tf_op jit(solution)/shard_map/ppermute | solution.py:353
  20.3 0.9 %collective-permute-done.8.other_ref = f32[4,4352]{1,0:T(4,128)S(1)} collective-permute-done((f32[4,4352]{1,0:T(4,128)S(1)}, f32[4,4352]{1,0:T(4,128)S(1)}, u32[]{:S(2)}, u32[]{:S(2)}) %collective-permute-start.8) | collective-permute-done | bytes 69664 | tf_op jit(solution)/shard_map/ppermute | solution.py:353
  21.2 0.8 %shard_map.71 = (f32[4,4096]{1,0:T(4,128)}, f32[1,4]{1,0:T(1,128)}, f32[1,64]{1,0:T(1,128)}) custom-call(f32[4,4352]{1,0:T(4,128)S(1)} %shard_map.70.own_ref, f32[4,4352]{1,0:T(4,128)S(1)} %collective-permute-done.8.other_ref, f32[1,128]{1,0:T(1,128)S(1)} %get-tuple-element.25.total_ref), custom_call_target="tpu_custom_call" | custom-call | tf_op jit(solution)/shard_map/pallas_call | solution.py:362
  (1 shorter events, 0.0 us)
Async XLA Ops:
  0.6 5.8 %collective-permute-start = (bf16[64,4096]{1,0:T(8,128)(2,1)}, bf16[64,4096]{1,0:T(8,128)(2,1)S(1)}, u32[]{:S(2)}, u32[]{:S(2)}) collective-permute-start(bf16[64,4096]{1,0:T(8,128)(2,1)} %own_hbm.1), channel_id=1, source_target_pairs={{0,1},{1,0},{2,3},{3,2},{4,5},{5,4},{6,7},{7,6},{8,9},{9,8},{10,11... | collective-permute-start | bytes 1572872 | tf_op jit(solution)/shard_map/ppermute | solution.py:353
  1.1 7.5 %collective-permute-start.1 = (bf16[4,4096]{1,0:T(4,128)(2,1)}, bf16[4,4096]{1,0:T(4,128)(2,1)S(1)}, u32[]{:S(2)}, u32[]{:S(2)}) collective-permute-start(bf16[4,4096]{1,0:T(4,128)(2,1)} %classes_hbm.1), channel_id=1, source_target_pairs={{0,8},{1,13},{2,10},{3,15},{4,12},{5,9},{6,14},{7,11},{8,0},{9,5},... | collective-permute-start | bytes 98312 | tf_op jit(solution)/shard_map/ppermute | solution.py:353
  4.8 4.3 %collective-permute-start.2 = (bf16[4,4096]{1,0:T(4,128)(2,1)}, bf16[4,4096]{1,0:T(4,128)(2,1)S(1)}, u32[]{:S(2)}, u32[]{:S(2)}) collective-permute-start(bf16[4,4096]{1,0:T(4,128)(2,1)} %classes_hbm.1), channel_id=1, source_target_pairs={{0,4},{1,5},{2,6},{3,7},{4,0},{5,1},{6,2},{7,3},{8,12},{9,13},{10,... | collective-permute-start | bytes 98312 | tf_op jit(solution)/shard_map/ppermute | solution.py:353
  9.7 1.3 %collective-permute-start.3 = (f32[24,256]{1,0:T(8,128)S(1)}, f32[24,256]{1,0:T(8,128)S(1)}, u32[]{:S(2)}, u32[]{:S(2)}) collective-permute-start(f32[24,256]{1,0:T(8,128)S(1)} %get-tuple-element.20.sent_ref), channel_id=1, source_target_pairs={{0,1},{1,0},{2,3},{3,2},{4,5},{5,4},{6,7},{7,6},{8,9},{9,8},{10,11... | collective-permute-start | bytes 73736 | tf_op jit(solution)/shard_map/ppermute | solution.py:353
  11.8 5.0 %collective-permute-start.4 = (bf16[4,4352]{1,0:T(4,128)(2,1)S(1)}, bf16[4,4352]{1,0:T(4,128)(2,1)S(1)}, u32[]{:S(2)}, u32[]{:S(2)}) collective-permute-start(bf16[4,4352]{1,0:T(4,128)(2,1)S(1)} %get-tuple-element.22), channel_id=1, source_target_pairs={{0,6},{1,15},{2,4},{3,13},{4,2},{5,11},{6,0},{7,9},{8,14},{9,7},{1... | collective-permute-start | bytes 104456 | tf_op jit(solution)/shard_map/ppermute | solution.py:353
  14.2 3.9 %collective-permute-start.5 = (bf16[4,4352]{1,0:T(4,128)(2,1)S(1)}, bf16[4,4352]{1,0:T(4,128)(2,1)S(1)}, u32[]{:S(2)}, u32[]{:S(2)}) collective-permute-start(bf16[4,4352]{1,0:T(4,128)(2,1)S(1)} %get-tuple-element.23), channel_id=1, source_target_pairs={{0,2},{1,11},{2,0},{3,9},{4,6},{5,15},{6,4},{7,13},{8,10},{9,3},{1... | collective-permute-start | bytes 104456 | tf_op jit(solution)/shard_map/ppermute | solution.py:353
  14.7 4.3 %collective-permute-start.6 = (bf16[4,4352]{1,0:T(4,128)(2,1)S(1)}, bf16[4,4352]{1,0:T(4,128)(2,1)S(1)}, u32[]{:S(2)}, u32[]{:S(2)}) collective-permute-start(bf16[4,4352]{1,0:T(4,128)(2,1)S(1)} %get-tuple-element.22), channel_id=1, source_target_pairs={{0,4},{1,13},{2,6},{3,15},{4,0},{5,9},{6,2},{7,11},{8,12},{9,5},{1... | collective-permute-start | bytes 104456 | tf_op jit(solution)/shard_map/ppermute | solution.py:353
  15.3 3.9 %collective-permute-start.7 = (bf16[4,4352]{1,0:T(4,128)(2,1)S(1)}, bf16[4,4352]{1,0:T(4,128)(2,1)S(1)}, u32[]{:S(2)}, u32[]{:S(2)}) collective-permute-start(bf16[4,4352]{1,0:T(4,128)(2,1)S(1)} %get-tuple-element.23), channel_id=1, source_target_pairs={{0,2},{1,9},{2,0},{3,11},{4,6},{5,13},{6,4},{7,15},{8,10},{9,1},{1... | collective-permute-start | bytes 104456 | tf_op jit(solution)/shard_map/ppermute | solution.py:353
  19.3 1.9 %collective-permute-start.8 = (f32[4,4352]{1,0:T(4,128)S(1)}, f32[4,4352]{1,0:T(4,128)S(1)}, u32[]{:S(2)}, u32[]{:S(2)}) collective-permute-start(f32[4,4352]{1,0:T(4,128)S(1)} %shard_map.70.own_ref), channel_id=1, source_target_pairs={{0,1},{1,0},{2,3},{3,2},{4,5},{5,4},{6,7},{7,6},{8,9},{9,8},{10,11... | collective-permute-start | bytes 208904 | tf_op jit(solution)/shard_map/ppermute | solution.py:353

commit v5 on v4

--- a/solution.py
+++ b/solution.py
@@ -97,7 +97,7 @@
     lead = lax.axis_index("rd") == 0
     two = two_ref[...].astype(F32)
     refs = jnp.concatenate(
-        [jnp.where(lead, one_ref[...].astype(F32), two), jnp.where(lead, two, own_ref[...].astype(F32))], axis=0
+        [jnp.where(lead, own_ref[...].astype(F32), two), jnp.where(lead, two, one_ref[...].astype(F32))], axis=0
     )
     squares = jnp.sum(refs * refs, axis=1, keepdims=True)
     stacked = jnp.concatenate([refs[:, b] for b in block_of], axis=0)
@@ -132,9 +132,11 @@
     arrived = jnp.concatenate(
         [rolled(arrived_ref[:top, :LANES], BOX), rolled(arrived_ref[:top, LANES:], BOX)], axis=1
     )
+    lead = lax.axis_index("rd") == 0
     scores = []
     for f in range(4):
-        scores += [scores_ref[f * half:f * half + per_dev], arrived[f * per_dev:(f + 1) * per_dev]]
+        here, there = scores_ref[f * half:f * half + per_dev], arrived[f * per_dev:(f + 1) * per_dev]
+        scores += [jnp.where(lead, there, here), jnp.where(lead, here, there)]
     scores = jnp.concatenate(scores, axis=0)
     highest = jnp.maximum(stats[0:1], other[0:1])
     summed = stats[1:2] * jnp.exp(stats[0:1] - highest) + other[1:2] * jnp.exp(other[0:1] - highest)
@@ -205,11 +207,11 @@
     width = pixels // pieces
     count = own_ref[:, extra] + other_ref[:, extra]
     count = count[:, 0:1] + count[:, 1:2] + count[:, 2:3]
-    scale = 1.0 / (count + 1.0)
+    divisor = count + 1.0
     copies = []
     for piece in range(pieces):
         span = pl.ds(piece * width, width)
-        means_ref[:, span] = (own_ref[:, span] + other_ref[:, span]) * scale
+        means_ref[:, span] = (own_ref[:, span] + other_ref[:, span]) / divisor
         copies.append(pltpu.make_async_copy(means_ref.at[:, span], means_hbm.at[:, span], sent.at[piece]))
         copies[-1].start()
     across = lax.broadcasted_iota(jnp.int32, (per_dev, per_dev), 1)
@@ -347,7 +349,7 @@
         devices = devices * lax.axis_size(axis)
     pairs = []
     for i in range(devices):
-        step = by(i & 1) if callable(by) else by
+        step = by(i) if callable(by) else by
         if step:
             pairs.append((i, i ^ step))
     return lax.ppermute(array, axes, pairs)
@@ -374,8 +376,8 @@
     capacity = read_rows // lax.axis_size("img")
     per_dev = references.shape[0]
     other_images = swapped_by(images, 1, ("rd",))
-    ref_one = swapped_by(references, 4)
-    ref_two = swapped_by(references, lambda rd: 12 if rd else 8)
+    ref_one = swapped_by(references, lambda i: 4 if i & 1 else 2)
+    ref_two = swapped_by(references, lambda i: (12 if i & 1 else 8) if (i >> 2) in (0, 3) else (9 if i & 1 else 13))
     shape = jax.ShapeDtypeStruct
     in_hbm = [pltpu.with_memory_space_constraint(x, pltpu.HBM) for x in (images, counts, owners, references)]
     turned, flat, slots, classes = call(
@@ -400,10 +402,10 @@
         (shape((per_dev, wide), BF16), shape((per_dev, wide), BF16), shape((1, LANES), F32), shape((per_dev, wide), BF16)),
         (scores, sent, arrived, flat), (), [pltpu.VMEM((8 * per_dev, pixels), F32)],
     )
-    two = swapped_by(far, lambda rd: 14 if rd else 6)
-    one = swapped_by(far, lambda rd: 12 if rd else 4)
-    four = swapped_by(near, lambda rd: 10 if rd else 2)
-    three = swapped_by(near, lambda rd: 8 if rd else 2)
+    two = swapped_by(far, lambda i: 14 if i & 1 else 6)
+    one = swapped_by(far, lambda i: 12 if i & 1 else 4)
+    four = swapped_by(near, lambda i: 10 if i & 1 else 2)
+    three = swapped_by(near, lambda i: 8 if i & 1 else 2)
     summed = call(add_kernel, shape((per_dev, wide), F32), (two, four, one, three, kept))
     other = swapped_by(summed, 1, ("rd",))
     outs = (shape((per_dev, pixels), F32), shape((1, per_dev), F32), shape((1, read_rows), F32))

time: 22.1 us -> 21.8 us (0.986)
  starting transfers between devices: 12 us -> 11.2 us
  waiting for transfers between devices: 4.89 us -> 5.3 us
    ppermute x9, starting transfers between devices: 12 us -> 11.2 us  [swapped_by(): return lax.ppermute(array, axes, pairs)]
    ppermute x9, waiting for transfers between devices: 4.89 us -> 5.3 us  [swapped_by(): return lax.ppermute(array, axes, pairs)]
where the time goes in v5:
time: 21.8 us; the launch traced here: 21.6 us
  starting transfers between devices  11.2 us (51%)
  waiting for transfers between devices  5.3 us (24%)
  Pallas kernels  4.49 us (21%)
  between operations  0.67 us (3%)
    ppermute x9, starting transfers between devices, swapped_by(): return lax.ppermute(array, axes, pairs)  11.2 us
    ppermute x9, waiting for transfers between devices, swapped_by(): return lax.ppermute(array, axes, pairs)  5.3 us
    pallas_call x5, Pallas kernels, call(): pl.pallas_call(kernel, out_shape=outs, in_specs=specs, out_specs=jax.tree...  4.49 us
  transfers between devices with their start and end apart: 9, of which 6 were waited for; matrix products, arithmetic and copies ran while one was open for 0% of the time, Pallas kernels for 10%

profile of v5, /device:TPU:0, one launch (start us, length us, event | category | flops | bytes accessed | tf_op | source)
XLA Modules:
  0.0 21.6 jit_solution(17391667953234556332)
XLA Ops:
  0.6 0.5 %collective-permute-start = (bf16[64,4096]{1,0:T(8,128)(2,1)}, bf16[64,4096]{1,0:T(8,128)(2,1)S(1)}, u32[]{:S(2)}, u32[]{:S(2)}) collective-permute-start(bf16[64,4096]{1,0:T(8,128)(2,1)} %own_hbm.1), channel_id=1, source_target_pairs={{0,1},{1,0},{2,3},{3,2},{4,5},{5,4},{6,7},{7,6},{8,9},{9,8},{10,11... | collective-permute-start | bytes 1572872 | tf_op jit(solution)/shard_map/ppermute | solution.py:355
  1.1 3.7 %collective-permute-start.1 = (bf16[4,4096]{1,0:T(4,128)(2,1)}, bf16[4,4096]{1,0:T(4,128)(2,1)S(1)}, u32[]{:S(2)}, u32[]{:S(2)}) collective-permute-start(bf16[4,4096]{1,0:T(4,128)(2,1)} %classes_hbm.1), channel_id=1, source_target_pairs={{0,8},{1,13},{2,10},{3,15},{4,9},{5,12},{6,11},{7,14},{8,5},{9,0},... | collective-permute-start | bytes 98312 | tf_op jit(solution)/shard_map/ppermute | solution.py:355
  4.8 1.5 %collective-permute-start.2 = (bf16[4,4096]{1,0:T(4,128)(2,1)}, bf16[4,4096]{1,0:T(4,128)(2,1)S(1)}, u32[]{:S(2)}, u32[]{:S(2)}) collective-permute-start(bf16[4,4096]{1,0:T(4,128)(2,1)} %classes_hbm.1), channel_id=1, source_target_pairs={{0,2},{1,5},{2,0},{3,7},{4,6},{5,1},{6,4},{7,3},{8,10},{9,13},{10,... | collective-permute-start | bytes 98312 | tf_op jit(solution)/shard_map/ppermute | solution.py:355
  6.3 0.0 collective-permute-done.other_ref
  6.3 2.2 %shard_map.67 = (bf16[4096,256]{1,0:T(8,128)(2,1)S(1)}, bf16[256,4096]{1,0:T(8,128)(2,1)S(1)}, f32[8,128]{1,0:T(8,128)S(1)}, bf16[4,4096]{1,0:T(4,128)(2,1)S(1)}) custom-call(bf16[64,4096]{1,0:T(8,128)(2,1)} %own_hbm.1, s32[1,4]{1,0:T(1,128)} %counts_hbm.1, s32[1,4]{1,0:T(1,128)} %owners_hbm.1, bf16[4,4096]{1,0:T(4,128)(2,1)} %classes_hbm.1, ...), custom_call_target="tpu_custom_call" | custom-call | tf_op jit(solution)/shard_map/pallas_call | solution.py:364
  8.5 0.0 collective-permute-done.1.two_ref
  8.5 0.4 %collective-permute-done.2.one_ref = bf16[4,4096]{1,0:T(4,128)(2,1)S(1)} collective-permute-done((bf16[4,4096]{1,0:T(4,128)(2,1)}, bf16[4,4096]{1,0:T(4,128)(2,1)S(1)}, u32[]{:S(2)}, u32[]{:S(2)}) %collective-permute-start.2) | collective-permute-done | bytes 32800 | tf_op jit(solution)/shard_map/ppermute | solution.py:355
  8.9 0.6 %shard_map.68 = (f32[32,256]{1,0:T(8,128)S(1)}, f32[24,256]{1,0:T(8,128)S(1)}) custom-call(f32[8,128]{1,0:T(8,128)S(1)} %get-tuple-element.16.slots_ref, bf16[4,4096]{1,0:T(4,128)(2,1)S(1)} %collective-permute-done.1.two_ref, bf16[4,4096]{1,0:T(4,128)(2,1)S(1)} %collective-permute-done.2.one_ref, bf16[4,4096]{1,0:T(4,128)(2,1)S(1)} %get-tuple-element.17.own_ref, ...), custom_call_target="tpu_custom_call" | custom-call | tf_op jit(solution)/shard_map/pallas_call | solution.py:364
  9.6 0.2 collective-permute-start.3
  9.7 1.1 %collective-permute-done.3.arrived_ref = f32[24,256]{1,0:T(8,128)S(1)} collective-permute-done((f32[24,256]{1,0:T(8,128)S(1)}, f32[24,256]{1,0:T(8,128)S(1)}, u32[]{:S(2)}, u32[]{:S(2)}) %collective-permute-start.3) | collective-permute-done | bytes 24608 | tf_op jit(solution)/shard_map/ppermute | solution.py:355
  10.8 0.8 %shard_map.69 = (bf16[4,4352]{1,0:T(4,128)(2,1)S(1)}, bf16[4,4352]{1,0:T(4,128)(2,1)S(1)}, f32[1,128]{1,0:T(1,128)S(1)}, bf16[4,4352]{1,0:T(4,128)(2,1)S(1)}) custom-call(f32[32,256]{1,0:T(8,128)S(1)} %get-tuple-element.19.scores_ref, f32[24,256]{1,0:T(8,128)S(1)} %get-tuple-element.20.sent_ref, f32[24,256]{1,0:T(8,128)S(1)} %collective-permute-done.3.arrived_ref, ...), custom_call_target="tpu_custom_call" | custom-call | tf_op jit(solution)/shard_map/pallas_call | solution.py:364
  11.6 1.7 %collective-permute-start.4 = (bf16[4,4352]{1,0:T(4,128)(2,1)S(1)}, bf16[4,4352]{1,0:T(4,128)(2,1)S(1)}, u32[]{:S(2)}, u32[]{:S(2)}) collective-permute-start(bf16[4,4352]{1,0:T(4,128)(2,1)S(1)} %get-tuple-element.22), channel_id=1, source_target_pairs={{0,6},{1,15},{2,4},{3,13},{4,2},{5,11},{6,0},{7,9},{8,14},{9,7},{1... | collective-permute-start | bytes 104456 | tf_op jit(solution)/shard_map/ppermute | solution.py:355
  13.3 0.5 %collective-permute-start.5 = (bf16[4,4352]{1,0:T(4,128)(2,1)S(1)}, bf16[4,4352]{1,0:T(4,128)(2,1)S(1)}, u32[]{:S(2)}, u32[]{:S(2)}) collective-permute-start(bf16[4,4352]{1,0:T(4,128)(2,1)S(1)} %get-tuple-element.23), channel_id=1, source_target_pairs={{0,2},{1,11},{2,0},{3,9},{4,6},{5,15},{6,4},{7,13},{8,10},{9,3},{1... | collective-permute-start | bytes 104456 | tf_op jit(solution)/shard_map/ppermute | solution.py:355
  13.8 1.3 %collective-permute-start.6 = (bf16[4,4352]{1,0:T(4,128)(2,1)S(1)}, bf16[4,4352]{1,0:T(4,128)(2,1)S(1)}, u32[]{:S(2)}, u32[]{:S(2)}) collective-permute-start(bf16[4,4352]{1,0:T(4,128)(2,1)S(1)} %get-tuple-element.22), channel_id=1, source_target_pairs={{0,4},{1,13},{2,6},{3,15},{4,0},{5,9},{6,2},{7,11},{8,12},{9,5},{1... | collective-permute-start | bytes 104456 | tf_op jit(solution)/shard_map/ppermute | solution.py:355
  15.2 1.5 %collective-permute-start.7 = (bf16[4,4352]{1,0:T(4,128)(2,1)S(1)}, bf16[4,4352]{1,0:T(4,128)(2,1)S(1)}, u32[]{:S(2)}, u32[]{:S(2)}) collective-permute-start(bf16[4,4352]{1,0:T(4,128)(2,1)S(1)} %get-tuple-element.23), channel_id=1, source_target_pairs={{0,2},{1,9},{2,0},{3,11},{4,6},{5,13},{6,4},{7,15},{8,10},{9,1},{1... | collective-permute-start | bytes 104456 | tf_op jit(solution)/shard_map/ppermute | solution.py:355
  16.6 0.0 collective-permute-done.4.two_ref
  16.6 1.0 %collective-permute-done.5.four_ref = bf16[4,4352]{1,0:T(4,128)(2,1)S(1)} collective-permute-done((bf16[4,4352]{1,0:T(4,128)(2,1)S(1)}, bf16[4,4352]{1,0:T(4,128)(2,1)S(1)}, u32[]{:S(2)}, u32[]{:S(2)}) %collective-permute-start.5) | collective-permute-done | bytes 34848 | tf_op jit(solution)/shard_map/ppermute | solution.py:355
  17.6 0.3 %collective-permute-done.6.one_ref = bf16[4,4352]{1,0:T(4,128)(2,1)S(1)} collective-permute-done((bf16[4,4352]{1,0:T(4,128)(2,1)S(1)}, bf16[4,4352]{1,0:T(4,128)(2,1)S(1)}, u32[]{:S(2)}, u32[]{:S(2)}) %collective-permute-start.6) | collective-permute-done | bytes 34848 | tf_op jit(solution)/shard_map/ppermute | solution.py:355
  17.9 1.6 %collective-permute-done.7.three_ref = bf16[4,4352]{1,0:T(4,128)(2,1)S(1)} collective-permute-done((bf16[4,4352]{1,0:T(4,128)(2,1)S(1)}, bf16[4,4352]{1,0:T(4,128)(2,1)S(1)}, u32[]{:S(2)}, u32[]{:S(2)}) %collective-permute-start.7) | collective-permute-done | bytes 34848 | tf_op jit(solution)/shard_map/ppermute | solution.py:355
  19.5 0.3 %collective-permute-start.8 = (f32[4,4352]{1,0:T(4,128)S(1)}, f32[4,4352]{1,0:T(4,128)S(1)}, u32[]{:S(2)}, u32[]{:S(2)}) collective-permute-start(f32[4,4352]{1,0:T(4,128)S(1)} %shard_map.70.own_ref), channel_id=1, source_target_pairs={{0,1},{1,0},{2,3},{3,2},{4,5},{5,4},{6,7},{7,6},{8,9},{9,8},{10,11... | collective-permute-start | bytes 208904 | tf_op jit(solution)/shard_map/ppermute | solution.py:355
  19.8 1.0 %collective-permute-done.8.other_ref = f32[4,4352]{1,0:T(4,128)S(1)} collective-permute-done((f32[4,4352]{1,0:T(4,128)S(1)}, f32[4,4352]{1,0:T(4,128)S(1)}, u32[]{:S(2)}, u32[]{:S(2)}) %collective-permute-start.8) | collective-permute-done | bytes 69664 | tf_op jit(solution)/shard_map/ppermute | solution.py:355
  20.8 0.8 %shard_map.71 = (f32[4,4096]{1,0:T(4,128)}, f32[1,4]{1,0:T(1,128)}, f32[1,64]{1,0:T(1,128)}) custom-call(f32[4,4352]{1,0:T(4,128)S(1)} %shard_map.70.own_ref, f32[4,4352]{1,0:T(4,128)S(1)} %collective-permute-done.8.other_ref, f32[1,128]{1,0:T(1,128)S(1)} %get-tuple-element.25.total_ref), custom_call_target="tpu_custom_call" | custom-call | tf_op jit(solution)/shard_map/pallas_call | solution.py:364
  (1 shorter events, 0.0 us)
Async XLA Ops:
  0.6 5.7 %collective-permute-start = (bf16[64,4096]{1,0:T(8,128)(2,1)}, bf16[64,4096]{1,0:T(8,128)(2,1)S(1)}, u32[]{:S(2)}, u32[]{:S(2)}) collective-permute-start(bf16[64,4096]{1,0:T(8,128)(2,1)} %own_hbm.1), channel_id=1, source_target_pairs={{0,1},{1,0},{2,3},{3,2},{4,5},{5,4},{6,7},{7,6},{8,9},{9,8},{10,11... | collective-permute-start | bytes 1572872 | tf_op jit(solution)/shard_map/ppermute | solution.py:355
  1.1 7.4 %collective-permute-start.1 = (bf16[4,4096]{1,0:T(4,128)(2,1)}, bf16[4,4096]{1,0:T(4,128)(2,1)S(1)}, u32[]{:S(2)}, u32[]{:S(2)}) collective-permute-start(bf16[4,4096]{1,0:T(4,128)(2,1)} %classes_hbm.1), channel_id=1, source_target_pairs={{0,8},{1,13},{2,10},{3,15},{4,9},{5,12},{6,11},{7,14},{8,5},{9,0},... | collective-permute-start | bytes 98312 | tf_op jit(solution)/shard_map/ppermute | solution.py:355
  4.8 4.1 %collective-permute-start.2 = (bf16[4,4096]{1,0:T(4,128)(2,1)}, bf16[4,4096]{1,0:T(4,128)(2,1)S(1)}, u32[]{:S(2)}, u32[]{:S(2)}) collective-permute-start(bf16[4,4096]{1,0:T(4,128)(2,1)} %classes_hbm.1), channel_id=1, source_target_pairs={{0,2},{1,5},{2,0},{3,7},{4,6},{5,1},{6,4},{7,3},{8,10},{9,13},{10,... | collective-permute-start | bytes 98312 | tf_op jit(solution)/shard_map/ppermute | solution.py:355
  9.6 1.3 %collective-permute-start.3 = (f32[24,256]{1,0:T(8,128)S(1)}, f32[24,256]{1,0:T(8,128)S(1)}, u32[]{:S(2)}, u32[]{:S(2)}) collective-permute-start(f32[24,256]{1,0:T(8,128)S(1)} %get-tuple-element.20.sent_ref), channel_id=1, source_target_pairs={{0,1},{1,0},{2,3},{3,2},{4,5},{5,4},{6,7},{7,6},{8,9},{9,8},{10,11... | collective-permute-start | bytes 73736 | tf_op jit(solution)/shard_map/ppermute | solution.py:355
  11.6 5.0 %collective-permute-start.4 = (bf16[4,4352]{1,0:T(4,128)(2,1)S(1)}, bf16[4,4352]{1,0:T(4,128)(2,1)S(1)}, u32[]{:S(2)}, u32[]{:S(2)}) collective-permute-start(bf16[4,4352]{1,0:T(4,128)(2,1)S(1)} %get-tuple-element.22), channel_id=1, source_target_pairs={{0,6},{1,15},{2,4},{3,13},{4,2},{5,11},{6,0},{7,9},{8,14},{9,7},{1... | collective-permute-start | bytes 104456 | tf_op jit(solution)/shard_map/ppermute | solution.py:355
  13.3 4.3 %collective-permute-start.5 = (bf16[4,4352]{1,0:T(4,128)(2,1)S(1)}, bf16[4,4352]{1,0:T(4,128)(2,1)S(1)}, u32[]{:S(2)}, u32[]{:S(2)}) collective-permute-start(bf16[4,4352]{1,0:T(4,128)(2,1)S(1)} %get-tuple-element.23), channel_id=1, source_target_pairs={{0,2},{1,11},{2,0},{3,9},{4,6},{5,15},{6,4},{7,13},{8,10},{9,3},{1... | collective-permute-start | bytes 104456 | tf_op jit(solution)/shard_map/ppermute | solution.py:355
  13.8 4.1 %collective-permute-start.6 = (bf16[4,4352]{1,0:T(4,128)(2,1)S(1)}, bf16[4,4352]{1,0:T(4,128)(2,1)S(1)}, u32[]{:S(2)}, u32[]{:S(2)}) collective-permute-start(bf16[4,4352]{1,0:T(4,128)(2,1)S(1)} %get-tuple-element.22), channel_id=1, source_target_pairs={{0,4},{1,13},{2,6},{3,15},{4,0},{5,9},{6,2},{7,11},{8,12},{9,5},{1... | collective-permute-start | bytes 104456 | tf_op jit(solution)/shard_map/ppermute | solution.py:355
  15.2 4.3 %collective-permute-start.7 = (bf16[4,4352]{1,0:T(4,128)(2,1)S(1)}, bf16[4,4352]{1,0:T(4,128)(2,1)S(1)}, u32[]{:S(2)}, u32[]{:S(2)}) collective-permute-start(bf16[4,4352]{1,0:T(4,128)(2,1)S(1)} %get-tuple-element.23), channel_id=1, source_target_pairs={{0,2},{1,9},{2,0},{3,11},{4,6},{5,13},{6,4},{7,15},{8,10},{9,1},{1... | collective-permute-start | bytes 104456 | tf_op jit(solution)/shard_map/ppermute | solution.py:355
  19.5 1.3 %collective-permute-start.8 = (f32[4,4352]{1,0:T(4,128)S(1)}, f32[4,4352]{1,0:T(4,128)S(1)}, u32[]{:S(2)}, u32[]{:S(2)}) collective-permute-start(f32[4,4352]{1,0:T(4,128)S(1)} %shard_map.70.own_ref), channel_id=1, source_target_pairs={{0,1},{1,0},{2,3},{3,2},{4,5},{5,4},{6,7},{7,6},{8,9},{9,8},{10,11... | collective-permute-start | bytes 208904 | tf_op jit(solution)/shard_map/ppermute | solution.py:355

commit v6 on v5

--- a/solution.py
+++ b/solution.py
@@ -43,14 +43,14 @@
 
 
 def turn_kernel(capacity, own_hbm, counts_hbm, owners_hbm, classes_hbm, other_ref,
-                out_ref, flat_ref, slots_ref, classes_ref, own_ref, counts_ref, owners_ref, arrived):
+                out_ref, flat_ref, slots_ref, classes_ref, counts_ref, owners_ref, arrived):
     pixels = other_ref.shape[1]
     pieces = arrived.shape[0] - 3
     width = pixels // pieces
     copies = []
     for piece in range(pieces):
         span = pl.ds(piece * width, width)
-        copies.append(pltpu.make_async_copy(own_hbm.at[:, span], own_ref.at[:, span], arrived.at[piece]))
+        copies.append(pltpu.make_async_copy(own_hbm.at[:, span], flat_ref.at[pl.ds(0, other_ref.shape[0]), span], arrived.at[piece]))
         copies[-1].start()
     small = [
         pltpu.make_async_copy(source, target, arrived.at[pieces + i])
@@ -63,8 +63,8 @@
     for block, span in enumerate(spans(pixels)):
         if block * LANES % width == 0:
             copies[block * LANES // width].wait()
-        tile = jnp.concatenate([own_ref[:, span], other_ref[:, span]], axis=0)
-        flat_ref[:LANES, span] = tile
+        flat_ref[other_ref.shape[0]:LANES, span] = other_ref[:, span]
+        tile = flat_ref[:LANES, span]
         out_ref[span, :LANES] = tile.T
     square = out_ref[:, :LANES].reshape(BOX, BOX, LANES)
     out_ref[:, LANES:] = jnp.swapaxes(square, 0, 1).reshape(pixels, LANES)
@@ -83,6 +83,12 @@
     return high, middle, (rest - middle).astype(BF16).astype(F32)
 
 
+def leads():
+    place = lax.axis_index("cls")
+    inner = ((place == 1) | (place == 2)).astype(jnp.int32)
+    return lax.axis_index("rd") == inner
+
+
 def mirror_of_rows():
     row = lax.broadcasted_iota(jnp.int32, (LANES, LANES), 0)
     column = lax.broadcasted_iota(jnp.int32, (LANES, LANES), 1)
@@ -94,11 +100,8 @@
     per_dev, pixels = own_ref.shape
     half = 2 * per_dev
     block_of = spans(pixels)
-    lead = lax.axis_index("rd") == 0
-    two = two_ref[...].astype(F32)
-    refs = jnp.concatenate(
-        [jnp.where(lead, own_ref[...].astype(F32), two), jnp.where(lead, two, one_ref[...].astype(F32))], axis=0
-    )
+    swapped_block = jnp.where(leads(), one_ref[...].astype(F32), own_ref[...].astype(F32))
+    refs = jnp.concatenate([two_ref[...].astype(F32), swapped_block], axis=0)
     squares = jnp.sum(refs * refs, axis=1, keepdims=True)
     stacked = jnp.concatenate([refs[:, b] for b in block_of], axis=0)
     mirrored = jnp.dot(stacked.astype(BF16), mirror_of_rows(), preferred_element_type=F32)
@@ -132,7 +135,7 @@
     arrived = jnp.concatenate(
         [rolled(arrived_ref[:top, :LANES], BOX), rolled(arrived_ref[:top, LANES:], BOX)], axis=1
     )
-    lead = lax.axis_index("rd") == 0
+    lead = leads()
     scores = []
     for f in range(4):
         here, there = scores_ref[f * half:f * half + per_dev], arrived[f * per_dev:(f + 1) * per_dev]
@@ -182,18 +185,18 @@
     )
     total_ref[...] = pieces[0:1] + pieces[1:2] + pieces[2:3]
     last = slice(pixels + LANES, pixels + 2 * LANES)
-    first_ref[:, last] = jnp.zeros((per_dev, LANES), BF16)
-    second_ref[:, last] = pieces[:per_dev].astype(BF16)
-    kept_ref[...] = second_ref[...]
-
-
-def add_kernel(two_ref, four_ref, one_ref, three_ref, own_ref, out_ref):
+    first_ref[:, last] = pieces[:per_dev].astype(BF16)
+    second_ref[:, last] = jnp.zeros((per_dev, LANES), BF16)
+    kept_ref[...] = first_ref[...]
+
+
+def add_kernel(pd_ref, qx_ref, po_ref, qx1_ref, kept_ref, out_ref):
     pixels = out_ref.shape[1] - LANES
-    middle = jnp.where(lax.axis_index("rd") == 1, three_ref[:, :pixels].astype(F32), own_ref[:, :pixels].astype(F32))
-    out_ref[:, :pixels] = (one_ref[:, :pixels].astype(F32) + two_ref[:, :pixels].astype(F32)) + (
-        middle + four_ref[:, :pixels].astype(F32)
-    )
-    pieces = four_ref[:, pixels:].astype(F32)
+    own = jnp.where(leads(), kept_ref[:, :pixels].astype(F32), pd_ref[:, :pixels].astype(F32))
+    out_ref[:, :pixels] = (qx_ref[:, :pixels].astype(F32) + qx1_ref[:, :pixels].astype(F32)) + (
+        own + po_ref[:, :pixels].astype(F32)
+    )
+    pieces = po_ref[:, pixels:].astype(F32)
     out_ref[:, pixels:] = jnp.broadcast_to(pieces[0:1] + pieces[1:2] + pieces[2:3], (out_ref.shape[0], LANES))
 
 
@@ -220,9 +223,7 @@
     copies.append(pltpu.make_async_copy(weights_ref, weights_hbm, sent.at[pieces]))
     copies[-1].start()
     first = lax.axis_index("img") == 0
-    arrived = jnp.where(
-        lax.axis_index("rd") == 1, rolled(other_ref[0:1, last], 2 * capacity), own_ref[0:1, last]
-    )
+    arrived = jnp.where(leads(), own_ref[0:1, last], rolled(other_ref[0:1, last], 2 * capacity))
     arrived = jnp.where(first, arrived[:, :capacity], arrived[:, capacity:2 * capacity])
     mine = jnp.where(first, total_ref[:, :capacity], total_ref[:, capacity:2 * capacity])
     loglik_ref[:, :capacity] = jnp.where(first, mine, arrived)
@@ -343,16 +344,17 @@
     return (class_means, own_totals, row_loglik)
 
 
-def swapped_by(array, by, axes=LINKED):
-    devices = 1
-    for axis in axes:
-        devices = devices * lax.axis_size(axis)
+def swapped(array):
+    return lax.ppermute(array, "rd", [(0, 1), (1, 0)])
+
+
+def traded(array, steps):
     pairs = []
-    for i in range(devices):
-        step = by(i) if callable(by) else by
-        if step:
-            pairs.append((i, i ^ step))
-    return lax.ppermute(array, axes, pairs)
+    for source in range(16):
+        role = (source & 1) ^ (source >> 2 in (1, 2))
+        target = (source & ~1) ^ steps[role]
+        pairs.append((source, target | (role ^ (target >> 2 in (1, 2)))))
+    return lax.ppermute(array, LINKED, pairs)
 
 
 def call(kernel, outs, args, scalars=(), scratch=(), in_hbm=(), outs_in_hbm=False):
@@ -373,11 +375,13 @@
 
 def direct(images, counts, owners, references):
     read_rows, pixels = images.shape
+    if 2 * read_rows != LANES:
+        return local(images, counts, owners, references)
     capacity = read_rows // lax.axis_size("img")
     per_dev = references.shape[0]
-    other_images = swapped_by(images, 1, ("rd",))
-    ref_one = swapped_by(references, lambda i: 4 if i & 1 else 2)
-    ref_two = swapped_by(references, lambda i: (12 if i & 1 else 8) if (i >> 2) in (0, 3) else (9 if i & 1 else 13))
+    other_images = swapped(images)
+    ref_one = traded(references, (4, 2))
+    ref_two = traded(references, (8, 12))
     shape = jax.ShapeDtypeStruct
     in_hbm = [pltpu.with_memory_space_constraint(x, pltpu.HBM) for x in (images, counts, owners, references)]
     turned, flat, slots, classes = call(
@@ -385,7 +389,7 @@
         (shape((pixels, 2 * LANES), BF16), shape((2 * LANES, pixels), BF16), shape((8, LANES), F32),
          shape(references.shape, BF16)),
         (*in_hbm, other_images), (),
-        [pltpu.VMEM((read_rows, pixels), BF16), pltpu.VMEM(counts.shape, jnp.int32),
+        [pltpu.VMEM(counts.shape, jnp.int32),
          pltpu.VMEM(owners.shape, jnp.int32), pltpu.SemaphoreType.DMA((5,))],
         in_hbm=(0, 1, 2, 3),
     )
@@ -395,19 +399,19 @@
         (slots, ref_two, ref_one, classes, turned), (),
         [pltpu.VMEM((8 * per_dev, pixels), BF16)],
     )
-    arrived = swapped_by(sent, 1, ("rd",))
+    arrived = swapped(sent)
     wide = pixels + 2 * LANES
-    far, near, totals, kept = call(
+    first, second, totals, kept = call(
         weigh_kernel,
         (shape((per_dev, wide), BF16), shape((per_dev, wide), BF16), shape((1, LANES), F32), shape((per_dev, wide), BF16)),
         (scores, sent, arrived, flat), (), [pltpu.VMEM((8 * per_dev, pixels), F32)],
     )
-    two = swapped_by(far, lambda i: 14 if i & 1 else 6)
-    one = swapped_by(far, lambda i: 12 if i & 1 else 4)
-    four = swapped_by(near, lambda i: 10 if i & 1 else 2)
-    three = swapped_by(near, lambda i: 8 if i & 1 else 2)
-    summed = call(add_kernel, shape((per_dev, wide), F32), (two, four, one, three, kept))
-    other = swapped_by(summed, 1, ("rd",))
+    po = traded(first, (2, 12))
+    pd = traded(first, (2, 14))
+    qx1 = traded(second, (10, 4))
+    qx = traded(second, (8, 6))
+    summed = call(add_kernel, shape((per_dev, wide), F32), (pd, qx, po, qx1, kept))
+    other = swapped(summed)
     outs = (shape((per_dev, pixels), F32), shape((1, per_dev), F32), shape((1, read_rows), F32))
     means, weights, loglik = call(
         finish_kernel, outs, (summed, other, totals), (),

time: 21.8 us -> 21.5 us (0.986)
  waiting for transfers between devices: 5.3 us -> 4.27 us
  starting transfers between devices: 11.2 us -> 12 us
    ppermute x9, waiting for transfers between devices: 5.3 us -> 4.27 us  [the longest x6 2.51 us: traded(): return lax.ppermute(array, LINKED, pairs)]
    ppermute x9, starting transfers between devices: 11.2 us -> 12 us  [the longest x6 9.92 us: traded(): return lax.ppermute(array, LINKED, pairs)]
  transfers between devices with their start and end apart: 9 -> 9, of which waited for: 6 -> 5; matrix products, arithmetic and copies ran while one was open for 0% -> 0% of each run, Pallas kernels for 10% -> 10%
where the time goes in v6:
time: 21.5 us; the launch traced here: 21.4 us
  starting transfers between devices  12 us (56%)
  Pallas kernels  4.4 us (20%)
  waiting for transfers between devices  4.27 us (20%)
  between operations  0.67 us (3%)
    ppermute x6, starting transfers between devices, traded(): return lax.ppermute(array, LINKED, pairs)  9.92 us
    pallas_call x5, Pallas kernels, call(): pl.pallas_call(kernel, out_shape=outs, in_specs=specs, out_specs=jax.tree...  4.4 us
    ppermute x6, waiting for transfers between devices, traded(): return lax.ppermute(array, LINKED, pairs)  2.51 us
    ppermute x3, starting transfers between devices, swapped(): return lax.ppermute(array, 'rd', [(0, 1), (1, 0)])  2.11 us
    ppermute x3, waiting for transfers between devices, swapped(): return lax.ppermute(array, 'rd', [(0, 1), (1, 0)])  1.76 us
  transfers between devices with their start and end apart: 9, of which 5 were waited for; matrix products, arithmetic and copies ran while one was open for 0% of the time, Pallas kernels for 10%

profile of v6, /device:TPU:0, one launch (start us, length us, event | category | flops | bytes accessed | tf_op | source)
XLA Modules:
  0.0 21.4 jit_solution(17738134772831208577)
XLA Ops:
  0.6 0.5 %collective-permute-start = (bf16[64,4096]{1,0:T(8,128)(2,1)}, bf16[64,4096]{1,0:T(8,128)(2,1)S(1)}, u32[]{:S(2)}, u32[]{:S(2)}) collective-permute-start(bf16[64,4096]{1,0:T(8,128)(2,1)} %own_hbm.1), channel_id=1, source_target_pairs={{0,1},{1,0},{2,3},{3,2},{4,5},{5,4},{6,7},{7,6},{8,9},{9,8},{10,11... | collective-permute-start | bytes 1572872 | tf_op jit(solution)/shard_map/ppermute | solution.py:348
  1.1 3.7 %collective-permute-start.1 = (bf16[4,4096]{1,0:T(4,128)(2,1)}, bf16[4,4096]{1,0:T(4,128)(2,1)S(1)}, u32[]{:S(2)}, u32[]{:S(2)}) collective-permute-start(bf16[4,4096]{1,0:T(4,128)(2,1)} %classes_hbm.1), channel_id=1, source_target_pairs={{0,9},{1,13},{2,11},{3,15},{4,8},{5,12},{6,10},{7,14},{8,4},{9,0},... | collective-permute-start | bytes 98312 | tf_op jit(solution)/shard_map/ppermute | solution.py:357
  4.8 1.3 %collective-permute-start.2 = (bf16[4,4096]{1,0:T(4,128)(2,1)}, bf16[4,4096]{1,0:T(4,128)(2,1)S(1)}, u32[]{:S(2)}, u32[]{:S(2)}) collective-permute-start(bf16[4,4096]{1,0:T(4,128)(2,1)} %classes_hbm.1), channel_id=1, source_target_pairs={{0,5},{1,3},{2,7},{3,1},{4,6},{5,0},{6,4},{7,2},{8,10},{9,12},{10,... | collective-permute-start | bytes 98312 | tf_op jit(solution)/shard_map/ppermute | solution.py:357
  6.1 0.0 collective-permute-done.other_ref
  6.1 2.1 %shard_map.67 = (bf16[4096,256]{1,0:T(8,128)(2,1)S(1)}, bf16[256,4096]{1,0:T(8,128)(2,1)S(1)}, f32[8,128]{1,0:T(8,128)S(1)}, bf16[4,4096]{1,0:T(4,128)(2,1)S(1)}) custom-call(bf16[64,4096]{1,0:T(8,128)(2,1)} %own_hbm.1, s32[1,4]{1,0:T(1,128)} %counts_hbm.1, s32[1,4]{1,0:T(1,128)} %owners_hbm.1, bf16[4,4096]{1,0:T(4,128)(2,1)} %classes_hbm.1, ...), custom_call_target="tpu_custom_call" | custom-call | tf_op jit(solution)/shard_map/pallas_call | solution.py:366
  8.3 0.0 collective-permute-done.1.two_ref
  8.3 0.1 collective-permute-done.2.one_ref
  8.4 0.6 %shard_map.68 = (f32[32,256]{1,0:T(8,128)S(1)}, f32[24,256]{1,0:T(8,128)S(1)}) custom-call(f32[8,128]{1,0:T(8,128)S(1)} %get-tuple-element.16.slots_ref, bf16[4,4096]{1,0:T(4,128)(2,1)S(1)} %collective-permute-done.1.two_ref, bf16[4,4096]{1,0:T(4,128)(2,1)S(1)} %collective-permute-done.2.one_ref, bf16[4,4096]{1,0:T(4,128)(2,1)S(1)} %get-tuple-element.17.own_ref, ...), custom_call_target="tpu_custom_call" | custom-call | tf_op jit(solution)/shard_map/pallas_call | solution.py:366
  9.0 1.0 %collective-permute-start.3 = (f32[24,256]{1,0:T(8,128)S(1)}, f32[24,256]{1,0:T(8,128)S(1)}, u32[]{:S(2)}, u32[]{:S(2)}) collective-permute-start(f32[24,256]{1,0:T(8,128)S(1)} %get-tuple-element.20.sent_ref), channel_id=1, source_target_pairs={{0,1},{1,0},{2,3},{3,2},{4,5},{5,4},{6,7},{7,6},{8,9},{9,8},{10,11... | collective-permute-start | bytes 73736 | tf_op jit(solution)/shard_map/ppermute | solution.py:348
  10.1 0.8 %collective-permute-done.3.arrived_ref = f32[24,256]{1,0:T(8,128)S(1)} collective-permute-done((f32[24,256]{1,0:T(8,128)S(1)}, f32[24,256]{1,0:T(8,128)S(1)}, u32[]{:S(2)}, u32[]{:S(2)}) %collective-permute-start.3) | collective-permute-done | bytes 24608 | tf_op jit(solution)/shard_map/ppermute | solution.py:348
  10.9 0.8 %shard_map.69 = (bf16[4,4352]{1,0:T(4,128)(2,1)S(1)}, bf16[4,4352]{1,0:T(4,128)(2,1)S(1)}, f32[1,128]{1,0:T(1,128)S(1)}, bf16[4,4352]{1,0:T(4,128)(2,1)S(1)}) custom-call(f32[32,256]{1,0:T(8,128)S(1)} %get-tuple-element.19.scores_ref, f32[24,256]{1,0:T(8,128)S(1)} %get-tuple-element.20.sent_ref, f32[24,256]{1,0:T(8,128)S(1)} %collective-permute-done.3.arrived_ref, ...), custom_call_target="tpu_custom_call" | custom-call | tf_op jit(solution)/shard_map/pallas_call | solution.py:366
  11.7 1.1 %collective-permute-start.4 = (bf16[4,4352]{1,0:T(4,128)(2,1)S(1)}, bf16[4,4352]{1,0:T(4,128)(2,1)S(1)}, u32[]{:S(2)}, u32[]{:S(2)}) collective-permute-start(bf16[4,4352]{1,0:T(4,128)(2,1)S(1)} %get-tuple-element.22), channel_id=1, source_target_pairs={{0,2},{1,15},{2,0},{3,13},{4,10},{5,7},{6,8},{7,5},{8,6},{9,11},{1... | collective-permute-start | bytes 104456 | tf_op jit(solution)/shard_map/ppermute | solution.py:357
  12.8 0.4 %collective-permute-start.5 = (bf16[4,4352]{1,0:T(4,128)(2,1)S(1)}, bf16[4,4352]{1,0:T(4,128)(2,1)S(1)}, u32[]{:S(2)}, u32[]{:S(2)}) collective-permute-start(bf16[4,4352]{1,0:T(4,128)(2,1)S(1)} %get-tuple-element.23), channel_id=1, source_target_pairs={{0,9},{1,6},{2,11},{3,4},{4,3},{5,12},{6,1},{7,14},{8,15},{9,0},{1... | collective-permute-start | bytes 104456 | tf_op jit(solution)/shard_map/ppermute | solution.py:357
  13.2 0.5 %collective-permute-start.6 = (bf16[4,4352]{1,0:T(4,128)(2,1)S(1)}, bf16[4,4352]{1,0:T(4,128)(2,1)S(1)}, u32[]{:S(2)}, u32[]{:S(2)}) collective-permute-start(bf16[4,4352]{1,0:T(4,128)(2,1)S(1)} %get-tuple-element.22), channel_id=1, source_target_pairs={{0,2},{1,13},{2,0},{3,15},{4,8},{5,7},{6,10},{7,5},{8,4},{9,11},{1... | collective-permute-start | bytes 104456 | tf_op jit(solution)/shard_map/ppermute | solution.py:357
  13.8 2.9 %collective-permute-start.7 = (bf16[4,4352]{1,0:T(4,128)(2,1)S(1)}, bf16[4,4352]{1,0:T(4,128)(2,1)S(1)}, u32[]{:S(2)}, u32[]{:S(2)}) collective-permute-start(bf16[4,4352]{1,0:T(4,128)(2,1)S(1)} %get-tuple-element.23), channel_id=1, source_target_pairs={{0,11},{1,4},{2,9},{3,6},{4,1},{5,14},{6,3},{7,12},{8,13},{9,2},{1... | collective-permute-start | bytes 104456 | tf_op jit(solution)/shard_map/ppermute | solution.py:357
  16.7 0.0 collective-permute-done.4.pd_ref
  16.7 0.8 %collective-permute-done.5.qx_ref = bf16[4,4352]{1,0:T(4,128)(2,1)S(1)} collective-permute-done((bf16[4,4352]{1,0:T(4,128)(2,1)S(1)}, bf16[4,4352]{1,0:T(4,128)(2,1)S(1)}, u32[]{:S(2)}, u32[]{:S(2)}) %collective-permute-start.5) | collective-permute-done | bytes 34848 | tf_op jit(solution)/shard_map/ppermute | solution.py:357
  17.5 0.0 collective-permute-done.6.po_ref
  17.5 1.6 %collective-permute-done.7.qx1_ref = bf16[4,4352]{1,0:T(4,128)(2,1)S(1)} collective-permute-done((bf16[4,4352]{1,0:T(4,128)(2,1)S(1)}, bf16[4,4352]{1,0:T(4,128)(2,1)S(1)}, u32[]{:S(2)}, u32[]{:S(2)}) %collective-permute-start.7) | collective-permute-done | bytes 34848 | tf_op jit(solution)/shard_map/ppermute | solution.py:357
  19.1 0.6 %collective-permute-start.8 = (f32[4,4352]{1,0:T(4,128)S(1)}, f32[4,4352]{1,0:T(4,128)S(1)}, u32[]{:S(2)}, u32[]{:S(2)}) collective-permute-start(f32[4,4352]{1,0:T(4,128)S(1)} %shard_map.70.own_ref), channel_id=1, source_target_pairs={{0,1},{1,0},{2,3},{3,2},{4,5},{5,4},{6,7},{7,6},{8,9},{9,8},{10,11... | collective-permute-start | bytes 208904 | tf_op jit(solution)/shard_map/ppermute | solution.py:348
  19.6 0.9 %collective-permute-done.8.other_ref = f32[4,4352]{1,0:T(4,128)S(1)} collective-permute-done((f32[4,4352]{1,0:T(4,128)S(1)}, f32[4,4352]{1,0:T(4,128)S(1)}, u32[]{:S(2)}, u32[]{:S(2)}) %collective-permute-start.8) | collective-permute-done | bytes 69664 | tf_op jit(solution)/shard_map/ppermute | solution.py:348
  20.5 0.8 %shard_map.71 = (f32[4,4096]{1,0:T(4,128)}, f32[1,4]{1,0:T(1,128)}, f32[1,64]{1,0:T(1,128)}) custom-call(f32[4,4352]{1,0:T(4,128)S(1)} %shard_map.70.own_ref, f32[4,4352]{1,0:T(4,128)S(1)} %collective-permute-done.8.other_ref, f32[1,128]{1,0:T(1,128)S(1)} %get-tuple-element.25.total_ref), custom_call_target="tpu_custom_call" | custom-call | tf_op jit(solution)/shard_map/pallas_call | solution.py:366
  (1 shorter events, 0.0 us)
Async XLA Ops:
  0.6 5.5 %collective-permute-start = (bf16[64,4096]{1,0:T(8,128)(2,1)}, bf16[64,4096]{1,0:T(8,128)(2,1)S(1)}, u32[]{:S(2)}, u32[]{:S(2)}) collective-permute-start(bf16[64,4096]{1,0:T(8,128)(2,1)} %own_hbm.1), channel_id=1, source_target_pairs={{0,1},{1,0},{2,3},{3,2},{4,5},{5,4},{6,7},{7,6},{8,9},{9,8},{10,11... | collective-permute-start | bytes 1572872 | tf_op jit(solution)/shard_map/ppermute | solution.py:348
  1.1 7.1 %collective-permute-start.1 = (bf16[4,4096]{1,0:T(4,128)(2,1)}, bf16[4,4096]{1,0:T(4,128)(2,1)S(1)}, u32[]{:S(2)}, u32[]{:S(2)}) collective-permute-start(bf16[4,4096]{1,0:T(4,128)(2,1)} %classes_hbm.1), channel_id=1, source_target_pairs={{0,9},{1,13},{2,11},{3,15},{4,8},{5,12},{6,10},{7,14},{8,4},{9,0},... | collective-permute-start | bytes 98312 | tf_op jit(solution)/shard_map/ppermute | solution.py:357
  4.8 3.6 %collective-permute-start.2 = (bf16[4,4096]{1,0:T(4,128)(2,1)}, bf16[4,4096]{1,0:T(4,128)(2,1)S(1)}, u32[]{:S(2)}, u32[]{:S(2)}) collective-permute-start(bf16[4,4096]{1,0:T(4,128)(2,1)} %classes_hbm.1), channel_id=1, source_target_pairs={{0,5},{1,3},{2,7},{3,1},{4,6},{5,0},{6,4},{7,2},{8,10},{9,12},{10,... | collective-permute-start | bytes 98312 | tf_op jit(solution)/shard_map/ppermute | solution.py:357
  9.0 1.9 %collective-permute-start.3 = (f32[24,256]{1,0:T(8,128)S(1)}, f32[24,256]{1,0:T(8,128)S(1)}, u32[]{:S(2)}, u32[]{:S(2)}) collective-permute-start(f32[24,256]{1,0:T(8,128)S(1)} %get-tuple-element.20.sent_ref), channel_id=1, source_target_pairs={{0,1},{1,0},{2,3},{3,2},{4,5},{5,4},{6,7},{7,6},{8,9},{9,8},{10,11... | collective-permute-start | bytes 73736 | tf_op jit(solution)/shard_map/ppermute | solution.py:348
  11.7 5.0 %collective-permute-start.4 = (bf16[4,4352]{1,0:T(4,128)(2,1)S(1)}, bf16[4,4352]{1,0:T(4,128)(2,1)S(1)}, u32[]{:S(2)}, u32[]{:S(2)}) collective-permute-start(bf16[4,4352]{1,0:T(4,128)(2,1)S(1)} %get-tuple-element.22), channel_id=1, source_target_pairs={{0,2},{1,15},{2,0},{3,13},{4,10},{5,7},{6,8},{7,5},{8,6},{9,11},{1... | collective-permute-start | bytes 104456 | tf_op jit(solution)/shard_map/ppermute | solution.py:357
  12.8 4.7 %collective-permute-start.5 = (bf16[4,4352]{1,0:T(4,128)(2,1)S(1)}, bf16[4,4352]{1,0:T(4,128)(2,1)S(1)}, u32[]{:S(2)}, u32[]{:S(2)}) collective-permute-start(bf16[4,4352]{1,0:T(4,128)(2,1)S(1)} %get-tuple-element.23), channel_id=1, source_target_pairs={{0,9},{1,6},{2,11},{3,4},{4,3},{5,12},{6,1},{7,14},{8,15},{9,0},{1... | collective-permute-start | bytes 104456 | tf_op jit(solution)/shard_map/ppermute | solution.py:357
  13.2 4.2 %collective-permute-start.6 = (bf16[4,4352]{1,0:T(4,128)(2,1)S(1)}, bf16[4,4352]{1,0:T(4,128)(2,1)S(1)}, u32[]{:S(2)}, u32[]{:S(2)}) collective-permute-start(bf16[4,4352]{1,0:T(4,128)(2,1)S(1)} %get-tuple-element.22), channel_id=1, source_target_pairs={{0,2},{1,13},{2,0},{3,15},{4,8},{5,7},{6,10},{7,5},{8,4},{9,11},{1... | collective-permute-start | bytes 104456 | tf_op jit(solution)/shard_map/ppermute | solution.py:357
  13.8 5.3 %collective-permute-start.7 = (bf16[4,4352]{1,0:T(4,128)(2,1)S(1)}, bf16[4,4352]{1,0:T(4,128)(2,1)S(1)}, u32[]{:S(2)}, u32[]{:S(2)}) collective-permute-start(bf16[4,4352]{1,0:T(4,128)(2,1)S(1)} %get-tuple-element.23), channel_id=1, source_target_pairs={{0,11},{1,4},{2,9},{3,6},{4,1},{5,14},{6,3},{7,12},{8,13},{9,2},{1... | collective-permute-start | bytes 104456 | tf_op jit(solution)/shard_map/ppermute | solution.py:357
  19.1 1.5 %collective-permute-start.8 = (f32[4,4352]{1,0:T(4,128)S(1)}, f32[4,4352]{1,0:T(4,128)S(1)}, u32[]{:S(2)}, u32[]{:S(2)}) collective-permute-start(f32[4,4352]{1,0:T(4,128)S(1)} %shard_map.70.own_ref), channel_id=1, source_target_pairs={{0,1},{1,0},{2,3},{3,2},{4,5},{5,4},{6,7},{7,6},{8,9},{9,8},{10,11... | collective-permute-start | bytes 208904 | tf_op jit(solution)/shard_map/ppermute | solution.py:348

commit v7 on v6

--- a/solution.py
+++ b/solution.py
@@ -17,6 +17,8 @@
 
 
 def rolled(tile, by):
+    if tile.shape[1] == LANES and by == BOX:
+        return pltpu.roll(tile, BOX, 1)
     return jnp.concatenate([tile[:, by:], tile[:, :by]], axis=1)
 
 
@@ -415,7 +417,7 @@
     outs = (shape((per_dev, pixels), F32), shape((1, per_dev), F32), shape((1, read_rows), F32))
     means, weights, loglik = call(
         finish_kernel, outs, (summed, other, totals), (),
-        [pltpu.VMEM(out.shape, out.dtype) for out in outs] + [pltpu.SemaphoreType.DMA((6,))],
+        [pltpu.VMEM(out.shape, out.dtype) for out in outs] + [pltpu.SemaphoreType.DMA((3,))],
         outs_in_hbm=True,
     )
     return means, weights.reshape(per_dev), loglik.reshape(read_rows)

time: 21.5 us -> 21.5 us (level)
  no operation moved by 1% of the time
where the time goes in v7:
time: 21.5 us; the launch traced here: 21.4 us
  starting transfers between devices  12 us (56%)
  Pallas kernels  4.38 us (20%)
  waiting for transfers between devices  4.27 us (20%)
  between operations  0.67 us (3%)
    ppermute x6, starting transfers between devices, traded(): return lax.ppermute(array, LINKED, pairs)  9.92 us
    pallas_call x5, Pallas kernels, call(): pl.pallas_call(kernel, out_shape=outs, in_specs=specs, out_specs=jax.tree...  4.38 us
    ppermute x6, waiting for transfers between devices, traded(): return lax.ppermute(array, LINKED, pairs)  2.51 us
    ppermute x3, starting transfers between devices, swapped(): return lax.ppermute(array, 'rd', [(0, 1), (1, 0)])  2.11 us
    ppermute x3, waiting for transfers between devices, swapped(): return lax.ppermute(array, 'rd', [(0, 1), (1, 0)])  1.76 us
  transfers between devices with their start and end apart: 9, of which 5 were waited for; matrix products, arithmetic and copies ran while one was open for 0% of the time, Pallas kernels for 10%

profile of v7, /device:TPU:0, one launch (start us, length us, event | category | flops | bytes accessed | tf_op | source)
XLA Modules:
  0.0 21.4 jit_solution(6735644163581143972)
XLA Ops:
  0.6 0.5 %collective-permute-start = (bf16[64,4096]{1,0:T(8,128)(2,1)}, bf16[64,4096]{1,0:T(8,128)(2,1)S(1)}, u32[]{:S(2)}, u32[]{:S(2)}) collective-permute-start(bf16[64,4096]{1,0:T(8,128)(2,1)} %own_hbm.1), channel_id=1, source_target_pairs={{0,1},{1,0},{2,3},{3,2},{4,5},{5,4},{6,7},{7,6},{8,9},{9,8},{10,11... | collective-permute-start | bytes 1572872 | tf_op jit(solution)/shard_map/ppermute | solution.py:350
  1.1 3.7 %collective-permute-start.1 = (bf16[4,4096]{1,0:T(4,128)(2,1)}, bf16[4,4096]{1,0:T(4,128)(2,1)S(1)}, u32[]{:S(2)}, u32[]{:S(2)}) collective-permute-start(bf16[4,4096]{1,0:T(4,128)(2,1)} %classes_hbm.1), channel_id=1, source_target_pairs={{0,9},{1,13},{2,11},{3,15},{4,8},{5,12},{6,10},{7,14},{8,4},{9,0},... | collective-permute-start | bytes 98312 | tf_op jit(solution)/shard_map/ppermute | solution.py:359
  4.8 1.3 %collective-permute-start.2 = (bf16[4,4096]{1,0:T(4,128)(2,1)}, bf16[4,4096]{1,0:T(4,128)(2,1)S(1)}, u32[]{:S(2)}, u32[]{:S(2)}) collective-permute-start(bf16[4,4096]{1,0:T(4,128)(2,1)} %classes_hbm.1), channel_id=1, source_target_pairs={{0,5},{1,3},{2,7},{3,1},{4,6},{5,0},{6,4},{7,2},{8,10},{9,12},{10,... | collective-permute-start | bytes 98312 | tf_op jit(solution)/shard_map/ppermute | solution.py:359
  6.1 0.0 collective-permute-done.other_ref
  6.1 2.1 %shard_map.67 = (bf16[4096,256]{1,0:T(8,128)(2,1)S(1)}, bf16[256,4096]{1,0:T(8,128)(2,1)S(1)}, f32[8,128]{1,0:T(8,128)S(1)}, bf16[4,4096]{1,0:T(4,128)(2,1)S(1)}) custom-call(bf16[64,4096]{1,0:T(8,128)(2,1)} %own_hbm.1, s32[1,4]{1,0:T(1,128)} %counts_hbm.1, s32[1,4]{1,0:T(1,128)} %owners_hbm.1, bf16[4,4096]{1,0:T(4,128)(2,1)} %classes_hbm.1, ...), custom_call_target="tpu_custom_call" | custom-call | tf_op jit(solution)/shard_map/pallas_call | solution.py:368
  8.3 0.0 collective-permute-done.1.two_ref
  8.3 0.1 collective-permute-done.2.one_ref
  8.4 0.6 %shard_map.68 = (f32[32,256]{1,0:T(8,128)S(1)}, f32[24,256]{1,0:T(8,128)S(1)}) custom-call(f32[8,128]{1,0:T(8,128)S(1)} %get-tuple-element.16.slots_ref, bf16[4,4096]{1,0:T(4,128)(2,1)S(1)} %collective-permute-done.1.two_ref, bf16[4,4096]{1,0:T(4,128)(2,1)S(1)} %collective-permute-done.2.one_ref, bf16[4,4096]{1,0:T(4,128)(2,1)S(1)} %get-tuple-element.17.own_ref, ...), custom_call_target="tpu_custom_call" | custom-call | tf_op jit(solution)/shard_map/pallas_call | solution.py:368
  9.0 1.0 %collective-permute-start.3 = (f32[24,256]{1,0:T(8,128)S(1)}, f32[24,256]{1,0:T(8,128)S(1)}, u32[]{:S(2)}, u32[]{:S(2)}) collective-permute-start(f32[24,256]{1,0:T(8,128)S(1)} %get-tuple-element.20.sent_ref), channel_id=1, source_target_pairs={{0,1},{1,0},{2,3},{3,2},{4,5},{5,4},{6,7},{7,6},{8,9},{9,8},{10,11... | collective-permute-start | bytes 73736 | tf_op jit(solution)/shard_map/ppermute | solution.py:350
  10.1 0.8 %collective-permute-done.3.arrived_ref = f32[24,256]{1,0:T(8,128)S(1)} collective-permute-done((f32[24,256]{1,0:T(8,128)S(1)}, f32[24,256]{1,0:T(8,128)S(1)}, u32[]{:S(2)}, u32[]{:S(2)}) %collective-permute-start.3) | collective-permute-done | bytes 24608 | tf_op jit(solution)/shard_map/ppermute | solution.py:350
  10.9 0.8 %shard_map.69 = (bf16[4,4352]{1,0:T(4,128)(2,1)S(1)}, bf16[4,4352]{1,0:T(4,128)(2,1)S(1)}, f32[1,128]{1,0:T(1,128)S(1)}, bf16[4,4352]{1,0:T(4,128)(2,1)S(1)}) custom-call(f32[32,256]{1,0:T(8,128)S(1)} %get-tuple-element.19.scores_ref, f32[24,256]{1,0:T(8,128)S(1)} %get-tuple-element.20.sent_ref, f32[24,256]{1,0:T(8,128)S(1)} %collective-permute-done.3.arrived_ref, ...), custom_call_target="tpu_custom_call" | custom-call | tf_op jit(solution)/shard_map/pallas_call | solution.py:368
  11.7 1.1 %collective-permute-start.4 = (bf16[4,4352]{1,0:T(4,128)(2,1)S(1)}, bf16[4,4352]{1,0:T(4,128)(2,1)S(1)}, u32[]{:S(2)}, u32[]{:S(2)}) collective-permute-start(bf16[4,4352]{1,0:T(4,128)(2,1)S(1)} %get-tuple-element.22), channel_id=1, source_target_pairs={{0,2},{1,15},{2,0},{3,13},{4,10},{5,7},{6,8},{7,5},{8,6},{9,11},{1... | collective-permute-start | bytes 104456 | tf_op jit(solution)/shard_map/ppermute | solution.py:359
  12.8 0.4 %collective-permute-start.5 = (bf16[4,4352]{1,0:T(4,128)(2,1)S(1)}, bf16[4,4352]{1,0:T(4,128)(2,1)S(1)}, u32[]{:S(2)}, u32[]{:S(2)}) collective-permute-start(bf16[4,4352]{1,0:T(4,128)(2,1)S(1)} %get-tuple-element.23), channel_id=1, source_target_pairs={{0,9},{1,6},{2,11},{3,4},{4,3},{5,12},{6,1},{7,14},{8,15},{9,0},{1... | collective-permute-start | bytes 104456 | tf_op jit(solution)/shard_map/ppermute | solution.py:359
  13.2 0.5 %collective-permute-start.6 = (bf16[4,4352]{1,0:T(4,128)(2,1)S(1)}, bf16[4,4352]{1,0:T(4,128)(2,1)S(1)}, u32[]{:S(2)}, u32[]{:S(2)}) collective-permute-start(bf16[4,4352]{1,0:T(4,128)(2,1)S(1)} %get-tuple-element.22), channel_id=1, source_target_pairs={{0,2},{1,13},{2,0},{3,15},{4,8},{5,7},{6,10},{7,5},{8,4},{9,11},{1... | collective-permute-start | bytes 104456 | tf_op jit(solution)/shard_map/ppermute | solution.py:359
  13.8 2.9 %collective-permute-start.7 = (bf16[4,4352]{1,0:T(4,128)(2,1)S(1)}, bf16[4,4352]{1,0:T(4,128)(2,1)S(1)}, u32[]{:S(2)}, u32[]{:S(2)}) collective-permute-start(bf16[4,4352]{1,0:T(4,128)(2,1)S(1)} %get-tuple-element.23), channel_id=1, source_target_pairs={{0,11},{1,4},{2,9},{3,6},{4,1},{5,14},{6,3},{7,12},{8,13},{9,2},{1... | collective-permute-start | bytes 104456 | tf_op jit(solution)/shard_map/ppermute | solution.py:359
  16.7 0.0 collective-permute-done.4.pd_ref
  16.7 0.8 %collective-permute-done.5.qx_ref = bf16[4,4352]{1,0:T(4,128)(2,1)S(1)} collective-permute-done((bf16[4,4352]{1,0:T(4,128)(2,1)S(1)}, bf16[4,4352]{1,0:T(4,128)(2,1)S(1)}, u32[]{:S(2)}, u32[]{:S(2)}) %collective-permute-start.5) | collective-permute-done | bytes 34848 | tf_op jit(solution)/shard_map/ppermute | solution.py:359
  17.5 0.0 collective-permute-done.6.po_ref
  17.5 1.6 %collective-permute-done.7.qx1_ref = bf16[4,4352]{1,0:T(4,128)(2,1)S(1)} collective-permute-done((bf16[4,4352]{1,0:T(4,128)(2,1)S(1)}, bf16[4,4352]{1,0:T(4,128)(2,1)S(1)}, u32[]{:S(2)}, u32[]{:S(2)}) %collective-permute-start.7) | collective-permute-done | bytes 34848 | tf_op jit(solution)/shard_map/ppermute | solution.py:359
  19.1 0.6 %collective-permute-start.8 = (f32[4,4352]{1,0:T(4,128)S(1)}, f32[4,4352]{1,0:T(4,128)S(1)}, u32[]{:S(2)}, u32[]{:S(2)}) collective-permute-start(f32[4,4352]{1,0:T(4,128)S(1)} %shard_map.70.own_ref), channel_id=1, source_target_pairs={{0,1},{1,0},{2,3},{3,2},{4,5},{5,4},{6,7},{7,6},{8,9},{9,8},{10,11... | collective-permute-start | bytes 208904 | tf_op jit(solution)/shard_map/ppermute | solution.py:350
  19.6 0.9 %collective-permute-done.8.other_ref = f32[4,4352]{1,0:T(4,128)S(1)} collective-permute-done((f32[4,4352]{1,0:T(4,128)S(1)}, f32[4,4352]{1,0:T(4,128)S(1)}, u32[]{:S(2)}, u32[]{:S(2)}) %collective-permute-start.8) | collective-permute-done | bytes 69664 | tf_op jit(solution)/shard_map/ppermute | solution.py:350
  20.5 0.8 %shard_map.71 = (f32[4,4096]{1,0:T(4,128)}, f32[1,4]{1,0:T(1,128)}, f32[1,64]{1,0:T(1,128)}) custom-call(f32[4,4352]{1,0:T(4,128)S(1)} %shard_map.70.own_ref, f32[4,4352]{1,0:T(4,128)S(1)} %collective-permute-done.8.other_ref, f32[1,128]{1,0:T(1,128)S(1)} %get-tuple-element.25.total_ref), custom_call_target="tpu_custom_call" | custom-call | tf_op jit(solution)/shard_map/pallas_call | solution.py:368
  (1 shorter events, 0.0 us)
Async XLA Ops:
  0.6 5.5 %collective-permute-start = (bf16[64,4096]{1,0:T(8,128)(2,1)}, bf16[64,4096]{1,0:T(8,128)(2,1)S(1)}, u32[]{:S(2)}, u32[]{:S(2)}) collective-permute-start(bf16[64,4096]{1,0:T(8,128)(2,1)} %own_hbm.1), channel_id=1, source_target_pairs={{0,1},{1,0},{2,3},{3,2},{4,5},{5,4},{6,7},{7,6},{8,9},{9,8},{10,11... | collective-permute-start | bytes 1572872 | tf_op jit(solution)/shard_map/ppermute | solution.py:350
  1.1 7.1 %collective-permute-start.1 = (bf16[4,4096]{1,0:T(4,128)(2,1)}, bf16[4,4096]{1,0:T(4,128)(2,1)S(1)}, u32[]{:S(2)}, u32[]{:S(2)}) collective-permute-start(bf16[4,4096]{1,0:T(4,128)(2,1)} %classes_hbm.1), channel_id=1, source_target_pairs={{0,9},{1,13},{2,11},{3,15},{4,8},{5,12},{6,10},{7,14},{8,4},{9,0},... | collective-permute-start | bytes 98312 | tf_op jit(solution)/shard_map/ppermute | solution.py:359
  4.8 3.6 %collective-permute-start.2 = (bf16[4,4096]{1,0:T(4,128)(2,1)}, bf16[4,4096]{1,0:T(4,128)(2,1)S(1)}, u32[]{:S(2)}, u32[]{:S(2)}) collective-permute-start(bf16[4,4096]{1,0:T(4,128)(2,1)} %classes_hbm.1), channel_id=1, source_target_pairs={{0,5},{1,3},{2,7},{3,1},{4,6},{5,0},{6,4},{7,2},{8,10},{9,12},{10,... | collective-permute-start | bytes 98312 | tf_op jit(solution)/shard_map/ppermute | solution.py:359
  9.0 1.9 %collective-permute-start.3 = (f32[24,256]{1,0:T(8,128)S(1)}, f32[24,256]{1,0:T(8,128)S(1)}, u32[]{:S(2)}, u32[]{:S(2)}) collective-permute-start(f32[24,256]{1,0:T(8,128)S(1)} %get-tuple-element.20.sent_ref), channel_id=1, source_target_pairs={{0,1},{1,0},{2,3},{3,2},{4,5},{5,4},{6,7},{7,6},{8,9},{9,8},{10,11... | collective-permute-start | bytes 73736 | tf_op jit(solution)/shard_map/ppermute | solution.py:350
  11.7 5.0 %collective-permute-start.4 = (bf16[4,4352]{1,0:T(4,128)(2,1)S(1)}, bf16[4,4352]{1,0:T(4,128)(2,1)S(1)}, u32[]{:S(2)}, u32[]{:S(2)}) collective-permute-start(bf16[4,4352]{1,0:T(4,128)(2,1)S(1)} %get-tuple-element.22), channel_id=1, source_target_pairs={{0,2},{1,15},{2,0},{3,13},{4,10},{5,7},{6,8},{7,5},{8,6},{9,11},{1... | collective-permute-start | bytes 104456 | tf_op jit(solution)/shard_map/ppermute | solution.py:359
  12.8 4.7 %collective-permute-start.5 = (bf16[4,4352]{1,0:T(4,128)(2,1)S(1)}, bf16[4,4352]{1,0:T(4,128)(2,1)S(1)}, u32[]{:S(2)}, u32[]{:S(2)}) collective-permute-start(bf16[4,4352]{1,0:T(4,128)(2,1)S(1)} %get-tuple-element.23), channel_id=1, source_target_pairs={{0,9},{1,6},{2,11},{3,4},{4,3},{5,12},{6,1},{7,14},{8,15},{9,0},{1... | collective-permute-start | bytes 104456 | tf_op jit(solution)/shard_map/ppermute | solution.py:359
  13.2 4.2 %collective-permute-start.6 = (bf16[4,4352]{1,0:T(4,128)(2,1)S(1)}, bf16[4,4352]{1,0:T(4,128)(2,1)S(1)}, u32[]{:S(2)}, u32[]{:S(2)}) collective-permute-start(bf16[4,4352]{1,0:T(4,128)(2,1)S(1)} %get-tuple-element.22), channel_id=1, source_target_pairs={{0,2},{1,13},{2,0},{3,15},{4,8},{5,7},{6,10},{7,5},{8,4},{9,11},{1... | collective-permute-start | bytes 104456 | tf_op jit(solution)/shard_map/ppermute | solution.py:359
  13.8 5.3 %collective-permute-start.7 = (bf16[4,4352]{1,0:T(4,128)(2,1)S(1)}, bf16[4,4352]{1,0:T(4,128)(2,1)S(1)}, u32[]{:S(2)}, u32[]{:S(2)}) collective-permute-start(bf16[4,4352]{1,0:T(4,128)(2,1)S(1)} %get-tuple-element.23), channel_id=1, source_target_pairs={{0,11},{1,4},{2,9},{3,6},{4,1},{5,14},{6,3},{7,12},{8,13},{9,2},{1... | collective-permute-start | bytes 104456 | tf_op jit(solution)/shard_map/ppermute | solution.py:359
  19.1 1.5 %collective-permute-start.8 = (f32[4,4352]{1,0:T(4,128)S(1)}, f32[4,4352]{1,0:T(4,128)S(1)}, u32[]{:S(2)}, u32[]{:S(2)}) collective-permute-start(f32[4,4352]{1,0:T(4,128)S(1)} %shard_map.70.own_ref), channel_id=1, source_target_pairs={{0,1},{1,0},{2,3},{3,2},{4,5},{5,4},{6,7},{7,6},{8,9},{9,8},{10,11... | collective-permute-start | bytes 208904 | tf_op jit(solution)/shard_map/ppermute | solution.py:350

commit v8 on v7

--- a/solution.py
+++ b/solution.py
@@ -192,7 +192,7 @@
     kept_ref[...] = first_ref[...]
 
 
-def add_kernel(pd_ref, qx_ref, po_ref, qx1_ref, kept_ref, out_ref):
+def add_kernel(po_ref, qx_ref, pd_ref, qx1_ref, kept_ref, out_ref):
     pixels = out_ref.shape[1] - LANES
     own = jnp.where(leads(), kept_ref[:, :pixels].astype(F32), pd_ref[:, :pixels].astype(F32))
     out_ref[:, :pixels] = (qx_ref[:, :pixels].astype(F32) + qx1_ref[:, :pixels].astype(F32)) + (
@@ -412,7 +412,7 @@
     pd = traded(first, (2, 14))
     qx1 = traded(second, (10, 4))
     qx = traded(second, (8, 6))
-    summed = call(add_kernel, shape((per_dev, wide), F32), (pd, qx, po, qx1, kept))
+    summed = call(add_kernel, shape((per_dev, wide), F32), (po, qx, pd, qx1, kept))
     other = swapped(summed)
     outs = (shape((per_dev, pixels), F32), shape((1, per_dev), F32), shape((1, read_rows), F32))
     means, weights, loglik = call(

time: 21.5 us -> 21.5 us (level)
  no operation moved by 1% of the time
where the time goes in v8:
time: 21.5 us; the launch traced here: 21.4 us
  starting transfers between devices  12.1 us (56%)
  Pallas kernels  4.38 us (20%)
  waiting for transfers between devices  4.17 us (19%)
  between operations  0.67 us (3%)
    ppermute x6, starting transfers between devices, traded(): return lax.ppermute(array, LINKED, pairs)  9.92 us
    pallas_call x5, Pallas kernels, call(): pl.pallas_call(kernel, out_shape=outs, in_specs=specs, out_specs=jax.tree...  4.38 us
    ppermute x6, waiting for transfers between devices, traded(): return lax.ppermute(array, LINKED, pairs)  2.41 us
    ppermute x3, starting transfers between devices, swapped(): return lax.ppermute(array, 'rd', [(0, 1), (1, 0)])  2.21 us
    ppermute x3, waiting for transfers between devices, swapped(): return lax.ppermute(array, 'rd', [(0, 1), (1, 0)])  1.76 us
  transfers between devices with their start and end apart: 9, of which 5 were waited for; matrix products, arithmetic and copies ran while one was open for 0% of the time, Pallas kernels for 10%

profile of v8, /device:TPU:0, one launch (start us, length us, event | category | flops | bytes accessed | tf_op | source)
XLA Modules:
  0.0 21.4 jit_solution(12819773706732420548)
XLA Ops:
  0.6 0.5 %collective-permute-start = (bf16[64,4096]{1,0:T(8,128)(2,1)}, bf16[64,4096]{1,0:T(8,128)(2,1)S(1)}, u32[]{:S(2)}, u32[]{:S(2)}) collective-permute-start(bf16[64,4096]{1,0:T(8,128)(2,1)} %own_hbm.1), channel_id=1, source_target_pairs={{0,1},{1,0},{2,3},{3,2},{4,5},{5,4},{6,7},{7,6},{8,9},{9,8},{10,11... | collective-permute-start | bytes 1572872 | tf_op jit(solution)/shard_map/ppermute | solution.py:350
  1.1 3.7 %collective-permute-start.1 = (bf16[4,4096]{1,0:T(4,128)(2,1)}, bf16[4,4096]{1,0:T(4,128)(2,1)S(1)}, u32[]{:S(2)}, u32[]{:S(2)}) collective-permute-start(bf16[4,4096]{1,0:T(4,128)(2,1)} %classes_hbm.1), channel_id=1, source_target_pairs={{0,9},{1,13},{2,11},{3,15},{4,8},{5,12},{6,10},{7,14},{8,4},{9,0},... | collective-permute-start | bytes 98312 | tf_op jit(solution)/shard_map/ppermute | solution.py:359
  4.8 1.3 %collective-permute-start.2 = (bf16[4,4096]{1,0:T(4,128)(2,1)}, bf16[4,4096]{1,0:T(4,128)(2,1)S(1)}, u32[]{:S(2)}, u32[]{:S(2)}) collective-permute-start(bf16[4,4096]{1,0:T(4,128)(2,1)} %classes_hbm.1), channel_id=1, source_target_pairs={{0,5},{1,3},{2,7},{3,1},{4,6},{5,0},{6,4},{7,2},{8,10},{9,12},{10,... | collective-permute-start | bytes 98312 | tf_op jit(solution)/shard_map/ppermute | solution.py:359
  6.1 0.0 collective-permute-done.other_ref
  6.1 2.1 %shard_map.67 = (bf16[4096,256]{1,0:T(8,128)(2,1)S(1)}, bf16[256,4096]{1,0:T(8,128)(2,1)S(1)}, f32[8,128]{1,0:T(8,128)S(1)}, bf16[4,4096]{1,0:T(4,128)(2,1)S(1)}) custom-call(bf16[64,4096]{1,0:T(8,128)(2,1)} %own_hbm.1, s32[1,4]{1,0:T(1,128)} %counts_hbm.1, s32[1,4]{1,0:T(1,128)} %owners_hbm.1, bf16[4,4096]{1,0:T(4,128)(2,1)} %classes_hbm.1, ...), custom_call_target="tpu_custom_call" | custom-call | tf_op jit(solution)/shard_map/pallas_call | solution.py:368
  8.3 0.0 collective-permute-done.1.two_ref
  8.3 0.1 collective-permute-done.2.one_ref
  8.4 0.6 %shard_map.68 = (f32[32,256]{1,0:T(8,128)S(1)}, f32[24,256]{1,0:T(8,128)S(1)}) custom-call(f32[8,128]{1,0:T(8,128)S(1)} %get-tuple-element.16.slots_ref, bf16[4,4096]{1,0:T(4,128)(2,1)S(1)} %collective-permute-done.1.two_ref, bf16[4,4096]{1,0:T(4,128)(2,1)S(1)} %collective-permute-done.2.one_ref, bf16[4,4096]{1,0:T(4,128)(2,1)S(1)} %get-tuple-element.17.own_ref, ...), custom_call_target="tpu_custom_call" | custom-call | tf_op jit(solution)/shard_map/pallas_call | solution.py:368
  9.0 1.0 %collective-permute-start.3 = (f32[24,256]{1,0:T(8,128)S(1)}, f32[24,256]{1,0:T(8,128)S(1)}, u32[]{:S(2)}, u32[]{:S(2)}) collective-permute-start(f32[24,256]{1,0:T(8,128)S(1)} %get-tuple-element.20.sent_ref), channel_id=1, source_target_pairs={{0,1},{1,0},{2,3},{3,2},{4,5},{5,4},{6,7},{7,6},{8,9},{9,8},{10,11... | collective-permute-start | bytes 73736 | tf_op jit(solution)/shard_map/ppermute | solution.py:350
  10.1 0.8 %collective-permute-done.3.arrived_ref = f32[24,256]{1,0:T(8,128)S(1)} collective-permute-done((f32[24,256]{1,0:T(8,128)S(1)}, f32[24,256]{1,0:T(8,128)S(1)}, u32[]{:S(2)}, u32[]{:S(2)}) %collective-permute-start.3) | collective-permute-done | bytes 24608 | tf_op jit(solution)/shard_map/ppermute | solution.py:350
  10.9 0.8 %shard_map.69 = (bf16[4,4352]{1,0:T(4,128)(2,1)S(1)}, bf16[4,4352]{1,0:T(4,128)(2,1)S(1)}, f32[1,128]{1,0:T(1,128)S(1)}, bf16[4,4352]{1,0:T(4,128)(2,1)S(1)}) custom-call(f32[32,256]{1,0:T(8,128)S(1)} %get-tuple-element.19.scores_ref, f32[24,256]{1,0:T(8,128)S(1)} %get-tuple-element.20.sent_ref, f32[24,256]{1,0:T(8,128)S(1)} %collective-permute-done.3.arrived_ref, ...), custom_call_target="tpu_custom_call" | custom-call | tf_op jit(solution)/shard_map/pallas_call | solution.py:368
  11.7 1.1 %collective-permute-start.4 = (bf16[4,4352]{1,0:T(4,128)(2,1)S(1)}, bf16[4,4352]{1,0:T(4,128)(2,1)S(1)}, u32[]{:S(2)}, u32[]{:S(2)}) collective-permute-start(bf16[4,4352]{1,0:T(4,128)(2,1)S(1)} %get-tuple-element.22), channel_id=1, source_target_pairs={{0,2},{1,13},{2,0},{3,15},{4,8},{5,7},{6,10},{7,5},{8,4},{9,11},{1... | collective-permute-start | bytes 104456 | tf_op jit(solution)/shard_map/ppermute | solution.py:359
  12.8 0.4 %collective-permute-start.5 = (bf16[4,4352]{1,0:T(4,128)(2,1)S(1)}, bf16[4,4352]{1,0:T(4,128)(2,1)S(1)}, u32[]{:S(2)}, u32[]{:S(2)}) collective-permute-start(bf16[4,4352]{1,0:T(4,128)(2,1)S(1)} %get-tuple-element.23), channel_id=1, source_target_pairs={{0,9},{1,6},{2,11},{3,4},{4,3},{5,12},{6,1},{7,14},{8,15},{9,0},{1... | collective-permute-start | bytes 104456 | tf_op jit(solution)/shard_map/ppermute | solution.py:359
  13.2 0.5 %collective-permute-start.6 = (bf16[4,4352]{1,0:T(4,128)(2,1)S(1)}, bf16[4,4352]{1,0:T(4,128)(2,1)S(1)}, u32[]{:S(2)}, u32[]{:S(2)}) collective-permute-start(bf16[4,4352]{1,0:T(4,128)(2,1)S(1)} %get-tuple-element.22), channel_id=1, source_target_pairs={{0,2},{1,15},{2,0},{3,13},{4,10},{5,7},{6,8},{7,5},{8,6},{9,11},{1... | collective-permute-start | bytes 104456 | tf_op jit(solution)/shard_map/ppermute | solution.py:359
  13.8 2.9 %collective-permute-start.7 = (bf16[4,4352]{1,0:T(4,128)(2,1)S(1)}, bf16[4,4352]{1,0:T(4,128)(2,1)S(1)}, u32[]{:S(2)}, u32[]{:S(2)}) collective-permute-start(bf16[4,4352]{1,0:T(4,128)(2,1)S(1)} %get-tuple-element.23), channel_id=1, source_target_pairs={{0,11},{1,4},{2,9},{3,6},{4,1},{5,14},{6,3},{7,12},{8,13},{9,2},{1... | collective-permute-start | bytes 104456 | tf_op jit(solution)/shard_map/ppermute | solution.py:359
  16.7 0.0 collective-permute-done.4.po_ref
  16.7 0.6 %collective-permute-done.5.qx_ref = bf16[4,4352]{1,0:T(4,128)(2,1)S(1)} collective-permute-done((bf16[4,4352]{1,0:T(4,128)(2,1)S(1)}, bf16[4,4352]{1,0:T(4,128)(2,1)S(1)}, u32[]{:S(2)}, u32[]{:S(2)}) %collective-permute-start.5) | collective-permute-done | bytes 34848 | tf_op jit(solution)/shard_map/ppermute | solution.py:359
  17.2 0.0 collective-permute-done.6.pd_ref
  17.2 1.7 %collective-permute-done.7.qx1_ref = bf16[4,4352]{1,0:T(4,128)(2,1)S(1)} collective-permute-done((bf16[4,4352]{1,0:T(4,128)(2,1)S(1)}, bf16[4,4352]{1,0:T(4,128)(2,1)S(1)}, u32[]{:S(2)}, u32[]{:S(2)}) %collective-permute-start.7) | collective-permute-done | bytes 34848 | tf_op jit(solution)/shard_map/ppermute | solution.py:359
  19.0 0.7 %collective-permute-start.8 = (f32[4,4352]{1,0:T(4,128)S(1)}, f32[4,4352]{1,0:T(4,128)S(1)}, u32[]{:S(2)}, u32[]{:S(2)}) collective-permute-start(f32[4,4352]{1,0:T(4,128)S(1)} %shard_map.70.own_ref), channel_id=1, source_target_pairs={{0,1},{1,0},{2,3},{3,2},{4,5},{5,4},{6,7},{7,6},{8,9},{9,8},{10,11... | collective-permute-start | bytes 208904 | tf_op jit(solution)/shard_map/ppermute | solution.py:350
  19.6 0.9 %collective-permute-done.8.other_ref = f32[4,4352]{1,0:T(4,128)S(1)} collective-permute-done((f32[4,4352]{1,0:T(4,128)S(1)}, f32[4,4352]{1,0:T(4,128)S(1)}, u32[]{:S(2)}, u32[]{:S(2)}) %collective-permute-start.8) | collective-permute-done | bytes 69664 | tf_op jit(solution)/shard_map/ppermute | solution.py:350
  20.5 0.8 %shard_map.71 = (f32[4,4096]{1,0:T(4,128)}, f32[1,4]{1,0:T(1,128)}, f32[1,64]{1,0:T(1,128)}) custom-call(f32[4,4352]{1,0:T(4,128)S(1)} %shard_map.70.own_ref, f32[4,4352]{1,0:T(4,128)S(1)} %collective-permute-done.8.other_ref, f32[1,128]{1,0:T(1,128)S(1)} %get-tuple-element.25.total_ref), custom_call_target="tpu_custom_call" | custom-call | tf_op jit(solution)/shard_map/pallas_call | solution.py:368
  (1 shorter events, 0.0 us)
Async XLA Ops:
  0.6 5.5 %collective-permute-start = (bf16[64,4096]{1,0:T(8,128)(2,1)}, bf16[64,4096]{1,0:T(8,128)(2,1)S(1)}, u32[]{:S(2)}, u32[]{:S(2)}) collective-permute-start(bf16[64,4096]{1,0:T(8,128)(2,1)} %own_hbm.1), channel_id=1, source_target_pairs={{0,1},{1,0},{2,3},{3,2},{4,5},{5,4},{6,7},{7,6},{8,9},{9,8},{10,11... | collective-permute-start | bytes 1572872 | tf_op jit(solution)/shard_map/ppermute | solution.py:350
  1.1 7.1 %collective-permute-start.1 = (bf16[4,4096]{1,0:T(4,128)(2,1)}, bf16[4,4096]{1,0:T(4,128)(2,1)S(1)}, u32[]{:S(2)}, u32[]{:S(2)}) collective-permute-start(bf16[4,4096]{1,0:T(4,128)(2,1)} %classes_hbm.1), channel_id=1, source_target_pairs={{0,9},{1,13},{2,11},{3,15},{4,8},{5,12},{6,10},{7,14},{8,4},{9,0},... | collective-permute-start | bytes 98312 | tf_op jit(solution)/shard_map/ppermute | solution.py:359
  4.8 3.6 %collective-permute-start.2 = (bf16[4,4096]{1,0:T(4,128)(2,1)}, bf16[4,4096]{1,0:T(4,128)(2,1)S(1)}, u32[]{:S(2)}, u32[]{:S(2)}) collective-permute-start(bf16[4,4096]{1,0:T(4,128)(2,1)} %classes_hbm.1), channel_id=1, source_target_pairs={{0,5},{1,3},{2,7},{3,1},{4,6},{5,0},{6,4},{7,2},{8,10},{9,12},{10,... | collective-permute-start | bytes 98312 | tf_op jit(solution)/shard_map/ppermute | solution.py:359
  9.0 1.9 %collective-permute-start.3 = (f32[24,256]{1,0:T(8,128)S(1)}, f32[24,256]{1,0:T(8,128)S(1)}, u32[]{:S(2)}, u32[]{:S(2)}) collective-permute-start(f32[24,256]{1,0:T(8,128)S(1)} %get-tuple-element.20.sent_ref), channel_id=1, source_target_pairs={{0,1},{1,0},{2,3},{3,2},{4,5},{5,4},{6,7},{7,6},{8,9},{9,8},{10,11... | collective-permute-start | bytes 73736 | tf_op jit(solution)/shard_map/ppermute | solution.py:350
  11.7 5.0 %collective-permute-start.4 = (bf16[4,4352]{1,0:T(4,128)(2,1)S(1)}, bf16[4,4352]{1,0:T(4,128)(2,1)S(1)}, u32[]{:S(2)}, u32[]{:S(2)}) collective-permute-start(bf16[4,4352]{1,0:T(4,128)(2,1)S(1)} %get-tuple-element.22), channel_id=1, source_target_pairs={{0,2},{1,13},{2,0},{3,15},{4,8},{5,7},{6,10},{7,5},{8,4},{9,11},{1... | collective-permute-start | bytes 104456 | tf_op jit(solution)/shard_map/ppermute | solution.py:359
  12.8 4.4 %collective-permute-start.5 = (bf16[4,4352]{1,0:T(4,128)(2,1)S(1)}, bf16[4,4352]{1,0:T(4,128)(2,1)S(1)}, u32[]{:S(2)}, u32[]{:S(2)}) collective-permute-start(bf16[4,4352]{1,0:T(4,128)(2,1)S(1)} %get-tuple-element.23), channel_id=1, source_target_pairs={{0,9},{1,6},{2,11},{3,4},{4,3},{5,12},{6,1},{7,14},{8,15},{9,0},{1... | collective-permute-start | bytes 104456 | tf_op jit(solution)/shard_map/ppermute | solution.py:359
  13.2 4.0 %collective-permute-start.6 = (bf16[4,4352]{1,0:T(4,128)(2,1)S(1)}, bf16[4,4352]{1,0:T(4,128)(2,1)S(1)}, u32[]{:S(2)}, u32[]{:S(2)}) collective-permute-start(bf16[4,4352]{1,0:T(4,128)(2,1)S(1)} %get-tuple-element.22), channel_id=1, source_target_pairs={{0,2},{1,15},{2,0},{3,13},{4,10},{5,7},{6,8},{7,5},{8,6},{9,11},{1... | collective-permute-start | bytes 104456 | tf_op jit(solution)/shard_map/ppermute | solution.py:359
  13.8 5.2 %collective-permute-start.7 = (bf16[4,4352]{1,0:T(4,128)(2,1)S(1)}, bf16[4,4352]{1,0:T(4,128)(2,1)S(1)}, u32[]{:S(2)}, u32[]{:S(2)}) collective-permute-start(bf16[4,4352]{1,0:T(4,128)(2,1)S(1)} %get-tuple-element.23), channel_id=1, source_target_pairs={{0,11},{1,4},{2,9},{3,6},{4,1},{5,14},{6,3},{7,12},{8,13},{9,2},{1... | collective-permute-start | bytes 104456 | tf_op jit(solution)/shard_map/ppermute | solution.py:359
  19.0 1.6 %collective-permute-start.8 = (f32[4,4352]{1,0:T(4,128)S(1)}, f32[4,4352]{1,0:T(4,128)S(1)}, u32[]{:S(2)}, u32[]{:S(2)}) collective-permute-start(f32[4,4352]{1,0:T(4,128)S(1)} %shard_map.70.own_ref), channel_id=1, source_target_pairs={{0,1},{1,0},{2,3},{3,2},{4,5},{5,4},{6,7},{7,6},{8,9},{9,8},{10,11... | collective-permute-start | bytes 208904 | tf_op jit(solution)/shard_map/ppermute | solution.py:350
